TPU v7x, 32 devices: a whole 2x2x4 slice. The times are simulated.
32 devices in a mesh: pb: 4 (over z), ka: 4 (over x, core), ha: 2 (over y).
Axes of the slice: x: 2, y: 2, z: 4, core: 2. Of those that a mesh axis runs over, the one named last changes fastest.
Arguments:
- tokens: bfloat16 [2, 3072, 768], P(None, ('pb', 'ka')), may hold values from -6 to 6
- cotangent: bfloat16 [2, 3072, 768], P(None, ('pb', 'ka')), may hold values from -6 to 6
- seq_lengths: int32 [2, 2], replicated, may hold values from 1024 to 2048, as said below
- slot_token: int32 [2, 3072], replicated, may hold values from 0 to 3071, each once within a row
- w_qkv: float32 [768, 3, 768], P(('pb', 'ka'), None, 'ha'), may hold values from -0.21875 to 0.21875
- w_proj: float32 [768, 768], P('ha', ('pb', 'ka')), may hold values from -6 to 6
- w_inner: float32 [768, 3072], P(('pb', 'ka'), 'ha'), may hold values from -0.21875 to 0.21875
- w_outer: float32 [3072, 768], P('ha', ('pb', 'ka')), may hold values from -0.109375 to 0.109375
- norm_gains: float32 [2, 768], P(None, ('pb', 'ka')), may hold values from 0.5 to 1.5
- norm_biases: float32 [2, 768], P(None, ('pb', 'ka')), may hold values from -1.75 to 1.75
- qkv_first: float32 [768, 3, 768], P(('pb', 'ka'), None, 'ha'), may hold values from -28 to 28
- qkv_second: float32 [768, 3, 768], P(('pb', 'ka'), None, 'ha'), may hold values from 39.936 to 645.12
- proj_first: float32 [768, 768], P('ha', ('pb', 'ka')), may hold values from -1 to 1
- proj_second: float32 [768, 768], P('ha', ('pb', 'ka')), may hold values from 0.075 to 1.2
- inner_first: float32 [768, 3072], P(('pb', 'ka'), 'ha'), may hold values from -8 to 8
- inner_second: float32 [768, 3072], P(('pb', 'ka'), 'ha'), may hold values from 3.5328 to 58.368
- outer_first: float32 [3072, 768], P('ha', ('pb', 'ka')), may hold values from -16 to 16
- outer_second: float32 [3072, 768], P('ha', ('pb', 'ka')), may hold values from 14.4384 to 230.4
- norm_first: float32 [4, 768], P(None, ('pb', 'ka')), may hold values from -28 to 28
- norm_second: float32 [4, 768], P(None, ('pb', 'ka')), may hold values from 39.936 to 645.12
Outputs:
- layer_out: bfloat16 [2, 3072, 768], P(None, ('pb', 'ka'))
- input_grad: float32 [2, 3072, 768], P(None, ('pb', 'ka'))
- qkv_first_new: float32 [768, 3, 768], P(('pb', 'ka'), None, 'ha')
- qkv_second_new: float32 [768, 3, 768], P(('pb', 'ka'), None, 'ha')
- qkv_new: float32 [768, 3, 768], P(('pb', 'ka'), None, 'ha')
- proj_first_new: float32 [768, 768], P('ha', ('pb', 'ka'))
- proj_second_new: float32 [768, 768], P('ha', ('pb', 'ka'))
- proj_new: float32 [768, 768], P('ha', ('pb', 'ka'))
- inner_first_new: float32 [768, 3072], P(('pb', 'ka'), 'ha')
- inner_second_new: float32 [768, 3072], P(('pb', 'ka'), 'ha')
- inner_new: float32 [768, 3072], P(('pb', 'ka'), 'ha')
- outer_first_new: float32 [3072, 768], P('ha', ('pb', 'ka'))
- outer_second_new: float32 [3072, 768], P('ha', ('pb', 'ka'))
- outer_new: float32 [3072, 768], P('ha', ('pb', 'ka'))
- norm_first_new: float32 [4, 768], P(None, ('pb', 'ka'))
- norm_second_new: float32 [4, 768], P(None, ('pb', 'ka'))
- norm_new: float32 [4, 768], P(None, ('pb', 'ka'))
- norm_two_grad: float32 [2, 768], P(None, ('pb', 'ka'))
Inputs may be any that keep to these rules, and one draw needn't show every extreme that they name: `seq_lengths`: in each micro-batch the 2 lengths sum to 3072, and one of them is exactly 2048. `slot_token`: each micro-batch's row is a permutation of the token numbers.
All inputs are finite; a program needn't handle non-finite values.
Results may differ from a plain program's by a relative error of at most 0.02.
Values may be sent and summed in bfloat16 or wider, within the bound.
No kernel may reach another device: no remote copies, remote signals or barrier semaphores. Data moves between devices by JAX's collectives and lax.ppermute only.
A program may use at most 192 MiB of HBM per device.

v0:
```python
import functools

import jax
import jax.numpy as jnp
from jax import lax
from jax.sharding import PartitionSpec as P

HD = 64
MICRO = 2
STEP = 8


NORM_EPS = 1e-05
BETA_ONE = 0.9
BETA_TWO = 0.95
ADAM_EPS = 1e-08
DECAY_RATE = 0.1
RATE_MATRIX = 0.02
RATE_PROJ = 0.6
RATE_NORM = 0.1


def joined(x, axis, join):
    gathered = jax.tree.map(
        lambda a, kind: lax.all_gather(a.astype(kind), axis), x, (jnp.bfloat16, jnp.bfloat16)
    )

    def take(source):
        return jax.tree.map(
            lambda a, own: lax.dynamic_index_in_dim(a, source, 0, False).astype(own.dtype),
            gathered,
            x,
        )

    return lax.fori_loop(
        1, lax.axis_size(axis), lambda source, state: join(state, take(source)), take(0)
    )


def layer_norm(values, gain_row, shift_row):
    center = values - jnp.mean(values, axis=-1, keepdims=True)
    spread = jnp.mean(center * center, axis=-1, keepdims=True)
    return center * lax.rsqrt(spread + NORM_EPS) * gain_row + shift_row


def gelu_tanh(values):
    return jax.nn.gelu(values, approximate=True)


def doc_and_place(tok_ids, lengths):
    seq_ends = jnp.cumsum(lengths)
    passed = tok_ids[:, None] >= seq_ends[None, :]
    doc_ids = jnp.sum(passed.astype(jnp.int32), axis=1)
    places = tok_ids - jnp.sum(jnp.where(passed, lengths[None, :], 0), axis=1)
    return (doc_ids, places)


def score_tile(query_blk, query_doc, query_pos, key_heads, key_doc, key_pos, score_scale):
    scores = (
        jnp.einsum("qhe,khe->hqk", query_blk, key_heads, preferred_element_type=jnp.float32)
        * score_scale
    )
    allowed = (query_doc[:, None] == key_doc[None, :]) & (key_pos[None, :] <= query_pos[:, None])
    radius = jnp.sqrt(scores * scores + 1.0)
    return (scores, allowed[None], radius)


def forward_block(key_heads, value_heads, key_doc, key_pos, score_scale, inputs):
    query_blk, query_doc, query_pos = inputs
    scores, allowed, radius = score_tile(
        query_blk, query_doc, query_pos, key_heads, key_doc, key_pos, score_scale
    )
    local_max = jnp.max(jnp.where(allowed, radius, 0.0), axis=-1)
    weights = jnp.where(allowed, jnp.exp(radius - local_max[..., None]), 0.0)
    local_sum = jnp.sum(weights, axis=-1)
    signed = (scores / radius * weights).astype(jnp.bfloat16)
    pieces = jnp.einsum("hqk,khe->qhe", signed, value_heads, preferred_element_type=jnp.float32)
    return (local_max, local_sum, pieces)


def backward_block(key_heads, value_heads, key_doc, key_pos, score_scale, carry_in, inputs):
    key_grad, value_grad = carry_in
    query_blk, query_doc, query_pos, local_max, factor, out_grad, row_delta = inputs
    scores, allowed, radius = score_tile(
        query_blk, query_doc, query_pos, key_heads, key_doc, key_pos, score_scale
    )
    weights = jnp.where(allowed, jnp.exp(radius - local_max[..., None]), 0.0)
    slope_term = scores / radius
    signed = (slope_term * weights).astype(jnp.bfloat16)
    scaled_grad = (jnp.transpose(factor)[:, :, None] * out_grad).astype(jnp.bfloat16)
    along_value = jnp.einsum(
        "qhe,khe->hqk", scaled_grad, value_heads, preferred_element_type=jnp.float32
    )
    prob_term = weights * factor[..., None]
    score_grad = (
        weights * (1.0 / (radius * radius * radius) + slope_term * slope_term) * along_value
        - prob_term * slope_term * jnp.transpose(row_delta)[..., None]
    )
    low_grad = score_grad.astype(jnp.bfloat16)
    query_grad = (
        jnp.einsum("hqk,khe->qhe", low_grad, key_heads, preferred_element_type=jnp.float32)
        * score_scale
    )
    key_grad = (
        key_grad
        + jnp.einsum("hqk,qhe->khe", low_grad, query_blk, preferred_element_type=jnp.float32)
        * score_scale
    )
    value_grad = value_grad + jnp.einsum(
        "hqk,qhe->khe", signed, scaled_grad, preferred_element_type=jnp.float32
    )
    return ((key_grad, value_grad), query_grad)


def merge_stats(first_pair, second_pair):
    row_top = jnp.maximum(first_pair[0], second_pair[0])
    row_total = first_pair[1] * jnp.exp(first_pair[0] - row_top) + second_pair[1] * jnp.exp(
        second_pair[0] - row_top
    )
    return (row_top, row_total)


def adam_step(master, first_state, second_state, grad_term, step_rate, weight_decay):
    first_new = BETA_ONE * first_state + (1.0 - BETA_ONE) * grad_term
    second_new = BETA_TWO * second_state + (1.0 - BETA_TWO) * grad_term * grad_term
    first_hat = first_new / (1.0 - BETA_ONE**STEP)
    second_hat = second_new / (1.0 - BETA_TWO**STEP)
    master_new = master - step_rate * (
        first_hat / (jnp.sqrt(second_hat) + ADAM_EPS) + weight_decay * master
    )
    return (first_new, second_new, master_new)


def shards(
    tokens,
    cotangent,
    seq_lengths,
    slot_token,
    w_qkv,
    w_proj,
    w_inner,
    w_outer,
    norm_gains,
    norm_biases,
    qkv_first,
    qkv_second,
    proj_first,
    proj_second,
    inner_first,
    inner_second,
    outer_first,
    outer_second,
    norm_first,
    norm_second,
):
    tok_rows = tokens.shape[1]
    feat_width = tokens.shape[2]
    qkv_full, proj_full, inner_full, outer_full, gain_full, bias_full = (
        lax.all_gather(w_qkv.astype(jnp.bfloat16), ("pb", "ka"), axis=0, tiled=True),
        lax.all_gather(w_proj.astype(jnp.bfloat16), ("pb", "ka"), axis=1, tiled=True),
        lax.all_gather(w_inner.astype(jnp.bfloat16), ("pb", "ka"), axis=0, tiled=True),
        lax.all_gather(w_outer.astype(jnp.bfloat16), ("pb", "ka"), axis=1, tiled=True),
        lax.all_gather(norm_gains.astype(jnp.bfloat16), ("pb", "ka"), axis=1, tiled=True),
        lax.all_gather(norm_biases.astype(jnp.bfloat16), ("pb", "ka"), axis=1, tiled=True),
    )
    gains = gain_full.astype(jnp.float32)
    shifts = bias_full.astype(jnp.float32)
    group_width = qkv_full.shape[2]
    group_heads = group_width // HD
    score_scale = float(HD) ** (-0.5)
    size_pb = lax.axis_size("pb")
    size_ka = lax.axis_size("ka")
    index_pb = lax.axis_index("pb")
    index_ka = lax.axis_index("ka")
    query_rows = tok_rows * size_ka
    key_rows = tok_rows * size_pb
    block_rows = 512 if query_rows % 512 == 0 else query_rows
    block_count = query_rows // block_rows
    grad_sums = (
        jnp.zeros(qkv_full.shape, jnp.float32),
        jnp.zeros(proj_full.shape, jnp.float32),
        jnp.zeros(inner_full.shape, jnp.float32),
        jnp.zeros(outer_full.shape, jnp.float32),
        jnp.zeros((4, feat_width), jnp.float32),
    )
    layer_outs = []
    input_grads = []
    for micro_step in range(MICRO):
        slot_row = slot_token[micro_step]
        query_tok = lax.dynamic_slice_in_dim(slot_row, index_pb * query_rows, query_rows)
        key_tok = lax.dynamic_index_in_dim(
            slot_row.reshape(size_pb, size_ka, tok_rows), index_ka, axis=1, keepdims=False
        ).reshape(key_rows)
        query_doc, query_pos = doc_and_place(query_tok, seq_lengths[micro_step])
        key_doc, key_pos = doc_and_place(key_tok, seq_lengths[micro_step])
        inputs = tokens[micro_step].astype(jnp.float32)
        normed, norm_pull = jax.vjp(layer_norm, inputs, gains[0], shifts[0])
        normed_low = normed.astype(jnp.bfloat16)
        mixed_qkv = jnp.einsum(
            "td,dkn->tkn", normed_low, qkv_full, preferred_element_type=jnp.float32
        ).astype(jnp.bfloat16)
        queries = lax.all_gather(mixed_qkv[:, 0], "ka", axis=0, tiled=True)
        key_vals = lax.all_gather(mixed_qkv[:, 1:], "pb", axis=0, tiled=True)
        key_heads = key_vals[:, 0].reshape(key_rows, group_heads, HD)
        value_heads = key_vals[:, 1].reshape(key_rows, group_heads, HD)
        query_blocks = queries.reshape(block_count, block_rows, group_heads, HD)
        doc_blocks = query_doc.reshape(block_count, block_rows)
        pos_blocks = query_pos.reshape(block_count, block_rows)
        step_fwd = functools.partial(
            forward_block, key_heads, value_heads, key_doc, key_pos, score_scale
        )
        local_max, local_sum, pieces = lax.map(step_fwd, (query_blocks, doc_blocks, pos_blocks))
        row_top, row_total = joined((local_max, local_sum), "ka", merge_stats)
        factor = jnp.exp(local_max - row_top) / row_total
        scaled = pieces * jnp.swapaxes(factor, 1, 2)[..., None]
        attended = lax.psum_scatter(
            scaled.reshape(query_rows, group_width).astype(jnp.bfloat16),
            "ka",
            scatter_dimension=0,
            tiled=True,
        ).astype(jnp.float32)
        attended_low = attended.astype(jnp.bfloat16)
        branch = lax.psum(
            jnp.dot(attended_low, proj_full, preferred_element_type=jnp.float32).astype(
                jnp.bfloat16
            ),
            "ha",
        ).astype(jnp.float32)
        middle = inputs + branch
        normed_two, norm_two_pull = jax.vjp(layer_norm, middle, gains[1], shifts[1])
        normed_two_low = normed_two.astype(jnp.bfloat16)
        hidden = jnp.dot(normed_two_low, inner_full, preferred_element_type=jnp.float32)
        active, gelu_pull = jax.vjp(gelu_tanh, hidden)
        active_low = active.astype(jnp.bfloat16)
        outer_term = lax.psum(
            jnp.dot(active_low, outer_full, preferred_element_type=jnp.float32).astype(
                jnp.bfloat16
            ),
            "ha",
        ).astype(jnp.float32)
        layer_outs.append((middle + outer_term).astype(jnp.bfloat16))
        out_grad = cotangent[micro_step].astype(jnp.float32)
        out_low = out_grad.astype(jnp.bfloat16)
        step_outer = jnp.dot(active_low.T, out_low, preferred_element_type=jnp.float32)
        act_grad = jnp.dot(out_low, outer_full.T, preferred_element_type=jnp.float32)
        hidden_low = gelu_pull(act_grad)[0].astype(jnp.bfloat16)
        step_inner = jnp.dot(normed_two_low.T, hidden_low, preferred_element_type=jnp.float32)
        normed_two_grad = lax.psum(
            jnp.dot(hidden_low, inner_full.T, preferred_element_type=jnp.float32).astype(
                jnp.bfloat16
            ),
            "ha",
        ).astype(jnp.float32)
        middle_part, gain_two, shift_two = norm_two_pull(normed_two_grad)
        middle_grad = out_grad + middle_part
        branch_low = middle_grad.astype(jnp.bfloat16)
        step_proj = jnp.dot(attended_low.T, branch_low, preferred_element_type=jnp.float32)
        attn_grad = jnp.dot(branch_low, proj_full.T, preferred_element_type=jnp.float32)
        row_delta = jnp.sum((attn_grad * attended).reshape(tok_rows, group_heads, HD), axis=-1)
        attn_grads, delta_rows = (
            lax.all_gather(attn_grad.astype(jnp.bfloat16), "ka", axis=0, tiled=True).astype(
                attn_grad.dtype
            ),
            lax.all_gather(row_delta.astype(jnp.bfloat16), "ka", axis=0, tiled=True).astype(
                row_delta.dtype
            ),
        )
        zero_keys = jnp.zeros((key_rows, group_heads, HD), jnp.float32)
        step_bwd = functools.partial(
            backward_block, key_heads, value_heads, key_doc, key_pos, score_scale
        )
        (key_grad, value_grad), query_grad = lax.scan(
            step_bwd,
            (zero_keys, zero_keys),
            (
                query_blocks,
                doc_blocks,
                pos_blocks,
                local_max,
                factor,
                attn_grads.reshape(block_count, block_rows, group_heads, HD),
                delta_rows.reshape(block_count, block_rows, group_heads),
            ),
        )
        query_part = lax.psum_scatter(
            query_grad.reshape(query_rows, group_width).astype(jnp.bfloat16),
            "ka",
            scatter_dimension=0,
            tiled=True,
        ).astype(jnp.float32)
        key_value_part = lax.psum_scatter(
            jnp.stack(
                [
                    key_grad.reshape(key_rows, group_width),
                    value_grad.reshape(key_rows, group_width),
                ],
                axis=1,
            ).astype(jnp.bfloat16),
            "pb",
            scatter_dimension=0,
            tiled=True,
        ).astype(jnp.float32)
        mixed_grad = jnp.concatenate([query_part[:, None], key_value_part], axis=1).astype(
            jnp.bfloat16
        )
        step_qkv = jnp.einsum(
            "td,tkn->dkn", normed_low, mixed_grad, preferred_element_type=jnp.float32
        )
        normed_grad = lax.psum(
            jnp.einsum(
                "tkn,dkn->td", mixed_grad, qkv_full, preferred_element_type=jnp.float32
            ).astype(jnp.bfloat16),
            "ha",
        ).astype(jnp.float32)
        input_part, gain_one, shift_one = norm_pull(normed_grad)
        input_grads.append(middle_grad + input_part)
        step_norm = jnp.stack([gain_one, gain_two, shift_one, shift_two])
        step_terms = (step_qkv, step_proj, step_inner, step_outer, step_norm)
        grad_sums = tuple(map(jnp.add, grad_sums, step_terms))
    grad_sums = (
        lax.psum_scatter(grad_sums[0], ("pb", "ka"), scatter_dimension=0, tiled=True),
        lax.psum_scatter(grad_sums[1], ("pb", "ka"), scatter_dimension=1, tiled=True),
        lax.psum_scatter(grad_sums[2], ("pb", "ka"), scatter_dimension=0, tiled=True),
        lax.psum_scatter(grad_sums[3], ("pb", "ka"), scatter_dimension=1, tiled=True),
        lax.psum_scatter(grad_sums[4], ("pb", "ka"), scatter_dimension=1, tiled=True),
    )
    grads_mean = tuple((summed / MICRO for summed in grad_sums))
    qkv_out = adam_step(w_qkv, qkv_first, qkv_second, grads_mean[0], RATE_MATRIX, DECAY_RATE)
    proj_out = adam_step(w_proj, proj_first, proj_second, grads_mean[1], RATE_PROJ, DECAY_RATE)
    inner_out = adam_step(
        w_inner, inner_first, inner_second, grads_mean[2], RATE_MATRIX, DECAY_RATE
    )
    outer_out = adam_step(
        w_outer, outer_first, outer_second, grads_mean[3], RATE_MATRIX, DECAY_RATE
    )
    norm_master = jnp.concatenate([norm_gains, norm_biases], axis=0)
    norm_out = adam_step(norm_master, norm_first, norm_second, grads_mean[4], RATE_NORM, 0.0)
    norm_two_grad = jnp.stack([grads_mean[4][1], grads_mean[4][3]])
    return (
        jnp.stack(layer_outs),
        jnp.stack(input_grads),
        qkv_out[0],
        qkv_out[1],
        qkv_out[2],
        proj_out[0],
        proj_out[1],
        proj_out[2],
        inner_out[0],
        inner_out[1],
        inner_out[2],
        outer_out[0],
        outer_out[1],
        outer_out[2],
        norm_out[0],
        norm_out[1],
        norm_out[2],
        norm_two_grad,
    )


def solution(mesh):
    in_specs = (
        P(None, ("pb", "ka"), None),
        P(None, ("pb", "ka"), None),
        P(),
        P(),
        P(("pb", "ka"), None, "ha"),
        P("ha", ("pb", "ka")),
        P(("pb", "ka"), "ha"),
        P("ha", ("pb", "ka")),
        P(None, ("pb", "ka")),
        P(None, ("pb", "ka")),
        P(("pb", "ka"), None, "ha"),
        P(("pb", "ka"), None, "ha"),
        P("ha", ("pb", "ka")),
        P("ha", ("pb", "ka")),
        P(("pb", "ka"), "ha"),
        P(("pb", "ka"), "ha"),
        P("ha", ("pb", "ka")),
        P("ha", ("pb", "ka")),
        P(None, ("pb", "ka")),
        P(None, ("pb", "ka")),
    )
    out_specs = (
        P(None, ("pb", "ka"), None),
        P(None, ("pb", "ka"), None),
        P(("pb", "ka"), None, "ha"),
        P(("pb", "ka"), None, "ha"),
        P(("pb", "ka"), None, "ha"),
        P("ha", ("pb", "ka")),
        P("ha", ("pb", "ka")),
        P("ha", ("pb", "ka")),
        P(("pb", "ka"), "ha"),
        P(("pb", "ka"), "ha"),
        P(("pb", "ka"), "ha"),
        P("ha", ("pb", "ka")),
        P("ha", ("pb", "ka")),
        P("ha", ("pb", "ka")),
        P(None, ("pb", "ka")),
        P(None, ("pb", "ka")),
        P(None, ("pb", "ka")),
        P(None, ("pb", "ka")),
    )
    return jax.shard_map(shards, mesh=mesh, in_specs=in_specs, out_specs=out_specs, check_vma=False)
```

profile of v0, /device:TPU:0, one launch (start us, length us, event | category | flops | bytes accessed | tf_op | source)
XLA Modules:
  0.0 1002.9 jit_solution(6087380409959311369)
XLA Ops:
  9.6 22.9 %all-gather.7 = bf16[16,48,2]{1,2,0:T(2,128)(2,1)S(1)} all-gather(bf16[1,48,2]{1,2,0:T(2,128)(2,1)S(1)} %convert_bitcast_fusion.8), channel_id=1, replica_groups=mesh['pb'=4,'ka'=4,'ha'=2] {'pb','ka'}, dimensions={0}, use_global_device_ids=true | all-gather | bytes 3264 | tf_op jit(solution)/shard_map/all_gather | solution.py:164
  33.3 17.4 %all-gather.6 = bf16[16,48,2]{1,2,0:T(2,128)(2,1)S(1)} all-gather(bf16[1,48,2]{1,2,0:T(2,128)(2,1)S(1)} %convert_bitcast_fusion.9), channel_id=1, replica_groups=mesh['pb'=4,'ka'=4,'ha'=2] {'pb','ka'}, dimensions={0}, use_global_device_ids=true | all-gather | bytes 3264 | tf_op jit(solution)/shard_map/all_gather | solution.py:163
  60.1 7.6 all-gather
  67.9 18.7 %all-gather.22.cloned.1.call-done = bf16[768,2,384]{2,0,1:T(8,128)(2,1)} async-done(((bf16[192,2,384]{2,0,1:T(8,128)(2,1)}), bf16[768,2,384]{2,0,1:T(8,128)(2,1)}) %all-gather.22.cloned.1.call-update) | async-done | bytes 1179664 | tf_op jit(solution)/shard_map/all_gather | solution.py:203
  88.5 8.8 select_reduce_fusion.1
  97.4 11.7 %fusion.17 = (bf16[6,768]{1,0:T(8,128)(2,1)S(1)}, bf16[6,768,768]{1,2,0:T(8,128)(2,1)}) fusion(f32[6,768,768]{1,2,0:T(8,128)S(1)} %get-tuple-element.630, f32[6,768]{1,0:T(8,128)S(1)} %get-tuple-element.629, pred[768,768]{0,1:T(8,128)(4,1)S(1)} %compare_and_fusion.1), kind=kLoop, calls=%fused_computation.29 | loop fusion | flops 31845888 | bytes 21851136 | tf_op jit(solution)/shard_map/while/body/eval_jaxpr/reduce_sum | solution.py:75
  109.1 5.2 all-gather.8
  114.3 5.2 all-gather.9
  120.3 4.4 fusion.22
  125.9 21.4 %all_gather.65 = bf16[384,768]{0,1:T(8,128)(2,1)S(1)} all-gather(bf16[384,48]{0,1:T(8,128)(2,1)S(1)} %convert_element_type.458), channel_id=1, replica_groups=mesh['pb'=4,'ka'=4,'ha'=2] {'pb','ka'}, dimensions={1}, use_global_device_ids=true | all-gather | bytes 626688 | tf_op jit(solution)/shard_map/all_gather | solution.py:160
  149.8 23.7 %all-reduce.7.cloned.1.call-done = bf16[192,768]{1,0:T(8,128)(2,1)} async-done(((bf16[192,768]{1,0:T(8,128)(2,1)}), bf16[192,768]{1,0:T(8,128)(2,1)}) %all-reduce.7.cloned.1.call-update) | async-done | bytes 294928 | tf_op jit(solution)/shard_map/psum | solution.py:223
  178.4 7.5 all-gather.3
  186.2 21.8 %all-gather.28.cloned.1.call-done = bf16[768,2,384]{2,0,1:T(8,128)(2,1)} async-done(((bf16[192,2,384]{2,0,1:T(8,128)(2,1)}), bf16[768,2,384]{2,0,1:T(8,128)(2,1)}) %all-gather.28.cloned.1.call-update) | async-done | bytes 1179664 | tf_op jit(solution)/shard_map/all_gather | solution.py:203
  212.0 8.8 select_reduce_fusion
  220.9 11.6 %fusion.16 = (bf16[6,768]{1,0:T(8,128)(2,1)S(1)}, bf16[6,768,768]{1,2,0:T(8,128)(2,1)}) fusion(f32[6,768,768]{1,2,0:T(8,128)S(1)} %get-tuple-element.632, f32[6,768]{1,0:T(8,128)S(1)} %get-tuple-element.631, pred[768,768]{0,1:T(8,128)(4,1)S(1)} %compare_and_fusion), kind=kLoop, calls=%fused_computation.24 | loop fusion | flops 31845888 | bytes 21851136 | tf_op jit(solution)/shard_map/while/body/eval_jaxpr/reduce_sum | solution.py:75
  232.5 5.2 all-gather.10
  237.8 5.2 all-gather.11
  244.5 4.4 fusion.23
  250.0 21.3 %reduce-scatter.16.cloned.1.call-done = bf16[192,384]{1,0:T(8,128)(2,1)} async-done(((bf16[768,384]{1,0:T(8,128)(2,1)}), bf16[192,384]{1,0:T(8,128)(2,1)}) %reduce-scatter.16.cloned.1.call-update) | async-done | bytes 147472 | tf_op jit(solution)/shard_map/reduce_scatter | solution.py:216
  274.6 23.3 %all-reduce.9.cloned.1.call-done = bf16[192,768]{1,0:T(8,128)(2,1)} async-done(((bf16[192,768]{1,0:T(8,128)(2,1)}), bf16[192,768]{1,0:T(8,128)(2,1)}) %all-reduce.9.cloned.1.call-update) | async-done | bytes 294928 | tf_op jit(solution)/shard_map/psum | solution.py:223
  300.9 42.2 %all-gather.24.cloned.1.call-done = bf16[768,1536]{1,0:T(8,128)(2,1)} async-done(((bf16[48,1536]{1,0:T(8,128)(2,1)}), bf16[768,1536]{1,0:T(8,128)(2,1)}) %all-gather.24.cloned.1.call-update) | async-done | bytes 2359312 | tf_op jit(solution)/shard_map/all_gather | solution.py:161
  349.4 3.1 convolution_add_fusion
  352.6 74.5 %reduce-scatter.32.cloned.1.call-done = f32[1536,48]{0,1:T(8,128)} async-done(((f32[1536,768]{0,1:T(8,128)}), f32[1536,48]{0,1:T(8,128)}) %reduce-scatter.32.cloned.1.call-update) | async-done | bytes 294928 | tf_op jit(solution)/shard_map/reduce_scatter | solution.py:324
  429.6 41.8 %all-gather.26.cloned.1.call-done = bf16[1536,768]{0,1:T(8,128)(2,1)} async-done(((bf16[1536,48]{0,1:T(8,128)(2,1)}), bf16[1536,768]{0,1:T(8,128)(2,1)}) %all-gather.26.cloned.1.call-update) | async-done | bytes 2359312 | tf_op jit(solution)/shard_map/all_gather | solution.py:162
  471.4 3.3 fusion.43
  479.4 29.1 %all-reduce.13.cloned.1.call-done = (bf16[192,768]{1,0:T(8,128)(2,1)}, bf16[192,768]{1,0:T(8,128)(2,1)}) async-done(((bf16[192,768]{1,0:T(8,128)(2,1)}, bf16[192,768]{1,0:T(8,128)(2,1)}), (bf16[192,768]{1,0:T(8,128)(2,1)}, bf16[192,768]{1,0:T(8,128)(2,1)})) %all-reduce.13.cloned.1.call-update) | async-done | bytes 589840 | tf_op jit(solution)/shard_map/psum | solution.py:248
  514.6 8.0 all_gather.74
  526.8 5.4 all-gather.13
  534.2 19.5 %fusion.18 = bf16[6,768,768]{1,2,0:T(8,128)(2,1)S(1)} fusion(f32[6,768,768]{1,2,0:T(8,128)} %copy-done.9, bf16[768,6,64]{0,2,1:T(8,128)(2,1)} %bitcast.379, f32[6,768]{1,0:T(8,128)} %bitcast.406, f32[6,768]{1,0:T(8,128)} %get-tuple-element.618, f32[6,768]{1,0:T(8,128)} %copy-done.57, pred[768,768]{0,1:T(8,128)(4,1)} %copy-done.40, ...), kind=kOutput, calls=%fused_computation.32 | convolution fusion | flops 517275648 | bytes 23666688 | tf_op jit(solution)/shard_map/while/body/eval_jaxpr/qhe,khe->hqk/dot_general | solution.py:91
  558.9 6.1 convolution_convert_fusion
  567.1 5.5 fusion.27
  574.7 9.1 all_gather.72
  585.2 5.2 all-gather.12
  593.9 17.9 %fusion.19 = bf16[6,768,768]{1,2,0:T(8,128)(2,1)S(1)} fusion(f32[6,768,768]{1,2,0:T(8,128)} %copy-done.8, bf16[768,6,64]{0,2,1:T(8,128)(2,1)S(1)} %bitcast.375, f32[6,768]{1,0:T(8,128)} %bitcast.405, f32[6,768]{1,0:T(8,128)} %get-tuple-element.616, f32[6,768]{1,0:T(8,128)} %copy-done.56, pred[768,768]{0,1:T(8,128)(4,1)} %copy-done.38, ...), kind=kOutput, calls=%fused_computation.33 | convolution fusion | flops 517275648 | bytes 23666688 | tf_op jit(solution)/shard_map/while/body/eval_jaxpr/qhe,khe->hqk/dot_general | solution.py:91
  615.8 6.2 convolution_convert_fusion.1
  623.3 5.2 fusion.25
  630.1 4.0 convolution_convert_fusion.8
  635.9 3.1 fusion.29
  639.0 7.1 reduce-scatter.18.cloned.1.call-done
  646.1 31.4 %reduce-scatter.20.cloned.1.call-done = bf16[192,2,384]{2,0,1:T(8,128)(2,1)} async-done(((bf16[768,2,384]{2,0,1:T(8,128)(2,1)}), bf16[192,2,384]{2,0,1:T(8,128)(2,1)}) %reduce-scatter.20.cloned.1.call-update) | async-done | bytes 294928 | tf_op jit(solution)/shard_map/reduce_scatter | solution.py:291
  677.5 3.1 fusion.28
  684.9 4.2 fusion.138
  689.1 34.0 %all-reduce.11.cloned.1.call-done = (bf16[192,768]{1,0:T(8,128)(2,1)}, bf16[192,768]{1,0:T(8,128)(2,1)}, bf16[192,768]{1,0:T(8,128)(2,1)}, bf16[192,768]{1,0:T(8,128)(2,1)}) async-done(((bf16[192,768]{1,0:T(8,128)(2,1)}, bf16[192,768]{1,0:T(8,128)(2,1)}, bf16[192,768]{1,0:T(8,128)(2,1)}, bf16[192,768]{1,0:T(8,128)(2,1)}), (bf16[192,768]{1,0:T(8,128)(2,1)}, bf16[192,768]{1,0:T(8,128)(2,1)}, ...) | async-done | bytes 1179664 | tf_op jit(solution)/shard_map/psum | solution.py:235
  728.6 5.4 convolution_add_fusion.1
  738.6 47.0 %reduce-scatter.28.cloned.1.call-done = f32[384,48]{0,1:T(8,128)} async-done(((f32[384,768]{0,1:T(8,128)}), f32[384,48]{0,1:T(8,128)}) %reduce-scatter.28.cloned.1.call-update) | async-done | bytes 73744 | tf_op jit(solution)/shard_map/reduce_scatter | solution.py:322
  792.1 51.9 %reduce-scatter.34.cloned.1.call-done = f32[48,4]{1,0:T(8,128)} async-done(((f32[768,4]{1,0:T(8,128)}), f32[48,4]{1,0:T(8,128)}) %reduce-scatter.34.cloned.1.call-update) | async-done | bytes 784
  846.0 76.5 %reduce-scatter.30.cloned.1.call-done = f32[48,1536]{1,0:T(8,128)} async-done(((f32[768,1536]{1,0:T(8,128)}), f32[48,1536]{1,0:T(8,128)}) %reduce-scatter.30.cloned.1.call-update) | async-done | bytes 294928 | tf_op jit(solution)/shard_map/reduce_scatter | solution.py:323
  924.5 69.3 %reduce-scatter.26.cloned.1.call-done = f32[48,3,384]{2,0,1:T(8,128)} async-done(((f32[768,3,384]{2,0,1:T(8,128)}), f32[48,3,384]{2,0,1:T(8,128)}) %reduce-scatter.26.cloned.1.call-update) | async-done | bytes 221200 | tf_op jit(solution)/shard_map/reduce_scatter | solution.py:321
  (414 shorter events, 111.7 us)
Async XLA Ops:
  7.2 46.9 %all-gather.20.cloned.1.call-start = ((), (), s32[]{:S(2)}) async-start(), calls=%async_computation.11 | async-start | bytes 1880064 | tf_op jit(solution)/shard_map/all_gather | solution.py:159
  8.9 77.8 %all-gather.22.cloned.1.call-start = ((), (), s32[]{:S(2)}) async-start(), calls=%async_computation.12 | async-start | bytes 1474560 | tf_op jit(solution)/shard_map/all_gather | solution.py:203
  50.8 125.0 %copy-start.60 = (f32[768]{0:T(1024)}, f32[768]{0:T(1024)S(1)}, u32[]{:S(2)}) copy-start(f32[768]{0:T(1024)S(1)} %get-tuple-element.635) | copy-start | bytes 9220
  50.9 125.0 %copy-start.64 = (f32[768]{0:T(1024)}, f32[768]{0:T(1024)S(1)}, u32[]{:S(2)}) copy-start(f32[768]{0:T(1024)S(1)} %get-tuple-element.533) | copy-start | bytes 9220
  57.1 90.4 %reduce-scatter.14.cloned.1.call-start = ((), (), s32[]{:S(2)}) async-start(), calls=%async_computation.13 | async-start | bytes 737280 | tf_op jit(solution)/shard_map/reduce_scatter | solution.py:216
  124.7 48.8 %copy-start = (bf16[2,192,768]{2,1,0:T(8,128)(2,1)S(1)}, bf16[2,192,768]{2,1,0:T(8,128)(2,1)}, u32[]{:S(2)}) copy-start(bf16[2,192,768]{2,1,0:T(8,128)(2,1)} %param.24) | copy-start | bytes 1769476
  125.8 50.1 %copy-start.113 = (bf16[768,3,384]{2,0,1:T(8,128)(2,1)S(1)}, bf16[768,3,384]{2,0,1:T(8,128)(2,1)}, u32[]{:S(2)}) copy-start(bf16[768,3,384]{2,0,1:T(8,128)(2,1)} %all-gather.20.cloned.1.call-done) | copy-start | bytes 5308420
  125.8 47.7 %all-reduce.7.cloned.1.call-start = ((), (), s32[]{:S(2)}) async-start(), calls=%async_computation.14 | async-start | bytes 589824 | tf_op jit(solution)/shard_map/psum | solution.py:223
  149.5 58.4 %all-gather.28.cloned.1.call-start = ((), (), s32[]{:S(2)}) async-start(), calls=%async_computation.17 | async-start | bytes 1474560 | tf_op jit(solution)/shard_map/all_gather | solution.py:203
  177.4 93.9 %reduce-scatter.16.cloned.1.call-start = ((), (), s32[]{:S(2)}) async-start(), calls=%async_computation.18 | async-start | bytes 737280 | tf_op jit(solution)/shard_map/reduce_scatter | solution.py:216
  178.4 42.5 %copy-start.40 = (pred[768,768]{0,1:T(8,128)(4,1)}, pred[768,768]{0,1:T(8,128)(4,1)S(1)}, u32[]{:S(2)}) copy-start(pred[768,768]{0,1:T(8,128)(4,1)S(1)} %compare_and_fusion) | copy-start | bytes 1769476
  248.9 49.0 %copy-start.6 = (bf16[192,768]{1,0:T(8,128)(2,1)S(1)}, bf16[192,768]{1,0:T(8,128)(2,1)}, u32[]{:S(2)}) copy-start(bf16[192,768]{1,0:T(8,128)(2,1)} %all-reduce.7.cloned.1.call-done) | copy-start | bytes 884740
  250.0 47.9 %all-reduce.9.cloned.1.call-start = ((), (), s32[]{:S(2)}) async-start(), calls=%async_computation.19 | async-start | bytes 589824 | tf_op jit(solution)/shard_map/psum | solution.py:223
  273.3 69.7 %all-gather.24.cloned.1.call-start = ((), (), s32[]{:S(2)}) async-start(), calls=%async_computation.15 | async-start | bytes 2506752 | tf_op jit(solution)/shard_map/all_gather | solution.py:161
  274.1 153.0 %reduce-scatter.32.cloned.1.call-start = ((), (), s32[]{:S(2)}) async-start(), calls=%async_computation.27 | async-start | bytes 5013504 | tf_op jit(solution)/shard_map/reduce_scatter | solution.py:324
  274.6 236.4 %copy-start.73 = (f32[192]{0:T(256)}, f32[192]{0:T(256)S(1)}, u32[]{:S(2)}) copy-start(f32[192]{0:T(256)S(1)} %broadcast_multiply_fusion.3) | copy-start | bytes 2308
  299.1 44.0 %copy-start.100 = (f32[192]{0:T(256)}, f32[192]{0:T(256)S(1)}, u32[]{:S(2)}) copy-start(f32[192]{0:T(256)S(1)} %get-tuple-element.518) | copy-start | bytes 2308
  300.3 42.8 %copy-start.96 = (f32[192]{0:T(256)}, f32[192]{0:T(256)S(1)}, u32[]{:S(2)}) copy-start(f32[192]{0:T(256)S(1)} %multiply_reduce_fusion) | copy-start | bytes 2308
  300.3 42.8 %copy-start.77 = (f32[192]{0:T(256)}, f32[192]{0:T(256)S(1)}, u32[]{:S(2)}) copy-start(f32[192]{0:T(256)S(1)} %fusion.119) | copy-start | bytes 2308
  352.6 118.9 %all-gather.26.cloned.1.call-start = ((), (), s32[]{:S(2)}) async-start(), calls=%async_computation.16 | async-start | bytes 2506752 | tf_op jit(solution)/shard_map/all_gather | solution.py:162
  429.6 78.9 %all-reduce.13.cloned.1.call-start = ((), (), s32[]{:S(2)}) async-start(), calls=%async_computation.30 | async-start | bytes 1179648 | tf_op jit(solution)/shard_map/psum | solution.py:248
  479.3 156.6 %reduce-scatter.22.cloned.1.call-start = ((), (), s32[]{:S(2)}) async-start(), calls=%async_computation.22 | async-start | bytes 737280 | tf_op jit(solution)/shard_map/reduce_scatter | solution.py:285
  558.8 77.1 %reduce-scatter.24.cloned.1.call-start = ((), (), s32[]{:S(2)}) async-start(), calls=%async_computation.23 | async-start | bytes 1474560 | tf_op jit(solution)/shard_map/reduce_scatter | solution.py:291
  593.6 52.5 %reduce-scatter.18.cloned.1.call-start = ((), (), s32[]{:S(2)}) async-start(), calls=%async_computation.20 | async-start | bytes 737280 | tf_op jit(solution)/shard_map/reduce_scatter | solution.py:285
  615.7 61.7 %reduce-scatter.20.cloned.1.call-start = ((), (), s32[]{:S(2)}) async-start(), calls=%async_computation.21 | async-start | bytes 1474560 | tf_op jit(solution)/shard_map/reduce_scatter | solution.py:291
  630.1 93.1 %all-reduce.11.cloned.1.call-start = ((), (), s32[]{:S(2)}) async-start(), calls=%async_computation.29 | async-start | bytes 2359296 | tf_op jit(solution)/shard_map/psum | solution.py:235
  680.6 105.0 %reduce-scatter.28.cloned.1.call-start = ((), (), s32[]{:S(2)}) async-start(), calls=%async_computation.25 | async-start | bytes 1253376 | tf_op jit(solution)/shard_map/reduce_scatter | solution.py:322
  684.5 40.2 %copy-start.81 = (f32[192]{0:T(256)S(1)}, f32[192]{0:T(256)}, u32[]{:S(2)}) copy-start(f32[192]{0:T(256)} %copy-done.80) | copy-start | bytes 2308
  684.5 159.4 %reduce-scatter.34.cloned.1.call-start = ((), (), s32[]{:S(2)}) async-start(), calls=%async_computation.28 | async-start | bytes 417792
  728.5 193.9 %reduce-scatter.30.cloned.1.call-start = ((), (), s32[]{:S(2)}) async-start(), calls=%async_computation.26 | async-start | bytes 5013504 | tf_op jit(solution)/shard_map/reduce_scatter | solution.py:323
  734.0 259.7 %reduce-scatter.26.cloned.1.call-start = ((), (), s32[]{:S(2)}) async-start(), calls=%async_computation.24 | async-start | bytes 3760128 | tf_op jit(solution)/shard_map/reduce_scatter | solution.py:321
  738.5 51.0 %copy-start.17 = (f32[192,768]{1,0:T(8,128)S(1)}, f32[192,768]{1,0:T(8,128)}, u32[]{:S(2)}) copy-start(f32[192,768]{1,0:T(8,128)} %copy-done.16) | copy-start | bytes 1769476
  738.5 51.0 %copy-start.19 = (f32[192,768]{1,0:T(8,128)S(1)}, f32[192,768]{1,0:T(8,128)}, u32[]{:S(2)}) copy-start(f32[192,768]{1,0:T(8,128)} %copy-done.18) | copy-start | bytes 1769476
  738.5 51.0 %copy-start.28 = (bf16[192,768]{1,0:T(8,128)(2,1)S(1)}, bf16[192,768]{1,0:T(8,128)(2,1)}, u32[]{:S(2)}) copy-start(bf16[192,768]{1,0:T(8,128)(2,1)} %get-tuple-element.568) | copy-start | bytes 884740
  738.5 51.0 %copy-start.29 = (bf16[192,768]{1,0:T(8,128)(2,1)S(1)}, bf16[192,768]{1,0:T(8,128)(2,1)}, u32[]{:S(2)}) copy-start(bf16[192,768]{1,0:T(8,128)(2,1)} %get-tuple-element.569) | copy-start | bytes 884740
  738.5 51.0 %copy-start.69 = (f32[192]{0:T(256)S(1)}, f32[192]{0:T(256)}, u32[]{:S(2)}) copy-start(f32[192]{0:T(256)} %copy-done.67) | copy-start | bytes 2308
  738.5 51.0 %copy-start.72 = (f32[192]{0:T(256)S(1)}, f32[192]{0:T(256)}, u32[]{:S(2)}) copy-start(f32[192]{0:T(256)} %copy-done.70) | copy-start | bytes 2308
  738.5 51.0 %copy-start.82 = (f32[192]{0:T(256)S(1)}, f32[192]{0:T(256)}, u32[]{:S(2)}) copy-start(f32[192]{0:T(256)} %copy-done.80) | copy-start | bytes 2308
  790.8 53.9 %copy-start.105 = (f32[4,48]{1,0:T(4,128)S(1)}, f32[4,48]{1,0:T(4,128)}, u32[]{:S(2)}) copy-start(f32[4,48]{1,0:T(4,128)} %param.43) | copy-start | bytes 2308
  790.9 53.9 %copy-start.106 = (f32[4,48]{1,0:T(4,128)S(1)}, f32[4,48]{1,0:T(4,128)}, u32[]{:S(2)}) copy-start(f32[4,48]{1,0:T(4,128)} %param.42) | copy-start | bytes 2308
  790.9 53.9 %copy-start.108 = (f32[2,48]{1,0:T(2,128)S(1)}, f32[2,48]{1,0:T(2,128)}, u32[]{:S(2)}) copy-start(f32[2,48]{1,0:T(2,128)} %param.33) | copy-start | bytes 1156
  790.9 53.9 %copy-start.109 = (f32[2,48]{1,0:T(2,128)S(1)}, f32[2,48]{1,0:T(2,128)}, u32[]{:S(2)}) copy-start(f32[2,48]{1,0:T(2,128)} %param.32) | copy-start | bytes 1156
  790.9 131.6 %copy-start.47 = (f32[48,1536]{1,0:T(8,128)S(1)}, f32[48,1536]{1,0:T(8,128)}, u32[]{:S(2)}) copy-start(f32[48,1536]{1,0:T(8,128)} %param.30) | copy-start | bytes 884740
  790.9 131.5 %copy-start.53 = (f32[48,1536]{1,0:T(8,128)S(1)}, f32[48,1536]{1,0:T(8,128)}, u32[]{:S(2)}) copy-start(f32[48,1536]{1,0:T(8,128)} %param.39) | copy-start | bytes 884740
  790.9 131.5 %copy-start.54 = (f32[48,1536]{1,0:T(8,128)S(1)}, f32[48,1536]{1,0:T(8,128)}, u32[]{:S(2)}) copy-start(f32[48,1536]{1,0:T(8,128)} %param.38) | copy-start | bytes 884740
  790.9 202.8 %copy-start.50 = (f32[48,3,384]{2,0,1:T(8,128)S(1)}, f32[48,3,384]{2,0,1:T(8,128)}, u32[]{:S(2)}) copy-start(f32[48,3,384]{2,0,1:T(8,128)} %param.28) | copy-start | bytes 663556
  790.9 202.8 %copy-start.58 = (f32[48,3,384]{2,0,1:T(8,128)S(1)}, f32[48,3,384]{2,0,1:T(8,128)}, u32[]{:S(2)}) copy-start(f32[48,3,384]{2,0,1:T(8,128)} %param.35) | copy-start | bytes 663556
  791.0 202.8 %copy-start.59 = (f32[48,3,384]{2,0,1:T(8,128)S(1)}, f32[48,3,384]{2,0,1:T(8,128)}, u32[]{:S(2)}) copy-start(f32[48,3,384]{2,0,1:T(8,128)} %param.34) | copy-start | bytes 663556
  (86 other events, 894.0 us)
Sparse Core Ops, SparseCore 0:
  10.9 43.1 all-gather.19
  57.2 29.3 all-gather.21
  125.9 21.5 reduce-scatter.13
  150.2 23.2 all-reduce.6
  177.5 30.4 all-gather.27
  250.1 21.1 reduce-scatter.15
  274.2 23.6 all-reduce.8
  300.7 42.3 all-gather.23
  352.7 74.3 reduce-scatter.31
  430.0 41.3 all-gather.25
  479.4 28.9 all-reduce.12
  559.0 23.2 reduce-scatter.21
  593.7 29.1 reduce-scatter.23
  625.3 20.7 reduce-scatter.17
  648.3 29.1 reduce-scatter.19
  680.9 42.1 all-reduce.10
  727.6 57.9 reduce-scatter.27
  789.3 54.5 reduce-scatter.33
  847.8 74.5 reduce-scatter.29
  926.7 67.0 reduce-scatter.25
where the time goes:
time: 1010 us; the launch traced here: 1000 us
  waiting for transfers between devices  614 us (61%)
  matrix products  143 us (14%)
  blocking collectives  125 us (12%)
  other arithmetic  66 us (7%)
  local copies, waits for them, and re-layouts  35.7 us (4%)
  between operations  16.4 us (2%)
    reduce_scatter x1, waiting for transfers between devices, shards(): lax.psum_scatter(grad_sums[2], ('pb', 'ka'), scatter_dimension=0, tiled=T...  76.5 us
    reduce_scatter x1, waiting for transfers between devices, shards(): lax.psum_scatter(grad_sums[3], ('pb', 'ka'), scatter_dimension=1, tiled=T...  74.5 us
    reduce_scatter x1, waiting for transfers between devices, shards(): lax.psum_scatter(grad_sums[0], ('pb', 'ka'), scatter_dimension=0, tiled=T...  69.3 us
    unnamed x21, waiting for transfers between devices  52.3 us
    reduce_scatter x1, waiting for transfers between devices, shards(): lax.psum_scatter(grad_sums[1], ('pb', 'ka'), scatter_dimension=1, tiled=T...  47 us
    psum x2, waiting for transfers between devices, shards(): lax.psum(jnp.dot(attended_low, proj_full, preferred_element_type=jnp.floa...  47 us
    all_gather x1, waiting for transfers between devices, shards(): lax.all_gather(w_inner.astype(jnp.bfloat16), ('pb', 'ka'), axis=0, tiled=...  42.2 us
    all_gather x1, waiting for transfers between devices, shards(): lax.all_gather(w_outer.astype(jnp.bfloat16), ('pb', 'ka'), axis=1, tiled=...  41.8 us
  transfers between devices with their start and end apart: 20, of which 18 were waited for; matrix products, arithmetic and copies ran while one was open for 11% of the time, Pallas kernels for 0%

commit v1 on v0

v1 whole, which is shorter than its diff:
```python
import functools

import jax
import jax.numpy as jnp
from jax import lax
from jax.experimental import pallas as pl
from jax.experimental.pallas import tpu as pltpu
from jax.sharding import PartitionSpec as P

HD = 64
MICRO = 2
STEP = 8
NORM_EPS = 1e-05
BETA_ONE = 0.9
BETA_TWO = 0.95
ADAM_EPS = 1e-08
DECAY_RATE = 0.1
RATE_MATRIX = 0.02
RATE_PROJ = 0.6
RATE_NORM = 0.1
BF = jnp.bfloat16
F32 = jnp.float32
PLANE = ("pb", "ka")
VMEM_LIMIT = 60 * 1024 * 1024
SCORE_BLOCK = 512
SORT_BLOCK = 256
NT = (((1,), (1,)), ((), ()))
NN = (((1,), (0,)), ((), ()))
TN = (((0,), (0,)), ((), ()))


def dot(a, b, dims=NN):
    return lax.dot_general(a, b, dims, preferred_element_type=F32)


def params(steps=1):
    return pltpu.CompilerParams(
        dimension_semantics=("arbitrary",) * steps, vmem_limit_bytes=VMEM_LIMIT
    )


def whole(shape):
    return pl.BlockSpec(shape, lambda *_: (0,) * len(shape))


def shape_of(shape, dtype):
    return jax.ShapeDtypeStruct(shape, dtype)


def head_places(group, heads):
    return tuple(h * group // heads for h in range(heads))


def one_hot(mask):
    return jnp.where(mask, 1.0, 0.0).astype(BF)


def normalize(x):
    center = x - jnp.mean(x, axis=-1, keepdims=True)
    spread = jnp.mean(center * center, axis=-1, keepdims=True)
    scale = lax.rsqrt(spread + NORM_EPS)
    return center * scale, scale


def normalize_back(grad, unit, scale):
    return scale * (
        grad
        - jnp.mean(grad, axis=-1, keepdims=True)
        - unit * jnp.mean(grad * unit, axis=-1, keepdims=True)
    )


def qkv_kernel(x_ref, w_ref, norm_ref, h_ref, qkv_ref):
    unit, _ = normalize(x_ref[...].astype(F32))
    h = (unit * norm_ref[0:1, :] + norm_ref[2:3, :]).astype(BF)
    h_ref[...] = h
    qkv_ref[...] = dot(h, w_ref[...]).astype(BF)


def qkv_of_head(x_full, head_w, norms):
    rows, width = x_full.shape
    block = min(512, rows)
    return pl.pallas_call(
        qkv_kernel,
        grid=(rows // block,),
        in_specs=[
            pl.BlockSpec((block, width), lambda i: (i, 0)),
            whole(head_w.shape),
            whole(norms.shape),
        ],
        out_specs=[
            pl.BlockSpec((block, width), lambda i: (i, 0)),
            pl.BlockSpec((block, head_w.shape[1]), lambda i: (i, 0)),
        ],
        out_shape=[shape_of((rows, width), BF), shape_of((rows, head_w.shape[1]), BF)],
        compiler_params=params(),
        name="qkv_head",
    )(x_full, head_w, norms)


def picked_rows(row_ids, first, count, source_ref, chunk):
    total = None
    wanted = first + lax.broadcasted_iota(jnp.int32, (count, 1), 0)
    for part in range(source_ref.shape[0] // chunk):
        cut = slice(part * chunk, (part + 1) * chunk)
        piece = dot(one_hot(row_ids[:, cut] == wanted), source_ref[cut, :])
        total = piece if total is None else total + piece
    return total


def sort_kernel(chunk, tok_ref, qkv_ref, q_ref, k_ref, v_ref, vt_ref):
    count = q_ref.shape[0]
    rows = picked_rows(tok_ref, pl.program_id(0) * count, count, qkv_ref, chunk)
    q_ref[...] = (rows[:, :HD] * float(HD) ** -0.5).astype(BF)
    k_ref[...] = rows[:, HD : 2 * HD].astype(BF)
    value = rows[:, 2 * HD : 3 * HD]
    v_ref[...] = value.astype(BF)
    vt_ref[...] = value.T.astype(BF)


def sort_qkv(tok_row, qkv):
    rows = qkv.shape[0]
    block = min(SORT_BLOCK, rows)
    narrow = pl.BlockSpec((block, HD), lambda i: (i, 0))
    return pl.pallas_call(
        functools.partial(sort_kernel, min(3072, rows)),
        grid=(rows // block,),
        in_specs=[whole(tok_row.shape), whole(qkv.shape)],
        out_specs=[narrow, narrow, narrow, pl.BlockSpec((HD, block), lambda i: (0, i))],
        out_shape=[shape_of((rows, HD), BF)] * 3 + [shape_of((HD, rows), BF)],
        compiler_params=params(),
        name="sort_qkv",
    )(tok_row, qkv)


def causal(block):
    return lax.broadcasted_iota(jnp.int32, (block, block), 0) <= lax.broadcasted_iota(
        jnp.int32, (block, block), 1
    )


def forward_kernel(first_ref, q_ref, k_ref, vt_ref, o_ref, low_ref, lse_ref):
    block = q_ref.shape[0]
    index = pl.program_id(0)
    query = q_ref[...]

    def step(key_block, state, diagonal):
        top, total, acc = state
        at = pl.multiple_of(key_block * block, block)
        scores = dot(k_ref[pl.ds(at, block), :], query, NT)
        square = scores * scores + 1.0
        inverse = lax.rsqrt(square)
        radius = square * inverse
        if diagonal:
            radius = jnp.where(causal(block), radius, -1e30)
        new_top = jnp.maximum(top, jnp.max(radius, axis=0, keepdims=True))
        weights = jnp.exp(radius - new_top)
        shrink = jnp.exp(top - new_top)
        signed = (scores * inverse * weights).astype(BF)
        acc = acc * shrink + dot(vt_ref[:, pl.ds(at, block)], signed)
        total = total * shrink + jnp.sum(weights, axis=0, keepdims=True)
        return (new_top, total, acc)

    state = (
        jnp.zeros((1, block), F32),
        jnp.zeros((1, block), F32),
        jnp.zeros((HD, block), F32),
    )
    state = lax.fori_loop(first_ref[index], index, lambda j, s: step(j, s, False), state)
    top, total, acc = step(index, state, True)
    out = acc * (1.0 / total)
    o_ref[...] = out
    low_ref[...] = out.astype(BF)
    lse_ref[...] = top + jnp.log(total)


def attend(first_block, q, k, vt, block):
    rows = q.shape[0]
    return pl.pallas_call(
        forward_kernel,
        grid_spec=pltpu.PrefetchScalarGridSpec(
            num_scalar_prefetch=1,
            grid=(rows // block,),
            in_specs=[
                pl.BlockSpec((block, HD), lambda i, *_: (i, 0)),
                whole(k.shape),
                whole(vt.shape),
            ],
            out_specs=[
                pl.BlockSpec((HD, block), lambda i, *_: (0, i)),
                pl.BlockSpec((HD, block), lambda i, *_: (0, i)),
                pl.BlockSpec((1, block), lambda i, *_: (0, i)),
            ],
        ),
        out_shape=[shape_of((HD, rows), F32), shape_of((HD, rows), BF), shape_of((1, rows), F32)],
        compiler_params=params(),
        name="attend_fwd",
    )(first_block, q, k, vt)


def slots_out_kernel(chunk, tok_ref, low_ref, out_ref):
    rows = tok_ref.shape[0]
    total = None
    for part in range(low_ref.shape[1] // chunk):
        cut = slice(part * chunk, (part + 1) * chunk)
        token = part * chunk + lax.broadcasted_iota(jnp.int32, (1, chunk), 1)
        piece = dot(one_hot(tok_ref[...] == token), low_ref[:, cut], NT)
        total = piece if total is None else total + piece
    total = total.astype(BF)
    out_ref[0] = jnp.concatenate([total[: rows // 2], total[rows // 2 :]], axis=1)


def slots_out(tok_col, low, group):
    rows = tok_col.shape[0] // group
    return pl.pallas_call(
        functools.partial(slots_out_kernel, min(3072, low.shape[1])),
        grid=(group,),
        in_specs=[pl.BlockSpec((rows, 1), lambda i: (i, 0)), whole(low.shape)],
        out_specs=pl.BlockSpec((1, rows // 2, 2 * HD), lambda i: (i, 0, 0)),
        out_shape=shape_of((group, rows // 2, 2 * HD), BF),
        compiler_params=params(),
        name="slots_out",
    )(tok_col, low)


def sort_grad_kernel(chunk, tok_ref, packed_ref, o_ref, g_ref, delta_ref, flat_ref):
    group, half, _ = packed_ref.shape

    @pl.when(pl.program_id(0) == 0)
    def _():
        for d in range(group):
            piece = packed_ref[d]
            flat_ref[2 * d * half : (2 * d + 1) * half, :] = piece[:, :HD]
            flat_ref[(2 * d + 1) * half : (2 * d + 2) * half, :] = piece[:, HD:]

    count = g_ref.shape[0]
    rows = picked_rows(tok_ref, pl.program_id(0) * count, count, flat_ref, chunk)
    g_ref[...] = rows.astype(BF)
    delta_ref[...] = jnp.sum(rows.T * o_ref[...], axis=0, keepdims=True)


def sort_grad(tok_row, packed, o):
    rows = o.shape[1]
    block = min(SORT_BLOCK, rows)
    return pl.pallas_call(
        functools.partial(sort_grad_kernel, min(3072, rows)),
        grid=(rows // block,),
        in_specs=[
            whole(tok_row.shape),
            whole(packed.shape),
            pl.BlockSpec((HD, block), lambda i: (0, i)),
        ],
        out_specs=[
            pl.BlockSpec((block, HD), lambda i: (i, 0)),
            pl.BlockSpec((1, block), lambda i: (0, i)),
        ],
        out_shape=[shape_of((rows, HD), BF), shape_of((1, rows), F32)],
        scratch_shapes=[pltpu.VMEM((rows, HD), BF)],
        compiler_params=params(),
        name="sort_grad",
    )(tok_row, packed, o)


def backward_kernel(
    last_ref, q_ref, k_ref, v_ref, g_ref, lse_ref, delta_ref, out_ref, dq_ref, dk_ref, dv_ref
):
    block = k_ref.shape[0]
    index = pl.program_id(0)

    @pl.when(index == 0)
    def _():
        dq_ref[...] = jnp.zeros_like(dq_ref)

    key = k_ref[...]
    key_t = key.T
    value = v_ref[...]
    dk_ref[...] = jnp.zeros_like(dk_ref)
    dv_ref[...] = jnp.zeros_like(dv_ref)

    def step(query_block, diagonal):
        at = pl.multiple_of(query_block * block, block)
        query = q_ref[pl.ds(at, block), :]
        grad = g_ref[pl.ds(at, block), :]
        scores = dot(key, query, NT)
        square = scores * scores + 1.0
        inverse = lax.rsqrt(square)
        shifted = square * inverse - lse_ref[:, pl.ds(at, block)]
        if diagonal:
            shifted = jnp.where(causal(block), shifted, -1e30)
        weights = jnp.exp(shifted)
        slope = scores * inverse
        along = dot(value, grad, NT)
        bend = 1.0 + inverse * inverse * (inverse - 1.0)
        score_grad = weights * (bend * along - slope * delta_ref[:, pl.ds(at, block)])
        signed = (slope * weights).astype(BF)
        low_grad = score_grad.astype(BF)
        dv_ref[...] += dot(signed, grad)
        dk_ref[...] += dot(low_grad, query)
        dq_ref[:, pl.ds(at, block)] += dot(key_t, low_grad)

    step(index, True)

    def body(query_block, carry):
        step(query_block, False)
        return carry

    lax.fori_loop(index + 1, last_ref[index], body, 0)
    at = pl.multiple_of(index * block, block)
    dq = dq_ref[:, pl.ds(at, block)].T * float(HD) ** -0.5
    out_ref[...] = jnp.concatenate([dq, dk_ref[...], dv_ref[...]], axis=1).astype(BF)


def attend_back(last_block, q, k, v, g, lse, delta, block):
    rows = q.shape[0]
    return pl.pallas_call(
        backward_kernel,
        grid_spec=pltpu.PrefetchScalarGridSpec(
            num_scalar_prefetch=1,
            grid=(rows // block,),
            in_specs=[
                whole(q.shape),
                pl.BlockSpec((block, HD), lambda i, *_: (i, 0)),
                pl.BlockSpec((block, HD), lambda i, *_: (i, 0)),
                whole(g.shape),
                whole(lse.shape),
                whole(delta.shape),
            ],
            out_specs=pl.BlockSpec((block, 3 * HD), lambda i, *_: (i, 0)),
            scratch_shapes=[
                pltpu.VMEM((HD, rows), F32),
                pltpu.VMEM((block, HD), F32),
                pltpu.VMEM((block, HD), F32),
            ],
        ),
        out_shape=shape_of((rows, 3 * HD), BF),
        compiler_params=params(),
        name="attend_bwd",
    )(last_block, q, k, v, g, lse, delta)


def grads_out_kernel(chunk, tok_ref, grad_ref, out_ref):
    rows = tok_ref.shape[0]
    half = rows // 2
    total = None
    for part in range(grad_ref.shape[0] // chunk):
        cut = slice(part * chunk, (part + 1) * chunk)
        token = part * chunk + lax.broadcasted_iota(jnp.int32, (1, chunk), 1)
        piece = dot(one_hot(tok_ref[...] == token), grad_ref[cut, :])
        total = piece if total is None else total + piece
    total = total.astype(BF)
    out_ref[0, :rows, :] = total[:, : 2 * HD]
    out_ref[0, rows:, :] = jnp.concatenate(
        [total[:half, 2 * HD :], total[half:, 2 * HD :]], axis=1
    )


def grads_out(tok_col, grads, group):
    rows = tok_col.shape[0] // group
    out_rows = rows + rows // 2
    return pl.pallas_call(
        functools.partial(grads_out_kernel, min(3072, grads.shape[0])),
        grid=(group,),
        in_specs=[pl.BlockSpec((rows, 1), lambda i: (i, 0)), whole(grads.shape)],
        out_specs=pl.BlockSpec((1, out_rows, 2 * HD), lambda i: (i, 0, 0)),
        out_shape=shape_of((group, out_rows, 2 * HD), BF),
        compiler_params=params(),
        name="grads_out",
    )(tok_col, grads)


def head_weight_kernel(h_ref, packed_ref, out_ref, flat_ref, acc_ref):
    count, out_rows, _ = packed_ref.shape
    rows = out_rows // 3 * 2
    half = rows // 2
    for d in range(count):
        piece = packed_ref[d]
        low = slice(d * rows, d * rows + half)
        high = slice(d * rows + half, (d + 1) * rows)
        flat_ref[d * rows : (d + 1) * rows, : 2 * HD] = piece[:rows]
        flat_ref[low, 2 * HD :] = piece[rows:, :HD]
        flat_ref[high, 2 * HD :] = piece[rows:, HD:]
    term = dot(flat_ref[...], h_ref[...], TN)

    @pl.when(pl.program_id(0) == 0)
    def _():
        acc_ref[...] = term

    @pl.when(pl.program_id(0) > 0)
    def _():
        acc_ref[...] += term

    @pl.when(pl.program_id(0) == pl.num_programs(0) - 1)
    def _():
        out_ref[...] = acc_ref[...].T.astype(BF)


def head_weight_grad(h_full, packed):
    group, out_rows, _ = packed.shape
    rows, width = h_full.shape
    count = 4 if group % 4 == 0 else 1
    return pl.pallas_call(
        head_weight_kernel,
        grid=(group // count,),
        in_specs=[
            pl.BlockSpec((rows // group * count, width), lambda i: (i, 0)),
            pl.BlockSpec((count, out_rows, 2 * HD), lambda i: (i, 0, 0)),
        ],
        out_specs=whole((width, 3 * HD)),
        out_shape=shape_of((width, 3 * HD), BF),
        scratch_shapes=[
            pltpu.VMEM((rows // group * count, 3 * HD), BF),
            pltpu.VMEM((3 * HD, width), F32),
        ],
        compiler_params=params(),
        name="head_weight",
    )(h_full, packed)


def middle_kernel(places, x_ref, packed_ref, proj_ref, norm_ref, mid_ref, h_ref, o_ref):
    half = packed_ref.shape[1]
    for h, place in enumerate(places):
        piece = packed_ref[place]
        o_ref[:half, h * HD : (h + 1) * HD] = piece[:, :HD]
        o_ref[half:, h * HD : (h + 1) * HD] = piece[:, HD:]
    mid = x_ref[...].astype(F32) + dot(o_ref[...], proj_ref[...], NT)
    mid_ref[...] = mid
    unit, _ = normalize(mid)
    h_ref[...] = (unit * norm_ref[1:2, :] + norm_ref[3:4, :]).astype(BF)


def middle(places, x, packed, weights, proj_at, norms):
    rows, width = x.shape
    return pl.pallas_call(
        functools.partial(middle_kernel, places),
        grid=(1,),
        in_specs=[
            whole(x.shape),
            whole(packed.shape),
            pl.BlockSpec((width, width), lambda i: (0, proj_at)),
            whole(norms.shape),
        ],
        out_specs=[whole((rows, width))] * 3,
        out_shape=[
            shape_of((rows, width), F32),
            shape_of((rows, width), BF),
            shape_of((rows, width), BF),
        ],
        compiler_params=params(),
        name="middle",
    )(x, packed, weights, norms)


def hidden_kernel(h_ref, dy_ref, inner_ref, outer_ref, act_ref, dpre_ref, dh_ref, out_ref):
    pre = dot(h_ref[...], inner_ref[...])
    root = 0.7978845608028654
    squared = pre * pre
    bend = jnp.tanh(root * (pre + 0.044715 * (squared * pre)))
    act = (0.5 * pre * (1.0 + bend)).astype(BF)
    act_ref[...] = act
    slope = 0.5 * (1.0 + bend) + 0.5 * pre * (1.0 - bend * bend) * (
        root * (1.0 + 3.0 * 0.044715 * squared)
    )
    dpre = (dot(dy_ref[...], outer_ref[...]) * slope).astype(BF)
    dpre_ref[...] = dpre
    dh = dot(dpre, inner_ref[...], NT)
    out = dot(act, outer_ref[...], NT)

    @pl.when(pl.program_id(0) == 0)
    def _():
        dh_ref[...] = dh
        out_ref[...] = out

    @pl.when(pl.program_id(0) > 0)
    def _():
        dh_ref[...] += dh
        out_ref[...] += out


def hidden(h, dy, weights, hidden_width):
    rows, width = h.shape
    chunk = 512
    steps = hidden_width // chunk
    return pl.pallas_call(
        hidden_kernel,
        grid=(steps,),
        in_specs=[
            whole(h.shape),
            whole(dy.shape),
            pl.BlockSpec((width, chunk), lambda i: (0, i)),
            pl.BlockSpec((width, chunk), lambda i: (0, i + steps)),
        ],
        out_specs=[
            pl.BlockSpec((rows, chunk), lambda i: (0, i)),
            pl.BlockSpec((rows, chunk), lambda i: (0, i)),
            whole((rows, width)),
            whole((rows, width)),
        ],
        out_shape=[
            shape_of((rows, hidden_width), BF),
            shape_of((rows, hidden_width), BF),
            shape_of((rows, width), F32),
            shape_of((rows, width), F32),
        ],
        compiler_params=params(),
        name="hidden",
    )(h, dy, weights, weights)


def middle_back_kernel(
    places, own_ref, other_ref, dy_ref, mid_ref, norm_ref, proj_ref, dmid_ref, low_ref, packed_ref, sums_ref
):
    half = packed_ref.shape[1]
    dh = own_ref[...] + other_ref[...].astype(F32)
    unit, scale = normalize(mid_ref[...])
    sums_ref[0:1, :] = jnp.sum(dh * unit, axis=0, keepdims=True)
    sums_ref[1:2, :] = jnp.sum(dh, axis=0, keepdims=True)
    dmid = dy_ref[...].astype(F32) + normalize_back(dh * norm_ref[1:2, :], unit, scale)
    dmid_ref[...] = dmid
    low = dmid.astype(BF)
    low_ref[...] = low
    grad = dot(low, proj_ref[...]).astype(BF)
    packed_ref[...] = jnp.zeros_like(packed_ref)
    for h, place in enumerate(places):
        cut = slice(h * HD, (h + 1) * HD)
        packed_ref[place] = jnp.concatenate([grad[:half, cut], grad[half:, cut]], axis=1)


def middle_back(places, group, own, other, dy, mid, norms, weights, proj_at):
    rows, width = mid.shape
    return pl.pallas_call(
        functools.partial(middle_back_kernel, places),
        grid=(1,),
        in_specs=[
            whole(own.shape),
            whole(other.shape),
            whole(dy.shape),
            whole(mid.shape),
            whole(norms.shape),
            pl.BlockSpec((width, width), lambda i: (0, proj_at)),
        ],
        out_specs=[
            whole((rows, width)),
            whole((rows, width)),
            whole((group, rows // 2, 2 * HD)),
            whole((2, width)),
        ],
        out_shape=[
            shape_of((rows, width), F32),
            shape_of((rows, width), BF),
            shape_of((group, rows // 2, 2 * HD), BF),
            shape_of((2, width), F32),
        ],
        compiler_params=params(),
        name="middle_back",
    )(own, other, dy, mid, norms, weights)


def weight_kernel(span, h0, h1, p0, p1, dy0, dy1, a0, a1, low_ref, o_ref, out_ref):
    index = pl.program_id(0)

    @pl.when(index < span)
    def _():
        out_ref[...] = (dot(h0[...], p0[...], TN) + dot(h1[...], p1[...], TN)).astype(BF)

    @pl.when((index >= span) & (index < 2 * span))
    def _():
        out_ref[...] = (dot(dy0[...], a0[...], TN) + dot(dy1[...], a1[...], TN)).astype(BF)

    @pl.when(index == 2 * span)
    def _():
        out_ref[...] = dot(low_ref[...], o_ref[...], TN).astype(BF)


def weight_grads(h_pair, dpre_pair, dy_pair, act_pair, low, o):
    rows, width = o.shape
    span = act_pair[0].shape[1] // width
    first = pl.BlockSpec((rows, width), lambda i: (0, jnp.minimum(i, span - 1)))
    second = pl.BlockSpec((rows, width), lambda i: (0, jnp.clip(i - span, 0, span - 1)))
    plain = whole((rows, width))
    return pl.pallas_call(
        functools.partial(weight_kernel, span),
        grid=(2 * span + 1,),
        in_specs=[plain, plain, first, first, plain, plain, second, second, plain, plain],
        out_specs=pl.BlockSpec((width, width), lambda i: (0, i)),
        out_shape=shape_of((width, (2 * span + 1) * width), BF),
        compiler_params=params(),
        name="weight_grads",
    )(*h_pair, *dpre_pair, *dy_pair, *act_pair, low, o)


def input_back_kernel(places, packed_ref, w_ref, x_ref, dmid_ref, norm_ref, out_ref, sums_ref, flat_ref):
    rows, _ = x_ref.shape
    half = rows // 2
    for h, place in enumerate(places):
        at = 3 * HD * h
        piece = packed_ref[place]
        flat_ref[:, at : at + 2 * HD] = piece[:rows]
        flat_ref[:half, at + 2 * HD : at + 3 * HD] = piece[rows:, :HD]
        flat_ref[half:, at + 2 * HD : at + 3 * HD] = piece[rows:, HD:]
    dh = dot(flat_ref[...], w_ref[...], NT)
    unit, scale = normalize(x_ref[...].astype(F32))
    sums_ref[0:1, :] = jnp.sum(dh * unit, axis=0, keepdims=True)
    sums_ref[1:2, :] = jnp.sum(dh, axis=0, keepdims=True)
    out_ref[...] = (dmid_ref[...] + normalize_back(dh * norm_ref[0:1, :], unit, scale)).astype(BF)


def input_back(places, packed, weights, x, dmid, norms):
    rows, width = x.shape
    return pl.pallas_call(
        functools.partial(input_back_kernel, places),
        grid=(1,),
        in_specs=[whole(a.shape) for a in (packed, weights, x, dmid, norms)],
        out_specs=[whole((rows, width)), whole((2, width))],
        out_shape=[shape_of((rows, width), BF), shape_of((2, width), F32)],
        scratch_shapes=[pltpu.VMEM((rows, weights.shape[1]), BF)],
        compiler_params=params(),
        name="input_back",
    )(packed, weights, x, dmid, norms)


def adam_step(master, first_state, second_state, grad_term, step_rate, weight_decay):
    first_new = BETA_ONE * first_state + (1.0 - BETA_ONE) * grad_term
    second_new = BETA_TWO * second_state + (1.0 - BETA_TWO) * grad_term * grad_term
    first_hat = first_new / (1.0 - BETA_ONE**STEP)
    second_hat = second_new / (1.0 - BETA_TWO**STEP)
    master_new = master - step_rate * (
        first_hat / (jnp.sqrt(second_hat) + ADAM_EPS) + weight_decay * master
    )
    return (first_new, second_new, master_new)


def shards(
    tokens,
    cotangent,
    seq_lengths,
    slot_token,
    w_qkv,
    w_proj,
    w_inner,
    w_outer,
    norm_gains,
    norm_biases,
    qkv_first,
    qkv_second,
    proj_first,
    proj_second,
    inner_first,
    inner_second,
    outer_first,
    outer_second,
    norm_first,
    norm_second,
):
    side = lax.axis_index("ha")
    group = lax.axis_size("pb") * lax.axis_size("ka")
    rows, width = tokens.shape[1:]
    total = rows * group
    w_rows = w_qkv.shape[0]
    half_width = w_qkv.shape[2]
    heads = 2 * half_width // HD
    hidden_half = w_inner.shape[1]
    places = head_places(group, heads)
    head_at = [0] * group
    for h, place in enumerate(places):
        head_at[place] = h
    block = min(SCORE_BLOCK, total)

    def swap(a):
        return lax.ppermute(a, "ha", [(0, 1), (1, 0)])

    def ordered(own, other):
        return jnp.where(side == 0, own, other), jnp.where(side == 0, other, own)

    def own_micro(a):
        return lax.dynamic_index_in_dim(a, side, 0, False)

    def other_micro(a):
        return lax.dynamic_index_in_dim(a, 1 - side, 0, False)

    x = own_micro(tokens)
    x_full = lax.all_gather(x, PLANE, axis=0, tiled=True)
    mine = jnp.concatenate(
        [w_qkv.astype(BF).reshape(w_rows, 3 * half_width), w_proj.astype(BF).T], axis=1
    )
    low_half, high_half = ordered(mine, swap(mine))
    qkv_rows = jnp.concatenate(
        [
            a[:, : 3 * half_width].reshape(w_rows, 3, heads // 2, HD).swapaxes(1, 2)
            for a in (low_half, high_half)
        ],
        axis=1,
    ).reshape(w_rows, heads, 3 * HD)
    proj_rows = jnp.concatenate(
        [a[:, 3 * half_width :] for a in (low_half, high_half)], axis=1
    )
    norm_master = jnp.concatenate([norm_gains, norm_biases], axis=0)
    head_rows = jnp.stack([qkv_rows[:, head_at[d]] for d in range(group)], axis=0)
    head_rows = jnp.concatenate(
        [
            head_rows,
            jnp.broadcast_to(norm_master.astype(BF).T[None], (group, w_rows, 4)),
            jnp.zeros((group, w_rows, HD - 4), BF),
        ],
        axis=2,
    )
    head_w = lax.all_to_all(head_rows, PLANE, 0, 0, tiled=True).reshape(width, 4 * HD)
    norms = head_w[:, 3 * HD : 3 * HD + 4].astype(F32).T
    main_rows = jnp.concatenate([w_inner.astype(BF), w_outer.astype(BF).T, proj_rows], axis=1)
    main_rows, x_full = lax.optimization_barrier((main_rows, x_full))
    main_w = lax.all_gather(main_rows, PLANE, axis=0, tiled=True)
    proj_at = 2 * hidden_half // width
    late_rows, main_w = lax.optimization_barrier((qkv_rows.reshape(w_rows, -1), main_w))
    qkv_w = lax.all_gather(late_rows, PLANE, axis=0, tiled=True)

    tok = own_micro(slot_token)
    tok_row = tok.reshape(1, total)
    tok_col = tok.reshape(total, 1)
    ends = jnp.cumsum(own_micro(seq_lengths))
    starts = jnp.arange(total // block, dtype=jnp.int32) * block
    first_block = jnp.max(jnp.where(ends[None] <= starts[:, None], ends[None], 0), axis=1) // block
    last_block = jnp.min(jnp.where(ends[None] > starts[:, None], ends[None], total), axis=1) // block
    first_block = first_block.astype(jnp.int32)
    last_block = last_block.astype(jnp.int32)

    h_full, qkv = qkv_of_head(x_full, head_w, norms)
    q, k, v, vt = sort_qkv(tok_row, qkv)
    o, o_low, lse = attend(first_block, q, k, vt, block)
    o_packed = lax.all_to_all(slots_out(tok_col, o_low, group), PLANE, 0, 0, tiled=True)
    mid, h_own, o_own = middle(places, x, o_packed, main_w, proj_at, norms)
    h_other = swap(h_own)
    dy_own, dy_other = own_micro(cotangent), other_micro(cotangent)
    act_other, dpre_other, dh_send, out_send = hidden(h_other, dy_other, main_w, hidden_half)
    dh_got = swap(dh_send.astype(BF))
    act_own, dpre_own, dh_own, out_own = hidden(h_own, dy_own, main_w, hidden_half)
    out_got = swap(out_send.astype(BF))
    layer_own = (mid + out_own + out_got.astype(F32)).astype(BF)
    layer_out = jnp.stack(ordered(layer_own, swap(layer_own)))

    dmid, dmid_low, g_packed, sums_two = middle_back(
        places, group, dh_own, dh_got, dy_own, mid, norms, main_w, proj_at
    )
    main_grad = weight_grads(
        (h_own, h_other), (dpre_own, dpre_other), (dy_own, dy_other), (act_own, act_other), dmid_low, o_own
    )
    main_sum = lax.psum_scatter(main_grad, PLANE, scatter_dimension=0, tiled=True)
    g_packed = lax.all_to_all(g_packed, PLANE, 0, 0, tiled=True)
    g, delta = sort_grad(tok_row, g_packed, o)
    dqkv = attend_back(last_block, q, k, v, g, lse, delta, block)
    dqkv_packed = grads_out(tok_col, dqkv, group)
    dqkv_own = lax.all_to_all(dqkv_packed, PLANE, 0, 0, tiled=True)
    head_grad = head_weight_grad(h_full, dqkv_packed)
    input_low, sums_one = input_back(places, dqkv_own, qkv_w, x, dmid, norms)
    input_grad = jnp.stack(ordered(input_low, swap(input_low))).astype(F32)

    norm_sums = jnp.stack([sums_one[0], sums_two[0], sums_one[1], sums_two[1]])
    norm_top = norm_sums.astype(BF)
    norm_rest = (norm_sums - norm_top.astype(F32)).astype(BF)
    last_grad = jnp.concatenate(
        [head_grad, norm_top.T, norm_rest.T, jnp.zeros((width, HD - 8), BF)], axis=1
    ).reshape(group, w_rows, 4 * HD)
    last_grad = lax.all_to_all(last_grad, PLANE, 0, 0, tiled=True)
    qkv_part = jnp.stack([last_grad[place, :, : 3 * HD] for place in places], axis=1)
    qkv_part = qkv_part.reshape(w_rows, heads, 3, HD).swapaxes(1, 2).reshape(w_rows, 3, 2, half_width)
    norm_part = jnp.sum(last_grad[:, :, 3 * HD : 3 * HD + 8].astype(F32), axis=0)
    norm_part = norm_part[:, :4] + norm_part[:, 4:]
    part_top = norm_part.astype(BF)
    part_rest = (norm_part - part_top.astype(F32)).astype(BF)
    keep, send = ordered(qkv_part[:, :, 0], qkv_part[:, :, 1])
    got = swap(
        jnp.concatenate([send.reshape(w_rows, 3 * half_width), part_top, part_rest], axis=1)
    ).astype(F32)
    qkv_grad = keep.astype(F32) + got[:, : 3 * half_width].reshape(w_rows, 3, half_width)
    norm_got = got[:, 3 * half_width :]
    norm_own = part_top.astype(F32) + part_rest.astype(F32)
    norm_grad = (norm_own + (norm_got[:, :4] + norm_got[:, 4:])).T

    inner_grad = main_sum[:, :hidden_half].astype(F32)
    outer_grad = main_sum[:, hidden_half : 2 * hidden_half].astype(F32).T
    proj_part = main_sum[:, 2 * hidden_half :]
    keep, send = ordered(proj_part[:, :half_width], proj_part[:, half_width:])
    proj_grad = (keep.astype(F32) + swap(send).astype(F32)).T

    qkv_out = adam_step(w_qkv, qkv_first, qkv_second, qkv_grad / MICRO, RATE_MATRIX, DECAY_RATE)
    proj_out = adam_step(w_proj, proj_first, proj_second, proj_grad / MICRO, RATE_PROJ, DECAY_RATE)
    inner_out = adam_step(
        w_inner, inner_first, inner_second, inner_grad / MICRO, RATE_MATRIX, DECAY_RATE
    )
    outer_out = adam_step(
        w_outer, outer_first, outer_second, outer_grad / MICRO, RATE_MATRIX, DECAY_RATE
    )
    norm_grad = norm_grad / MICRO
    norm_out = adam_step(norm_master, norm_first, norm_second, norm_grad, RATE_NORM, 0.0)
    norm_two_grad = jnp.stack([norm_grad[1], norm_grad[3]])
    return (
        layer_out,
        input_grad,
        *qkv_out,
        *proj_out,
        *inner_out,
        *outer_out,
        *norm_out,
        norm_two_grad,
    )


def solution(mesh):
    tok = P(None, PLANE, None)
    qkv = P(PLANE, None, "ha")
    down = P("ha", PLANE)
    inner = P(PLANE, "ha")
    norm = P(None, PLANE)
    in_specs = (
        (tok, tok, P(), P(), qkv, down, inner, down, norm, norm)
        + (qkv, qkv, down, down, inner, inner, down, down, norm, norm)
    )
    out_specs = (
        (tok, tok, qkv, qkv, qkv, down, down, down)
        + (inner, inner, inner, down, down, down, norm, norm, norm, norm)
    )
    return jax.shard_map(shards, mesh=mesh, in_specs=in_specs, out_specs=out_specs, check_vma=False)
```

time: 1010 us -> 419 us (0.41)
  waiting for transfers between devices: 614 us -> 201 us
  matrix products: 143 us -> 0 us
  Pallas kernels: 0 us -> 128 us
  blocking collectives: 125 us -> 0 us
  other arithmetic: 66 us -> 16.6 us
  starting transfers between devices: 1.91 us -> 38.7 us
  local copies, waits for them, and re-layouts: 35.7 us -> 17.6 us
    reduce_scatter x10 -> x1, waiting for transfers between devices: 327 us -> 0.01 us  [shards(): lax.psum_scatter(main_grad, PLANE, scatter_dimension=0, tiled=True)]
    dot_general x36 -> x0, matrix products: 143 us -> none  [the longest x2 37.4 us: backward_block(): jnp.einsum('qhe,khe->hqk', scaled_grad, value_heads, preferred_element_ty...]
    pallas_call x0 -> x14, Pallas kernels: none -> 128 us  [the longest x1 20 us: attend_back(): pl.pallas_call(backward_kernel, grid_spec=pltpu.PrefetchScalarGridSpec(nu...]
    all_gather x13 -> x0, blocking collectives: 125 us -> none  [the longest x1 22.9 us: shards(): lax.all_gather(norm_biases.astype(jnp.bfloat16), ('pb', 'ka'), axis=1, ti...]
    psum x4 -> x0, waiting for transfers between devices: 110 us -> none  [the longest x2 47 us: shards(): lax.psum(jnp.dot(attended_low, proj_full, preferred_element_type=jnp.floa...]
    all_to_all x0 -> x5, waiting for transfers between devices: none -> 62.1 us  [the longest x1 20.6 us: shards(): dqkv_own = lax.all_to_all(dqkv_packed, PLANE, 0, 0, tiled=True)]
    unnamed x21 -> x4, waiting for transfers between devices: 52.3 us -> 0.07 us
    reduce_sum x15 -> x1, other arithmetic: 39.8 us -> 0.13 us  [shards(): norm_part = jnp.sum(last_grad[:, :, 3 * HD:3 * HD + 8].astype(F32), axis=0)]
  transfers between devices with their start and end apart: 20 -> 17, of which waited for: 18 -> 13; matrix products, arithmetic and copies ran while one was open for 11% -> 6% of each run, Pallas kernels for 0% -> 31%
where the time goes in v1:
time: 419 us; the launch traced here: 416 us
  waiting for transfers between devices  201 us (48%)
  Pallas kernels  128 us (31%)
  starting transfers between devices  38.7 us (9%)
  local copies, waits for them, and re-layouts  17.6 us (4%)
  other arithmetic  16.6 us (4%)
  between operations  14.5 us (3%)
    all_gather x1, waiting for transfers between devices, shards(): main_w = lax.all_gather(main_rows, PLANE, axis=0, tiled=True)  59.1 us
    all_gather x1, waiting for transfers between devices, shards(): x_full = lax.all_gather(x, PLANE, axis=0, tiled=True)  48.2 us
    ppermute x8, waiting for transfers between devices, swap(): return lax.ppermute(a, 'ha', [(0, 1), (1, 0)])  31.2 us
    all_to_all x1, waiting for transfers between devices, shards(): dqkv_own = lax.all_to_all(dqkv_packed, PLANE, 0, 0, tiled=True)  20.6 us
    pallas_call x1, Pallas kernels, attend_back(): pl.pallas_call(backward_kernel, grid_spec=pltpu.PrefetchScalarGridSpec(nu...  20 us
    all_to_all x1, waiting for transfers between devices, shards(): lax.all_to_all(head_rows, PLANE, 0, 0, tiled=True).reshape(width, 4 * HD)  15.9 us
    ppermute x8, starting transfers between devices, swap(): return lax.ppermute(a, 'ha', [(0, 1), (1, 0)])  14.5 us
    pallas_call x1, Pallas kernels, grads_out(): pl.pallas_call(functools.partial(grads_out_kernel, min(3072, grads.shape[...  14 us
  transfers between devices with their start and end apart: 17, of which 13 were waited for; matrix products, arithmetic and copies ran while one was open for 6% of the time, Pallas kernels for 31%

profile of v1, /device:TPU:0, one launch (start us, length us, event | category | flops | bytes accessed | tf_op | source)
XLA Modules:
  0.0 415.9 jit_solution(1926030690941195310)
XLA Ops:
  7.3 1.0 copy-done
  11.0 3.0 collective-permute-start
  14.1 3.8 collective-permute-done
  18.7 48.2 %all-gather.9.cloned.1.call-done = bf16[1,3072,768]{2,1,0:T(8,128)(2,1)} async-done(((bf16[1,192,768]{2,1,0:T(8,128)(2,1)}), bf16[1,3072,768]{2,1,0:T(8,128)(2,1)}) %all-gather.9.cloned.1.call-update) | async-done | bytes 4718608 | tf_op jit(solution)/shard_map/all_gather | solution.py:681
  67.9 1.1 reshape_reshape.3
  69.0 59.1 %all-gather.5.cloned.1.call-done.proj_ref.inner_ref.outer_ref = bf16[768,3840]{1,0:T(8,128)(2,1)} async-done(((bf16[48,3840]{1,0:T(8,128)(2,1)}), bf16[768,3840]{1,0:T(8,128)(2,1)}) %all-gather.5.cloned.1.call-update) | async-done | bytes 5898256 | tf_op jit(solution)/shard_map/all_gather | solution.py:710
  128.1 1.7 copy.191.tok_ref
  131.9 3.6 all-to-all-start
  136.7 15.9 %all-to-all-done = bf16[16,48,256]{2,1,0:T(8,128)(2,1)S(1)} async-done(((bf16[16,48,256]{2,1,0:T(8,128)(2,1)}), bf16[16,48,256]{2,1,0:T(8,128)(2,1)S(1)}, u32[]{:S(2)}, u32[]{:S(2)}) %all-to-all-start) | async-done | bytes 393248 | tf_op jit(solution)/shard_map/all_to_all | solution.py:706
  153.5 7.9 %qkv_head.1 = (bf16[3072,768]{1,0:T(8,128)(2,1)}, bf16[3072,256]{1,0:T(8,128)(2,1)}) custom-call(bf16[3072,768]{1,0:T(8,128)(2,1)} %bitcast.132, bf16[768,256]{1,0:T(8,128)(2,1)} %bitcast.134, f32[4,768]{1,0:T(4,128)} %bitcast.144), custom_call_target="tpu_custom_call" | custom-call | tf_op jit(solution)/shard_map/qkv_head/pallas_call | solution.py:83
  161.4 10.3 %sort_qkv.1 = (bf16[3072,64]{1,0:T(8,128)(2,1)}, bf16[3072,64]{1,0:T(8,128)(2,1)}, bf16[3072,64]{1,0:T(8,128)(2,1)}, bf16[64,3072]{1,0:T(8,128)(2,1)}) custom-call(s32[1,3072]{1,0:T(1,128)} %constant_dynamic-slice_fusion.1.tok_ref, bf16[3072,256]{1,0:T(8,128)(2,1)} %get-tuple-element.51.qkv_ref), custom_call_target="tpu_custom_call" | custom-call | tf_op jit(solution)/shard_map/sort_qkv/pallas_call | solution.py:125
  171.7 13.9 %attend_fwd.1 = (f32[64,3072]{1,0:T(8,128)}, bf16[64,3072]{1,0:T(8,128)(2,1)}, f32[1,3072]{1,0:T(1,128)}) custom-call(s32[6]{0:T(128)} %and_select_fusion.1.first_ref, bf16[3072,64]{1,0:T(8,128)(2,1)} %get-tuple-element.52.q_ref, bf16[3072,64]{1,0:T(8,128)(2,1)} %get-tuple-element.53.k_ref, bf16[64,3072]{1,0:T(8,128)(2,1)} %get-tuple-element.54.vt_ref), custom_call_target="tpu_custom_call" | custom-call | tf_op jit(solution)/shard_map/attend_fwd/pallas_call | solution.py:179
  185.6 13.3 %slots_out.1 = bf16[16,96,128]{2,1,0:T(8,128)(2,1)} custom-call(s32[3072,1]{1,0:T(8,128)} %copy.191.tok_ref, bf16[64,3072]{1,0:T(8,128)(2,1)} %get-tuple-element.55.low_ref), custom_call_target="tpu_custom_call" | custom-call | tf_op jit(solution)/shard_map/slots_out/pallas_call | solution.py:215
  198.9 5.0 %all-to-all-start.1 = ((bf16[16,96,128]{2,1,0:T(8,128)(2,1)}), bf16[16,96,128]{2,1,0:T(8,128)(2,1)S(1)}, u32[]{:S(2)}, u32[]{:S(2)}) async-start(bf16[16,96,128]{2,1,0:T(8,128)(2,1)} %slots_out.1), calls=%async_computation.1 | async-start | bytes 786432 | tf_op jit(solution)/shard_map/all_to_all | solution.py:728
  205.0 11.2 %all-to-all-done.1.packed_ref = bf16[16,96,128]{2,1,0:T(8,128)(2,1)S(1)} async-done(((bf16[16,96,128]{2,1,0:T(8,128)(2,1)}), bf16[16,96,128]{2,1,0:T(8,128)(2,1)S(1)}, u32[]{:S(2)}, u32[]{:S(2)}) %all-to-all-start.1) | async-done | bytes 393248 | tf_op jit(solution)/shard_map/all_to_all | solution.py:728
  217.0 3.1 middle.1
  220.1 1.5 collective-permute-start.1
  222.4 6.9 %collective-permute-done.1.h_ref.h1 = bf16[192,768]{1,0:T(8,128)(2,1)S(1)} collective-permute-done((bf16[192,768]{1,0:T(8,128)(2,1)}, bf16[192,768]{1,0:T(8,128)(2,1)S(1)}, u32[]{:S(2)}, u32[]{:S(2)}) %collective-permute-start.1) | collective-permute-done | bytes 294944 | tf_op jit(solution)/shard_map/ppermute | solution.py:669
  230.1 6.6 %hidden.3 = (bf16[192,1536]{1,0:T(8,128)(2,1)}, bf16[192,1536]{1,0:T(8,128)(2,1)}, f32[192,768]{1,0:T(8,128)}, f32[192,768]{1,0:T(8,128)}) custom-call(bf16[192,768]{1,0:T(8,128)(2,1)} %copy-done.8, bf16[192,768]{1,0:T(8,128)(2,1)} %get-tuple-element.180.dy_ref.dy1, bf16[768,3840]{1,0:T(8,128)(2,1)} %all-gather.5.cloned.1.call-done.proj_ref.inner_ref.outer_ref, ...), custom_call_target="tpu_custom_call" | custom-call | tf_op jit(solution)/shard_map/hidden/pallas_call | solution.py:483
  236.7 1.1 convert_element_type.85
  237.8 1.5 collective-permute-start.4
  239.3 6.6 %hidden.2 = (bf16[192,1536]{1,0:T(8,128)(2,1)}, bf16[192,1536]{1,0:T(8,128)(2,1)}, f32[192,768]{1,0:T(8,128)}, f32[192,768]{1,0:T(8,128)}) custom-call(bf16[192,768]{1,0:T(8,128)(2,1)} %get-tuple-element.59.h_ref.h0, bf16[192,768]{1,0:T(8,128)(2,1)} %get-tuple-element.179.dy_ref.dy0, ...), custom_call_target="tpu_custom_call" | custom-call | tf_op jit(solution)/shard_map/hidden/pallas_call | solution.py:483
  246.8 3.5 middle_back.1
  250.3 7.7 %weight_grads.1 = bf16[768,3840]{1,0:T(8,128)(2,1)} custom-call(bf16[192,768]{1,0:T(8,128)(2,1)} %get-tuple-element.59.h_ref.h0, bf16[192,768]{1,0:T(8,128)(2,1)} %copy-done.8, bf16[192,1536]{1,0:T(8,128)(2,1)} %get-tuple-element.76.p0, bf16[192,1536]{1,0:T(8,128)(2,1)} %get-tuple-element.77.p1, bf16[192,768]{1,0:T(8,128)(2,1)} %get-tuple-element.179.dy_ref.dy0, ...), custom_call_target="tpu_custom_call" | custom-call | tf_op jit(solution)/shard_map/weight_grads/pallas_call | solution.py:580
  257.9 3.9 all-to-all-start.2
  262.4 11.7 %all-to-all-done.2.packed_ref = bf16[16,96,128]{2,1,0:T(8,128)(2,1)S(1)} async-done(((bf16[16,96,128]{2,1,0:T(8,128)(2,1)}), bf16[16,96,128]{2,1,0:T(8,128)(2,1)S(1)}, u32[]{:S(2)}, u32[]{:S(2)}) %all-to-all-start.2) | async-done | bytes 393248 | tf_op jit(solution)/shard_map/all_to_all | solution.py:746
  274.8 10.6 %sort_grad.1 = (bf16[3072,64]{1,0:T(8,128)(2,1)}, f32[1,3072]{1,0:T(1,128)}) custom-call(s32[1,3072]{1,0:T(1,128)} %constant_dynamic-slice_fusion.1.tok_ref, bf16[16,96,128]{2,1,0:T(8,128)(2,1)} %copy-done.7, f32[64,3072]{1,0:T(8,128)} %get-tuple-element.66.o_ref), custom_call_target="tpu_custom_call" | custom-call | tf_op jit(solution)/shard_map/sort_grad/pallas_call | solution.py:245
  285.4 20.0 %attend_bwd.1.grad_ref = bf16[3072,192]{1,0:T(8,128)(2,1)} custom-call(s32[6]{0:T(128)} %and_select_fusion.last_ref, bf16[3072,64]{1,0:T(8,128)(2,1)} %get-tuple-element.52.q_ref, bf16[3072,64]{1,0:T(8,128)(2,1)} %get-tuple-element.53.k_ref, bf16[3072,64]{1,0:T(8,128)(2,1)} %get-tuple-element.62.v_ref, bf16[3072,64]{1,0:T(8,128)(2,1)} %get-tuple-element.67.g_ref, ...), custom_call_target="tpu_custom_call" | custom-call | tf_op jit(solution)/shard_map/attend_bwd/pallas_call | solution.py:315
  305.4 14.0 %grads_out.1.packed_ref = bf16[16,288,128]{2,1,0:T(8,128)(2,1)} custom-call(s32[3072,1]{1,0:T(8,128)} %copy.191.tok_ref, bf16[3072,192]{1,0:T(8,128)(2,1)} %attend_bwd.1.grad_ref), custom_call_target="tpu_custom_call" | custom-call | tf_op jit(solution)/shard_map/grads_out/pallas_call | solution.py:360
  319.4 4.1 all-to-all-start.3
  323.5 1.5 collective-permute-start.2
  325.1 7.5 %collective-permute-done.2 = bf16[192,768]{1,0:T(8,128)(2,1)S(1)} collective-permute-done((bf16[192,768]{1,0:T(8,128)(2,1)S(1)}, bf16[192,768]{1,0:T(8,128)(2,1)S(1)}, u32[]{:S(2)}, u32[]{:S(2)}) %collective-permute-start.2) | collective-permute-done | bytes 294944 | tf_op jit(solution)/shard_map/ppermute | solution.py:669
  332.6 1.5 collective-permute-start.3
  334.1 5.4 %head_weight.1 = bf16[768,192]{1,0:T(8,128)(2,1)} custom-call(bf16[3072,768]{1,0:T(8,128)(2,1)} %get-tuple-element.73.h_ref, bf16[16,288,128]{2,1,0:T(8,128)(2,1)} %grads_out.1.packed_ref), custom_call_target="tpu_custom_call" | custom-call | tf_op jit(solution)/shard_map/head_weight/pallas_call | solution.py:401
  339.6 20.6 %all-to-all-done.3.packed_ref = bf16[16,288,128]{2,1,0:T(8,128)(2,1)S(1)} async-done(((bf16[16,288,128]{2,1,0:T(8,128)(2,1)}), bf16[16,288,128]{2,1,0:T(8,128)(2,1)S(1)}, u32[]{:S(2)}, u32[]{:S(2)}) %all-to-all-start.3) | async-done | bytes 1179680 | tf_op jit(solution)/shard_map/all_to_all | solution.py:750
  360.2 1.0 copy-done.2
  361.2 4.9 %input_back.1 = (bf16[192,768]{1,0:T(8,128)(2,1)}, f32[2,768]{1,0:T(2,128)}) custom-call(bf16[16,288,128]{2,1,0:T(8,128)(2,1)} %copy-done.2, bf16[768,2304]{1,0:T(8,128)(2,1)} %all-gather.7.cloned.1.call-done.w_ref, bf16[192,768]{1,0:T(8,128)(2,1)} %fusion.30.x_ref, f32[192,768]{1,0:T(8,128)} %get-tuple-element.71.dmid_ref, f32[4,768]{1,0:T(4,128)} %bitcast.147), custom_call_target="tpu_custom_call" | custom-call | tf_op jit(solution)/shard_map/input_back/pallas_call | solution.py:609
  367.3 1.0 maximum_maximum_fusion.1
  368.2 7.3 %all-to-all-start.4 = ((bf16[16,48,256]{2,1,0:T(8,128)(2,1)}), bf16[16,48,256]{2,1,0:T(8,128)(2,1)S(1)}, u32[]{:S(2)}, u32[]{:S(2)}) async-start(bf16[16,48,256]{2,1,0:T(8,128)(2,1)} %bitcast.32), calls=%async_computation.4 | async-start | bytes 786432 | tf_op jit(solution)/shard_map/all_to_all | solution.py:761
  375.5 1.8 collective-permute-start.5
  378.3 6.7 %collective-permute-done.5 = bf16[192,768]{1,0:T(8,128)(2,1)S(1)} collective-permute-done((bf16[192,768]{1,0:T(8,128)(2,1)S(1)}, bf16[192,768]{1,0:T(8,128)(2,1)S(1)}, u32[]{:S(2)}, u32[]{:S(2)}) %collective-permute-start.5) | collective-permute-done | bytes 294944 | tf_op jit(solution)/shard_map/ppermute | solution.py:669
  385.0 2.7 all-to-all-done.4
  391.1 1.8 collective-permute-start.6
  392.9 1.1 maximum_convert_fusion
  394.0 6.2 %collective-permute-done.6 = bf16[48,1160]{0,1:T(8,128)(2,1)S(1)} collective-permute-done((bf16[48,1160]{0,1:T(8,128)(2,1)S(1)}, bf16[48,1160]{0,1:T(8,128)(2,1)S(1)}, u32[]{:S(2)}, u32[]{:S(2)}) %collective-permute-start.6) | collective-permute-done | bytes 111392 | tf_op jit(solution)/shard_map/ppermute | solution.py:669
  403.7 1.8 collective-permute-start.7
  405.5 2.0 multiply_subtract_fusion.1
  407.5 1.1 multiply_subtract_fusion
  (191 shorter events, 23.8 us)
Async XLA Ops:
  7.2 1.1 copy-start
  7.2 6.8 %copy-start.10 = (f32[1536,48]{0,1:T(8,128)S(1)}, f32[1536,48]{0,1:T(8,128)}, u32[]{:S(2)}) copy-start(f32[1536,48]{0,1:T(8,128)} %param.27) | copy-start | bytes 884740
  7.2 6.8 %copy-start.9 = (f32[48,1536]{1,0:T(8,128)S(1)}, f32[48,1536]{1,0:T(8,128)}, u32[]{:S(2)}) copy-start(f32[48,1536]{1,0:T(8,128)} %param.26) | copy-start | bytes 884740
  7.2 59.7 %all-gather.9.cloned.1.call-start = ((), (), s32[]{:S(2)}) async-start(), calls=%async_computation.9 | async-start | bytes 5013504 | tf_op jit(solution)/shard_map/all_gather | solution.py:681
  9.0 119.0 %all-gather.5.cloned.1.call-start = ((), (), s32[]{:S(2)}) async-start(), calls=%async_computation.6 | async-start | bytes 6266880 | tf_op jit(solution)/shard_map/all_gather | solution.py:710
  11.0 6.9 %collective-permute-start = (bf16[48,1536]{1,0:T(8,128)(2,1)S(1)}, bf16[48,1536]{1,0:T(8,128)(2,1)S(1)}, u32[]{:S(2)}, u32[]{:S(2)}) collective-permute-start(bf16[48,1536]{1,0:T(8,128)(2,1)S(1)} %pad_maximum_fusion.3), channel_id=1, source_target_pairs={{0,1},{1,0},{2,3},{3,2},{4,5},{5,4},{6,7},{7,6},{8,9},{9,8},{10,11... | collective-permute-start | bytes 442376 | tf_op jit(solution)/shard_map/ppermute | solution.py:669
  66.9 293.3 %all-gather.7.cloned.1.call-start = ((), (), s32[]{:S(2)}) async-start(), calls=%async_computation.7 | async-start | bytes 3760128 | tf_op jit(solution)/shard_map/all_gather | solution.py:713
  67.4 60.7 %copy-start.27 = (s32[2,3072]{1,0:T(2,128)S(1)}, s32[2,3072]{1,0:T(2,128)}, u32[]{:S(2)}) copy-start(s32[2,3072]{1,0:T(2,128)} %param.23) | copy-start | bytes 73732
  67.9 61.9 %copy-start.33 = (s32[2,2]{1,0:T(2,128)S(1)}, s32[2,2]{1,0:T(2,128)}, u32[]{:S(2)}) copy-start(s32[2,2]{1,0:T(2,128)} %param.22) | copy-start | bytes 52
  67.9 62.1 %copy-start.29 = (f32[2,48]{1,0:T(2,128)S(1)}, f32[2,48]{1,0:T(2,128)}, u32[]{:S(2)}) copy-start(f32[2,48]{1,0:T(2,128)} %param.29) | copy-start | bytes 1156
  67.9 62.1 %copy-start.30 = (f32[2,48]{1,0:T(2,128)S(1)}, f32[2,48]{1,0:T(2,128)}, u32[]{:S(2)}) copy-start(f32[2,48]{1,0:T(2,128)} %param.28) | copy-start | bytes 1156
  131.9 20.7 %all-to-all-start = ((bf16[16,48,256]{2,1,0:T(8,128)(2,1)}), bf16[16,48,256]{2,1,0:T(8,128)(2,1)S(1)}, u32[]{:S(2)}, u32[]{:S(2)}) async-start(bf16[16,48,256]{2,1,0:T(8,128)(2,1)} %maximum_maximum_fusion), calls=%async_computation | async-start | bytes 786432 | tf_op jit(solution)/shard_map/all_to_all | solution.py:706
  152.6 0.9 copy-start.3
  198.9 17.3 %all-to-all-start.1 = ((bf16[16,96,128]{2,1,0:T(8,128)(2,1)}), bf16[16,96,128]{2,1,0:T(8,128)(2,1)S(1)}, u32[]{:S(2)}, u32[]{:S(2)}) async-start(bf16[16,96,128]{2,1,0:T(8,128)(2,1)} %slots_out.1), calls=%async_computation.1 | async-start | bytes 786432 | tf_op jit(solution)/shard_map/all_to_all | solution.py:728
  204.0 198.8 %reduce-scatter.2.cloned.1.call-start = ((), (), s32[]{:S(2)}) async-start(), calls=%async_computation.8 | async-start | bytes 6266880 | tf_op jit(solution)/shard_map/reduce_scatter | solution.py:745
  205.0 16.6 %copy-start.14 = (bf16[2,192,768]{2,1,0:T(8,128)(2,1)S(1)}, bf16[2,192,768]{2,1,0:T(8,128)(2,1)}, u32[]{:S(2)}) copy-start(bf16[2,192,768]{2,1,0:T(8,128)(2,1)} %param.21) | copy-start | bytes 1769476
  216.2 0.8 copy-start.6
  220.1 9.2 %collective-permute-start.1 = (bf16[192,768]{1,0:T(8,128)(2,1)}, bf16[192,768]{1,0:T(8,128)(2,1)S(1)}, u32[]{:S(2)}, u32[]{:S(2)}) collective-permute-start(bf16[192,768]{1,0:T(8,128)(2,1)} %get-tuple-element.59.h_ref.h0), channel_id=1, source_target_pairs={{0,1},{1,0},{2,3},{3,2},{4,5},{5,4},{6,7},{7,6},{8,9},{9,8},{10,11... | collective-permute-start | bytes 884744 | tf_op jit(solution)/shard_map/ppermute | solution.py:669
  237.8 8.3 %collective-permute-start.4 = (bf16[192,768]{1,0:T(8,128)(2,1)S(1)}, bf16[192,768]{1,0:T(8,128)(2,1)S(1)}, u32[]{:S(2)}, u32[]{:S(2)}) collective-permute-start(bf16[192,768]{1,0:T(8,128)(2,1)S(1)} %convert_element_type.85), channel_id=1, source_target_pairs={{0,1},{1,0},{2,3},{3,2},{4,5},{5,4},{6,7},{7,6},{8,9},{9,8},{10,11... | collective-permute-start | bytes 884744 | tf_op jit(solution)/shard_map/ppermute | solution.py:669
  257.9 16.1 %all-to-all-start.2 = ((bf16[16,96,128]{2,1,0:T(8,128)(2,1)}), bf16[16,96,128]{2,1,0:T(8,128)(2,1)S(1)}, u32[]{:S(2)}, u32[]{:S(2)}) async-start(bf16[16,96,128]{2,1,0:T(8,128)(2,1)} %get-tuple-element.65), calls=%async_computation.2 | async-start | bytes 786432 | tf_op jit(solution)/shard_map/all_to_all | solution.py:746
  319.4 4.1 copy-start.13
  319.4 13.2 %copy-start.4 = (f32[192,768]{1,0:T(8,128)S(1)}, f32[192,768]{1,0:T(8,128)}, u32[]{:S(2)}) copy-start(f32[192,768]{1,0:T(8,128)} %get-tuple-element.58.mid_ref) | copy-start | bytes 1769476
  319.4 13.2 %copy-start.12 = (f32[192,768]{1,0:T(8,128)S(1)}, f32[192,768]{1,0:T(8,128)}, u32[]{:S(2)}) copy-start(f32[192,768]{1,0:T(8,128)} %get-tuple-element.60) | copy-start | bytes 1769476
  319.4 40.8 %all-to-all-start.3 = ((bf16[16,288,128]{2,1,0:T(8,128)(2,1)}), bf16[16,288,128]{2,1,0:T(8,128)(2,1)S(1)}, u32[]{:S(2)}, u32[]{:S(2)}) async-start(bf16[16,288,128]{2,1,0:T(8,128)(2,1)} %grads_out.1.packed_ref), calls=%async_computation.3 | async-start | bytes 2359296 | tf_op jit(solution)/shard_map/all_to_all | solution.py:750
  323.4 10.7 %copy-start.28 = (f32[2,768]{1,0:T(2,128)S(1)}, f32[2,768]{1,0:T(2,128)}, u32[]{:S(2)}) copy-start(f32[2,768]{1,0:T(2,128)} %get-tuple-element.75) | copy-start | bytes 18436
  323.5 9.0 %collective-permute-start.2 = (bf16[192,768]{1,0:T(8,128)(2,1)S(1)}, bf16[192,768]{1,0:T(8,128)(2,1)S(1)}, u32[]{:S(2)}, u32[]{:S(2)}) collective-permute-start(bf16[192,768]{1,0:T(8,128)(2,1)S(1)} %convert_element_type.82), channel_id=1, source_target_pairs={{0,1},{1,0},{2,3},{3,2},{4,5},{5,4},{6,7},{7,6},{8,9},{9,8},{10,11... | collective-permute-start | bytes 884744 | tf_op jit(solution)/shard_map/ppermute | solution.py:669
  332.6 44.7 %collective-permute-start.3 = (bf16[192,768]{1,0:T(8,128)(2,1)S(1)}, bf16[192,768]{1,0:T(8,128)(2,1)S(1)}, u32[]{:S(2)}, u32[]{:S(2)}) collective-permute-start(bf16[192,768]{1,0:T(8,128)(2,1)S(1)} %add_convert_fusion), channel_id=1, source_target_pairs={{0,1},{1,0},{2,3},{3,2},{4,5},{5,4},{6,7},{7,6},{8,9},{9,8},{10,11... | collective-permute-start | bytes 884744 | tf_op jit(solution)/shard_map/ppermute | solution.py:669
  360.2 1.0 copy-start.2
  361.2 6.1 %copy-start.5 = (bf16[768,192]{1,0:T(8,128)(2,1)S(1)}, bf16[768,192]{1,0:T(8,128)(2,1)}, u32[]{:S(2)}) copy-start(bf16[768,192]{1,0:T(8,128)(2,1)} %head_weight.1) | copy-start | bytes 884740
  366.0 9.5 %copy-start.18 = (bf16[192,768]{1,0:T(8,128)(2,1)S(1)}, bf16[192,768]{1,0:T(8,128)(2,1)}, u32[]{:S(2)}) copy-start(bf16[192,768]{1,0:T(8,128)(2,1)} %get-tuple-element.72) | copy-start | bytes 884740
  368.2 19.5 %all-to-all-start.4 = ((bf16[16,48,256]{2,1,0:T(8,128)(2,1)}), bf16[16,48,256]{2,1,0:T(8,128)(2,1)S(1)}, u32[]{:S(2)}, u32[]{:S(2)}) async-start(bf16[16,48,256]{2,1,0:T(8,128)(2,1)} %bitcast.32), calls=%async_computation.4 | async-start | bytes 786432 | tf_op jit(solution)/shard_map/all_to_all | solution.py:761
  375.5 9.4 %collective-permute-start.5 = (bf16[192,768]{1,0:T(8,128)(2,1)S(1)}, bf16[192,768]{1,0:T(8,128)(2,1)S(1)}, u32[]{:S(2)}, u32[]{:S(2)}) collective-permute-start(bf16[192,768]{1,0:T(8,128)(2,1)S(1)} %copy-done.18), channel_id=1, source_target_pairs={{0,1},{1,0},{2,3},{3,2},{4,5},{5,4},{6,7},{7,6},{8,9},{9,8},{10,11... | collective-permute-start | bytes 884744 | tf_op jit(solution)/shard_map/ppermute | solution.py:669
  391.1 9.2 %collective-permute-start.6 = (bf16[48,1160]{0,1:T(8,128)(2,1)S(1)}, bf16[48,1160]{0,1:T(8,128)(2,1)S(1)}, u32[]{:S(2)}, u32[]{:S(2)}) collective-permute-start(bf16[48,1160]{0,1:T(8,128)(2,1)S(1)} %concatenate.28), channel_id=1, source_target_pairs={{0,1},{1,0},{2,3},{3,2},{4,5},{5,4},{6,7},{7,6},{8,9},{9,8},{10,11... | collective-permute-start | bytes 334088 | tf_op jit(solution)/shard_map/ppermute | solution.py:669
  394.0 7.2 %copy-start.31 = (f32[4,48]{1,0:T(4,128)S(1)}, f32[4,48]{1,0:T(4,128)}, u32[]{:S(2)}) copy-start(f32[4,48]{1,0:T(4,128)} %param.39) | copy-start | bytes 2308
  394.0 7.2 %copy-start.32 = (f32[4,48]{1,0:T(4,128)S(1)}, f32[4,48]{1,0:T(4,128)}, u32[]{:S(2)}) copy-start(f32[4,48]{1,0:T(4,128)} %param.38) | copy-start | bytes 2308
  394.0 7.8 %copy-start.11 = (f32[48,3,384]{2,0,1:T(8,128)S(1)}, f32[48,3,384]{2,0,1:T(8,128)}, u32[]{:S(2)}) copy-start(f32[48,3,384]{2,0,1:T(8,128)} %param.24) | copy-start | bytes 663556
  394.0 7.8 %copy-start.23 = (f32[48,3,384]{2,0,1:T(8,128)S(1)}, f32[48,3,384]{2,0,1:T(8,128)}, u32[]{:S(2)}) copy-start(f32[48,3,384]{2,0,1:T(8,128)} %param.31) | copy-start | bytes 663556
  394.0 7.8 %copy-start.24 = (f32[48,3,384]{2,0,1:T(8,128)S(1)}, f32[48,3,384]{2,0,1:T(8,128)}, u32[]{:S(2)}) copy-start(f32[48,3,384]{2,0,1:T(8,128)} %param.30) | copy-start | bytes 663556
  400.3 5.2 %copy-start.19 = (f32[48,1536]{1,0:T(8,128)S(1)}, f32[48,1536]{1,0:T(8,128)}, u32[]{:S(2)}) copy-start(f32[48,1536]{1,0:T(8,128)} %param.35) | copy-start | bytes 884740
  400.3 5.2 %copy-start.20 = (f32[48,1536]{1,0:T(8,128)S(1)}, f32[48,1536]{1,0:T(8,128)}, u32[]{:S(2)}) copy-start(f32[48,1536]{1,0:T(8,128)} %param.34) | copy-start | bytes 884740
  401.8 5.7 %copy-start.21 = (f32[1536,48]{0,1:T(8,128)S(1)}, f32[1536,48]{0,1:T(8,128)}, u32[]{:S(2)}) copy-start(f32[1536,48]{0,1:T(8,128)} %param.37) | copy-start | bytes 884740
  401.8 5.7 %copy-start.22 = (f32[1536,48]{0,1:T(8,128)S(1)}, f32[1536,48]{0,1:T(8,128)}, u32[]{:S(2)}) copy-start(f32[1536,48]{0,1:T(8,128)} %param.36) | copy-start | bytes 884740
  402.8 4.7 %copy-start.15 = (bf16[48,3840]{1,0:T(8,128)(2,1)S(1)}, bf16[48,3840]{1,0:T(8,128)(2,1)}, u32[]{:S(2)}) copy-start(bf16[48,3840]{1,0:T(8,128)(2,1)} %reduce-scatter.2.cloned.1.call-done) | copy-start | bytes 1105924
  403.6 4.9 %copy-start.17 = (f32[384,48]{0,1:T(8,128)S(1)}, f32[384,48]{0,1:T(8,128)}, u32[]{:S(2)}) copy-start(f32[384,48]{0,1:T(8,128)} %param.25) | copy-start | bytes 221188
  403.6 4.9 %copy-start.25 = (f32[384,48]{0,1:T(8,128)S(1)}, f32[384,48]{0,1:T(8,128)}, u32[]{:S(2)}) copy-start(f32[384,48]{0,1:T(8,128)} %param.33) | copy-start | bytes 221188
  403.7 4.9 %copy-start.26 = (f32[384,48]{0,1:T(8,128)S(1)}, f32[384,48]{0,1:T(8,128)}, u32[]{:S(2)}) copy-start(f32[384,48]{0,1:T(8,128)} %param.32) | copy-start | bytes 221188
  403.7 4.9 %collective-permute-start.7 = (bf16[48,384]{1,0:T(8,128)(2,1)S(1)}, bf16[48,384]{1,0:T(8,128)(2,1)S(1)}, u32[]{:S(2)}, u32[]{:S(2)}) collective-permute-start(bf16[48,384]{1,0:T(8,128)(2,1)S(1)} %broadcast_select_fusion.4), channel_id=1, source_target_pairs={{0,1},{1,0},{2,3},{3,2},{4,5},{5,4},{6,7},{7,6},{8,9},{9,8},{10,11... | collective-permute-start | bytes 110600 | tf_op jit(solution)/shard_map/ppermute | solution.py:669
  405.5 3.8 copy-start.1
  (3 other events, 2.2 us)
Sparse Core Ops, SparseCore 0:
  10.9 55.9 all-gather.8
  69.7 58.2 all-gather.4
  130.9 49.5 all-gather.6
  258.1 100.2 reduce-scatter.1

commit v2 on v1

v2 whole, which is shorter than its diff:
```python
import functools

import jax
import jax.numpy as jnp
from jax import lax
from jax.experimental import pallas as pl
from jax.experimental.pallas import tpu as pltpu
from jax.sharding import PartitionSpec as P

HD = 64
MICRO = 2
STEP = 8
NORM_EPS = 1e-05
BETA_ONE = 0.9
BETA_TWO = 0.95
ADAM_EPS = 1e-08
DECAY_RATE = 0.1
RATE_MATRIX = 0.02
RATE_PROJ = 0.6
RATE_NORM = 0.1
BF = jnp.bfloat16
F32 = jnp.float32
PLANE = ("pb", "ka")
VMEM_LIMIT = 60 * 1024 * 1024
SCORE_BLOCK = 512
SORT_BLOCK = 1024
NT = (((1,), (1,)), ((), ()))
NN = (((1,), (0,)), ((), ()))
TN = (((0,), (0,)), ((), ()))


def dot(a, b, dims=NN):
    return lax.dot_general(a, b, dims, preferred_element_type=F32)


def params(steps=1):
    return pltpu.CompilerParams(
        dimension_semantics=("arbitrary",) * steps, vmem_limit_bytes=VMEM_LIMIT
    )


def cost(us):
    return pl.CostEstimate(flops=int(us * 2e8), bytes_accessed=int(us * 1e6), transcendentals=0)


def tie(*arrays):
    return lax.optimization_barrier(arrays)


def whole(shape):
    return pl.BlockSpec(shape, lambda *_: (0,) * len(shape))


def shape_of(shape, dtype):
    return jax.ShapeDtypeStruct(shape, dtype)


def head_places(group, heads):
    return tuple(h * group // heads for h in range(heads))


def normalize(x):
    center = x - jnp.mean(x, axis=-1, keepdims=True)
    spread = jnp.mean(center * center, axis=-1, keepdims=True)
    scale = lax.rsqrt(spread + NORM_EPS)
    return center * scale, scale


def normalize_back(grad, unit, scale):
    return scale * (
        grad
        - jnp.mean(grad, axis=-1, keepdims=True)
        - unit * jnp.mean(grad * unit, axis=-1, keepdims=True)
    )


def matching(row_ids, index):
    low = jnp.where(
        lax.shift_right_logical(row_ids, 8) == index, lax.bitwise_and(row_ids, 255), 256
    )
    line = lax.broadcasted_iota(jnp.int32, (256, 1), 0)
    return jnp.where(
        low.astype(F32).astype(BF) == line.astype(F32).astype(BF),
        jnp.ones((), BF),
        jnp.zeros((), BF),
    )


def rearranged(row_ids, source_ref):
    count = source_ref.shape[1] // 256
    span = min(count, 12)

    def some(start, total):
        for part in range(span):
            index = start * span + part
            at = index * 256 if isinstance(index, int) else pl.multiple_of(index * 256, 256)
            piece = dot(source_ref[:, pl.ds(at, 256)], matching(row_ids, index))
            total = piece if total is None else total + piece
        return total

    if count == span:
        return some(0, None)
    empty = jnp.zeros((source_ref.shape[0], row_ids.shape[1]), F32)
    return lax.fori_loop(0, count // span, some, empty)


def place_kernel(tok_ref, out_ref):
    index = pl.program_id(0)
    total = tok_ref.shape[1]
    chunk = min(3072, total)
    hits = None
    line = lax.broadcasted_iota(jnp.int32, (8, chunk), 0)
    for part in range(total // chunk):
        slot = part * chunk + lax.broadcasted_iota(jnp.int32, (8, chunk), 1)
        ids = jnp.where(line == 0, lax.shift_right_logical(slot, 8), lax.bitwise_and(slot, 255))
        found = matching(tok_ref[:, part * chunk : (part + 1) * chunk], index)
        piece = dot(ids.astype(F32).astype(BF), found, NT)
        hits = piece if hits is None else hits + piece
    out_ref[...] = (hits[0:1] * 256.0 + hits[1:2]).astype(jnp.int32)


def slots_of_tokens(tok_row):
    total = tok_row.shape[1]
    return pl.pallas_call(
        place_kernel,
        grid=(total // 256,),
        in_specs=[whole(tok_row.shape)],
        out_specs=pl.BlockSpec((1, 256), lambda i: (0, i)),
        out_shape=shape_of((1, total), jnp.int32),
        compiler_params=params(),
        cost_estimate=cost(8),
        name="slots_of_tokens",
    )(tok_row)


def qkv_kernel(x_ref, w_ref, norm_ref, unit_ref, qkv_ref):
    unit, _ = normalize(x_ref[...].astype(F32))
    h = (unit * norm_ref[0:1, :] + norm_ref[2:3, :]).astype(BF)
    unit_ref[...] = unit.astype(BF)
    qkv_ref[...] = dot(w_ref[...], h, NT).astype(BF)


def qkv_piece_kernel(counts, at_ref, *refs):
    sources = refs[: 4 * len(counts)]
    w_ref, norm_ref = refs[4 * len(counts) :][:2]
    unit_ref, qkv_ref, x_ref = refs[-3:]
    rows = x_ref.shape[0] // 2
    even = at_ref[3] == 0
    slot = 0
    for group, count in enumerate(counts):
        for place in range(count):
            for side in range(2):

                @pl.when((pl.program_id(0) == slot) & (pl.program_id(1) == side))
                def _():
                    own = sources[4 * group + side][place]
                    other = sources[4 * group + 2 + side][place]
                    x_ref[:rows, :] = jnp.where(even, own, other)
                    x_ref[rows:, :] = jnp.where(even, other, own)

            slot += 1
    unit, _ = normalize(x_ref[...].astype(F32))
    h = (unit * norm_ref[0:1, :] + norm_ref[2:3, :]).astype(BF)
    unit_ref[...] = unit.astype(BF)
    qkv_ref[...] = dot(w_ref[...], h, NT).astype(BF)


def qkv_of_piece(at, groups, head_w, norms, total, buffers):
    counts = tuple(group[0].shape[0] for group in groups)
    pieces = [a for group in groups for a in group]
    _, rows, width = pieces[0].shape
    kept = [pl.BlockSpec(memory_space=pl.ANY)] * len(buffers)
    first = 1 + len(pieces) + 2

    def place(i, j, at):
        return (at[0] ^ (at[1] + i)) * 2 + (at[2] ^ j)

    return pl.pallas_call(
        functools.partial(qkv_piece_kernel, counts),
        grid_spec=pltpu.PrefetchScalarGridSpec(
            num_scalar_prefetch=1,
            grid=(sum(counts), 2),
            in_specs=[whole(a.shape) for a in (*pieces, head_w, norms)] + kept,
            out_specs=[
                pl.BlockSpec((2 * rows, width), lambda i, j, at: (place(i, j, at), 0)),
                pl.BlockSpec((head_w.shape[0], 2 * rows), lambda i, j, at: (0, place(i, j, at))),
            ],
            scratch_shapes=[pltpu.VMEM((2 * rows, width), BF)],
        ),
        out_shape=[shape_of((total, width), BF), shape_of((head_w.shape[0], total), BF)],
        input_output_aliases={first: 0, first + 1: 1} if buffers else {},
        compiler_params=params(2),
        cost_estimate=cost(3 * sum(counts)),
        name="qkv_piece",
    )(at, *pieces, head_w, norms, *buffers)


def qkv_of_head(x_full, head_w, norms):
    rows, width = x_full.shape
    block = min(512, rows)
    return pl.pallas_call(
        qkv_kernel,
        grid=(rows // block,),
        in_specs=[
            pl.BlockSpec((block, width), lambda i: (i, 0)),
            whole(head_w.shape),
            whole(norms.shape),
        ],
        out_specs=[
            pl.BlockSpec((block, width), lambda i: (i, 0)),
            pl.BlockSpec((head_w.shape[0], block), lambda i: (0, i)),
        ],
        out_shape=[shape_of((rows, width), BF), shape_of((head_w.shape[0], rows), BF)],
        compiler_params=params(),
        cost_estimate=cost(8),
        name="qkv_head",
    )(x_full, head_w, norms)


def sort_kernel(slot_ref, qkv_ref, q_ref, qt_ref, k_ref, v_ref, vt_ref):
    found = rearranged(slot_ref[...], qkv_ref)
    query = found[:HD] * float(HD) ** -0.5
    value = found[2 * HD :]
    qt_ref[...] = query.astype(BF)
    q_ref[...] = query.T.astype(BF)
    k_ref[...] = found[HD : 2 * HD].T.astype(BF)
    v_ref[...] = value.T.astype(BF)
    vt_ref[...] = value.astype(BF)


def sort_qkv(slot_row, qkv):
    rows = qkv.shape[1]
    block = min(SORT_BLOCK, rows)
    narrow = pl.BlockSpec((block, HD), lambda i: (i, 0))
    wide = pl.BlockSpec((HD, block), lambda i: (0, i))
    return pl.pallas_call(
        sort_kernel,
        grid=(rows // block,),
        in_specs=[pl.BlockSpec((1, block), lambda i: (0, i)), whole(qkv.shape)],
        out_specs=[narrow, wide, narrow, narrow, wide],
        out_shape=[shape_of((HD, rows) if spec is wide else (rows, HD), BF) for spec in (narrow, wide, narrow, narrow, wide)],
        compiler_params=params(),
        cost_estimate=cost(7),
        name="sort_qkv",
    )(slot_row, qkv)


def causal(block):
    return lax.broadcasted_iota(jnp.int32, (block, block), 0) <= lax.broadcasted_iota(
        jnp.int32, (block, block), 1
    )


def forward_kernel(first_ref, qt_ref, k_ref, vt_ref, o_ref, low_ref, lse_ref):
    block = qt_ref.shape[1]
    index = pl.program_id(0)
    query = qt_ref[...]

    def step(key_block, state, diagonal):
        top, total, acc = state
        at = pl.multiple_of(key_block * block, block)
        scores = dot(k_ref[pl.ds(at, block), :], query)
        square = scores * scores + 1.0
        inverse = lax.rsqrt(square)
        radius = square * inverse
        if diagonal:
            radius = jnp.where(causal(block), radius, -1e30)
        new_top = jnp.maximum(top, jnp.max(radius, axis=0, keepdims=True))
        weights = jnp.exp(radius - new_top)
        shrink = jnp.exp(top - new_top)
        signed = (scores * inverse * weights).astype(BF)
        acc = acc * shrink + dot(vt_ref[:, pl.ds(at, block)], signed)
        total = total * shrink + jnp.sum(weights, axis=0, keepdims=True)
        return (new_top, total, acc)

    state = (
        jnp.zeros((1, block), F32),
        jnp.zeros((1, block), F32),
        jnp.zeros((HD, block), F32),
    )
    state = lax.fori_loop(first_ref[index], index, lambda j, s: step(j, s, False), state)
    top, total, acc = step(index, state, True)
    out = acc * (1.0 / total)
    o_ref[...] = out
    low_ref[...] = out.astype(BF)
    lse_ref[...] = top + jnp.log(total)


def attend(first_block, qt, k, vt, block):
    rows = k.shape[0]
    return pl.pallas_call(
        forward_kernel,
        grid_spec=pltpu.PrefetchScalarGridSpec(
            num_scalar_prefetch=1,
            grid=(rows // block,),
            in_specs=[
                pl.BlockSpec((HD, block), lambda i, *_: (0, i)),
                whole(k.shape),
                whole(vt.shape),
            ],
            out_specs=[
                pl.BlockSpec((HD, block), lambda i, *_: (0, i)),
                pl.BlockSpec((HD, block), lambda i, *_: (0, i)),
                pl.BlockSpec((1, block), lambda i, *_: (0, i)),
            ],
        ),
        out_shape=[shape_of((HD, rows), F32), shape_of((HD, rows), BF), shape_of((1, rows), F32)],
        compiler_params=params(),
        cost_estimate=cost(13),
        name="attend_fwd",
    )(first_block, qt, k, vt)


def slots_out_kernel(rows, tok_ref, low_ref, out_ref):
    half = rows // 2
    found = rearranged(tok_ref[...], low_ref).T.astype(BF)
    for d in range(out_ref.shape[0]):
        at = d * rows
        out_ref[d] = jnp.concatenate([found[at : at + half], found[at + half : at + rows]], axis=1)


def slots_out(tok_row, low, group):
    total = tok_row.shape[1]
    rows = total // group
    count = owners_per_step(group, rows)
    return pl.pallas_call(
        functools.partial(slots_out_kernel, rows),
        grid=(group // count,),
        in_specs=[pl.BlockSpec((1, count * rows), lambda i: (0, i)), whole(low.shape)],
        out_specs=pl.BlockSpec((count, rows // 2, 2 * HD), lambda i: (i, 0, 0)),
        out_shape=shape_of((group, rows // 2, 2 * HD), BF),
        compiler_params=params(),
        cost_estimate=cost(6),
        name="slots_out",
    )(tok_row, low)


def owners_per_step(group, rows):
    for count in (4, 2, 1):
        if group % count == 0 and count * rows % 128 == 0:
            return count
    return group


def sort_grad_kernel(slot_ref, packed_ref, o_ref, g_ref, gt_ref, delta_ref, slots_ref, flat_ref):
    group, half, _ = packed_ref.shape

    @pl.when(pl.program_id(0) == 0)
    def _():
        for d in range(group):
            piece = packed_ref[d]
            flat_ref[2 * d * half : (2 * d + 1) * half, :] = piece[:, :HD]
            flat_ref[(2 * d + 1) * half : (2 * d + 2) * half, :] = piece[:, HD:]
        for part in range(flat_ref.shape[0] // 256):
            cut = slice(part * 256, (part + 1) * 256)
            slots_ref[:, cut] = flat_ref[cut, :].astype(F32).T.astype(BF)

    found = rearranged(slot_ref[...], slots_ref)
    gt_ref[...] = found.astype(BF)
    g_ref[...] = found.T.astype(BF)
    delta_ref[...] = jnp.sum(found * o_ref[...], axis=0, keepdims=True)


def sort_grad(slot_row, packed, o):
    rows = o.shape[1]
    block = min(SORT_BLOCK, rows)
    wide = pl.BlockSpec((HD, block), lambda i: (0, i))
    line = pl.BlockSpec((1, block), lambda i: (0, i))
    return pl.pallas_call(
        sort_grad_kernel,
        grid=(rows // block,),
        in_specs=[line, whole(packed.shape), wide],
        out_specs=[pl.BlockSpec((block, HD), lambda i: (i, 0)), wide, line],
        out_shape=[shape_of((rows, HD), BF), shape_of((HD, rows), BF), shape_of((1, rows), F32)],
        scratch_shapes=[pltpu.VMEM((HD, rows), BF), pltpu.VMEM((rows, HD), BF)],
        compiler_params=params(),
        cost_estimate=cost(6),
        name="sort_grad",
    )(slot_row, packed, o)


def backward_kernel(
    last_ref, q_ref, qt_ref, k_ref, v_ref, g_ref, gt_ref, lse_ref, delta_ref, out_ref, dq_ref, dk_ref, dv_ref
):
    block = k_ref.shape[0]
    index = pl.program_id(0)

    @pl.when(index == 0)
    def _():
        dq_ref[...] = jnp.zeros_like(dq_ref)

    key = k_ref[...]
    key_t = key.astype(F32).T.astype(BF)
    value = v_ref[...]
    dk_ref[...] = jnp.zeros_like(dk_ref)
    dv_ref[...] = jnp.zeros_like(dv_ref)

    def step(query_block, diagonal):
        at = pl.multiple_of(query_block * block, block)
        scores = dot(key, qt_ref[:, pl.ds(at, block)])
        square = scores * scores + 1.0
        inverse = lax.rsqrt(square)
        shifted = square * inverse - lse_ref[:, pl.ds(at, block)]
        if diagonal:
            shifted = jnp.where(causal(block), shifted, -1e30)
        weights = jnp.exp(shifted)
        slope = scores * inverse
        along = dot(value, gt_ref[:, pl.ds(at, block)])
        bend = 1.0 + inverse * inverse * (inverse - 1.0)
        score_grad = weights * (bend * along - slope * delta_ref[:, pl.ds(at, block)])
        signed = (slope * weights).astype(BF)
        low_grad = score_grad.astype(BF)
        dv_ref[...] += dot(signed, g_ref[pl.ds(at, block), :])
        dk_ref[...] += dot(low_grad, q_ref[pl.ds(at, block), :])
        dq_ref[:, pl.ds(at, block)] += dot(key_t, low_grad)

    step(index, True)

    def body(query_block, carry):
        step(query_block, False)
        return carry

    lax.fori_loop(index + 1, last_ref[index], body, 0)
    at = pl.multiple_of(index * block, block)
    out_ref[:HD] = (dq_ref[:, pl.ds(at, block)] * float(HD) ** -0.5).astype(BF)
    out_ref[HD : 2 * HD] = dk_ref[...].T.astype(BF)
    out_ref[2 * HD :] = dv_ref[...].T.astype(BF)


def attend_back(last_block, q, qt, k, v, g, gt, lse, delta, block):
    rows = q.shape[0]
    return pl.pallas_call(
        backward_kernel,
        grid_spec=pltpu.PrefetchScalarGridSpec(
            num_scalar_prefetch=1,
            grid=(rows // block,),
            in_specs=[
                whole(q.shape),
                whole(qt.shape),
                pl.BlockSpec((block, HD), lambda i, *_: (i, 0)),
                pl.BlockSpec((block, HD), lambda i, *_: (i, 0)),
                whole(g.shape),
                whole(gt.shape),
                whole(lse.shape),
                whole(delta.shape),
            ],
            out_specs=pl.BlockSpec((3 * HD, block), lambda i, *_: (0, i)),
            scratch_shapes=[
                pltpu.VMEM((HD, rows), F32),
                pltpu.VMEM((block, HD), F32),
                pltpu.VMEM((block, HD), F32),
            ],
        ),
        out_shape=shape_of((3 * HD, rows), BF),
        compiler_params=params(),
        cost_estimate=cost(19),
        name="attend_bwd",
    )(last_block, q, qt, k, v, g, gt, lse, delta)


def head_results(acc, column, w_ref, norm_ref, sums_ref):
    weights = w_ref[...].astype(F32)
    grad = acc * norm_ref[0:1, :] + column * norm_ref[2:3, :]
    sums = jnp.concatenate(
        [
            jnp.sum(weights * acc, axis=0, keepdims=True),
            sums_ref[0:1, :],
            jnp.sum(weights * column, axis=0, keepdims=True),
            sums_ref[1:2, :],
        ],
        axis=0,
    )
    top = sums.astype(BF).astype(F32)
    rest = jnp.concatenate([top, sums - top, jnp.zeros((HD - 8, sums.shape[1]), F32)], axis=0)
    return jnp.concatenate([grad, rest], axis=0).T.astype(BF)


def all_grads_kernel(
    rows, tok_ref, grad_ref, unit_ref, w_ref, norm_ref, sums_ref, out_ref, head_ref, acc_ref, line_ref
):
    half = rows // 2
    step = pl.program_id(0)
    count = out_ref.shape[0]
    found = rearranged(tok_ref[...], grad_ref)
    low = found.astype(BF)
    term = dot(low, unit_ref[...])
    line = jnp.sum(found, axis=1, keepdims=True)

    @pl.when(step == 0)
    def _():
        acc_ref[...] = term
        line_ref[...] = line

    @pl.when(step > 0)
    def _():
        acc_ref[...] += term
        line_ref[...] += line

    turned = found.T.astype(BF)
    for d in range(count):
        at = d * rows
        out_ref[d, :rows, :] = turned[at : at + rows, : 2 * HD]
        out_ref[d, rows:, :] = jnp.concatenate(
            [turned[at : at + half, 2 * HD :], turned[at + half : at + rows, 2 * HD :]], axis=1
        )

    @pl.when(step == pl.num_programs(0) - 1)
    def _():
        head_ref[...] = head_results(acc_ref[...], line_ref[...], w_ref, norm_ref, sums_ref)


def all_grads_out(tok_row, grads, unit, head_w, norms, sums_two, group):
    total = tok_row.shape[1]
    rows = total // group
    width = unit.shape[1]
    count = owners_per_step(group, rows)
    out_rows = rows + rows // 2
    return pl.pallas_call(
        functools.partial(all_grads_kernel, rows),
        grid=(group // count,),
        in_specs=[
            pl.BlockSpec((1, count * rows), lambda i: (0, i)),
            whole(grads.shape),
            pl.BlockSpec((count * rows, width), lambda i: (i, 0)),
            whole(head_w.shape),
            whole(norms.shape),
            whole(sums_two.shape),
        ],
        out_specs=[
            pl.BlockSpec((count, out_rows, 2 * HD), lambda i: (i, 0, 0)),
            whole((width, 4 * HD)),
        ],
        out_shape=[shape_of((group, out_rows, 2 * HD), BF), shape_of((width, 4 * HD), BF)],
        scratch_shapes=[pltpu.VMEM((3 * HD, width), F32), pltpu.VMEM((3 * HD, 1), F32)],
        compiler_params=params(),
        cost_estimate=cost(9),
        name="all_grads_out",
    )(tok_row, grads, unit, head_w, norms, sums_two)


def middle_kernel(places, x_ref, packed_ref, proj_ref, norm_ref, mid_ref, h_ref, o_ref):
    half = packed_ref.shape[1]
    for h, place in enumerate(places):
        piece = packed_ref[place]
        o_ref[:half, h * HD : (h + 1) * HD] = piece[:, :HD]
        o_ref[half:, h * HD : (h + 1) * HD] = piece[:, HD:]
    mid = x_ref[...].astype(F32) + dot(o_ref[...], proj_ref[...], NT)
    mid_ref[...] = mid
    unit, _ = normalize(mid)
    h_ref[...] = (unit * norm_ref[1:2, :] + norm_ref[3:4, :]).astype(BF)


def middle(places, x, packed, weights, proj_at, norms):
    rows, width = x.shape
    return pl.pallas_call(
        functools.partial(middle_kernel, places),
        grid=(1,),
        in_specs=[
            whole(x.shape),
            whole(packed.shape),
            pl.BlockSpec((width, width), lambda i: (0, proj_at)),
            whole(norms.shape),
        ],
        out_specs=[whole((rows, width))] * 3,
        out_shape=[
            shape_of((rows, width), F32),
            shape_of((rows, width), BF),
            shape_of((rows, width), BF),
        ],
        compiler_params=params(),
        cost_estimate=cost(3),
        name="middle",
    )(x, packed, weights, norms)


def hidden_kernel(
    h_ref, dy_ref, inner_ref, outer_ref, act_ref, dpre_ref, dh_ref, out_ref, dh_acc, out_acc
):
    pre = dot(h_ref[...], inner_ref[...])
    root = 0.7978845608028654
    squared = pre * pre
    bend = jnp.tanh(root * (pre + 0.044715 * (squared * pre)))
    act = (0.5 * pre * (1.0 + bend)).astype(BF)
    act_ref[...] = act
    slope = 0.5 * (1.0 + bend) + 0.5 * pre * (1.0 - bend * bend) * (
        root * (1.0 + 3.0 * 0.044715 * squared)
    )
    dpre = (dot(dy_ref[...], outer_ref[...]) * slope).astype(BF)
    dpre_ref[...] = dpre
    dh = dot(dpre, inner_ref[...], NT)
    out = dot(act, outer_ref[...], NT)

    @pl.when(pl.program_id(0) == 0)
    def _():
        dh_acc[...] = dh
        out_acc[...] = out

    @pl.when(pl.program_id(0) > 0)
    def _():
        dh_acc[...] += dh
        out_acc[...] += out

    @pl.when(pl.program_id(0) == pl.num_programs(0) - 1)
    def _():
        dh_ref[...] = dh_acc[...].astype(dh_ref.dtype)
        out_ref[...] = out_acc[...].astype(out_ref.dtype)


def hidden(h, dy, weights, hidden_width, kind):
    rows, width = h.shape
    chunk = 512
    steps = hidden_width // chunk
    return pl.pallas_call(
        hidden_kernel,
        grid=(steps,),
        in_specs=[
            whole(h.shape),
            whole(dy.shape),
            pl.BlockSpec((width, chunk), lambda i: (0, i)),
            pl.BlockSpec((width, chunk), lambda i: (0, i + steps)),
        ],
        out_specs=[
            pl.BlockSpec((rows, chunk), lambda i: (0, i)),
            pl.BlockSpec((rows, chunk), lambda i: (0, i)),
            whole((rows, width)),
            whole((rows, width)),
        ],
        out_shape=[
            shape_of((rows, hidden_width), BF),
            shape_of((rows, hidden_width), BF),
            shape_of((rows, width), kind),
            shape_of((rows, width), kind),
        ],
        scratch_shapes=[pltpu.VMEM((rows, width), F32)] * 2,
        compiler_params=params(),
        cost_estimate=cost(6),
        name="hidden",
    )(h, dy, weights, weights)


def middle_back_kernel(
    places, own_ref, other_ref, dy_ref, mid_ref, norm_ref, proj_ref, dmid_ref, low_ref, packed_ref, sums_ref
):
    half = packed_ref.shape[1]
    dh = own_ref[...] + other_ref[...].astype(F32)
    unit, scale = normalize(mid_ref[...])
    sums_ref[0:1, :] = jnp.sum(dh * unit, axis=0, keepdims=True)
    sums_ref[1:2, :] = jnp.sum(dh, axis=0, keepdims=True)
    dmid = dy_ref[...].astype(F32) + normalize_back(dh * norm_ref[1:2, :], unit, scale)
    dmid_ref[...] = dmid
    low = dmid.astype(BF)
    low_ref[...] = low
    grad = dot(low, proj_ref[...]).astype(BF)
    packed_ref[...] = jnp.zeros_like(packed_ref)
    for h, place in enumerate(places):
        cut = slice(h * HD, (h + 1) * HD)
        packed_ref[place] = jnp.concatenate([grad[:half, cut], grad[half:, cut]], axis=1)


def middle_back(places, group, own, other, dy, mid, norms, weights, proj_at):
    rows, width = mid.shape
    return pl.pallas_call(
        functools.partial(middle_back_kernel, places),
        grid=(1,),
        in_specs=[
            whole(own.shape),
            whole(other.shape),
            whole(dy.shape),
            whole(mid.shape),
            whole(norms.shape),
            pl.BlockSpec((width, width), lambda i: (0, proj_at)),
        ],
        out_specs=[
            whole((rows, width)),
            whole((rows, width)),
            whole((group, rows // 2, 2 * HD)),
            whole((2, width)),
        ],
        out_shape=[
            shape_of((rows, width), F32),
            shape_of((rows, width), BF),
            shape_of((group, rows // 2, 2 * HD), BF),
            shape_of((2, width), F32),
        ],
        compiler_params=params(),
        cost_estimate=cost(4),
        name="middle_back",
    )(own, other, dy, mid, norms, weights)


def weight_kernel(span, h0, h1, p0, p1, dy0, dy1, a0, a1, out_ref):
    index = pl.program_id(0)

    @pl.when(index < span)
    def _():
        out_ref[...] = (dot(h0[...], p0[...], TN) + dot(h1[...], p1[...], TN)).astype(BF)

    @pl.when(index >= span)
    def _():
        out_ref[...] = (dot(dy0[...], a0[...], TN) + dot(dy1[...], a1[...], TN)).astype(BF)


def weight_grads(h_pair, dpre_pair, dy_pair, act_pair):
    rows, width = h_pair[0].shape
    span = act_pair[0].shape[1] // width
    first = pl.BlockSpec((rows, width), lambda i: (0, jnp.minimum(i, span - 1)))
    second = pl.BlockSpec((rows, width), lambda i: (0, jnp.clip(i - span, 0, span - 1)))
    plain = whole((rows, width))
    return pl.pallas_call(
        functools.partial(weight_kernel, span),
        grid=(2 * span,),
        in_specs=[plain, plain, first, first, plain, plain, second, second],
        out_specs=pl.BlockSpec((width, width), lambda i: (0, i)),
        out_shape=shape_of((width, 2 * span * width), BF),
        compiler_params=params(),
        cost_estimate=cost(7),
        name="weight_grads",
    )(*h_pair, *dpre_pair, *dy_pair, *act_pair)


def proj_kernel(low_ref, o_ref, out_ref):
    out_ref[...] = dot(low_ref[...], o_ref[...], TN).astype(BF)


def proj_grads(low, o):
    width = o.shape[1]
    return pl.pallas_call(
        proj_kernel,
        grid=(1,),
        in_specs=[whole(low.shape), whole(o.shape)],
        out_specs=whole((width, width)),
        out_shape=shape_of((width, width), BF),
        compiler_params=params(),
        cost_estimate=cost(2),
        name="proj_grads",
    )(low, o)


def input_back_kernel(places, packed_ref, w_ref, x_ref, dmid_ref, norm_ref, out_ref, flat_ref):
    rows, _ = x_ref.shape
    half = rows // 2
    for h, place in enumerate(places):
        at = 3 * HD * h
        piece = packed_ref[place]
        flat_ref[:, at : at + 2 * HD] = piece[:rows]
        flat_ref[:half, at + 2 * HD : at + 3 * HD] = piece[rows : rows + half, :HD]
        flat_ref[half:, at + 2 * HD : at + 3 * HD] = piece[rows : rows + half, HD:]
    dh = dot(flat_ref[...], w_ref[...], NT)
    unit, scale = normalize(x_ref[...].astype(F32))
    out_ref[...] = (dmid_ref[...] + normalize_back(dh * norm_ref[0:1, :], unit, scale)).astype(BF)


def input_back(places, packed, weights, late_at, x, dmid, norms):
    rows, width = x.shape
    late = 3 * HD * len(places)
    return pl.pallas_call(
        functools.partial(input_back_kernel, places),
        grid=(1,),
        in_specs=[
            whole(packed.shape),
            pl.BlockSpec((width, late), lambda i: (0, late_at)),
            whole(x.shape),
            whole(dmid.shape),
            whole(norms.shape),
        ],
        out_specs=whole((rows, width)),
        out_shape=shape_of((rows, width), BF),
        scratch_shapes=[pltpu.VMEM((rows, late), BF)],
        compiler_params=params(),
        cost_estimate=cost(5),
        name="input_back",
    )(packed, weights, x, dmid, norms)


def adam_step(master, first_state, second_state, grad_term, step_rate, weight_decay):
    first_new = BETA_ONE * first_state + (1.0 - BETA_ONE) * grad_term
    second_new = BETA_TWO * second_state + (1.0 - BETA_TWO) * grad_term * grad_term
    first_hat = first_new / (1.0 - BETA_ONE**STEP)
    second_hat = second_new / (1.0 - BETA_TWO**STEP)
    master_new = master - step_rate * (
        first_hat / (jnp.sqrt(second_hat) + ADAM_EPS) + weight_decay * master
    )
    return (first_new, second_new, master_new)


def shards(
    tokens,
    cotangent,
    seq_lengths,
    slot_token,
    w_qkv,
    w_proj,
    w_inner,
    w_outer,
    norm_gains,
    norm_biases,
    qkv_first,
    qkv_second,
    proj_first,
    proj_second,
    inner_first,
    inner_second,
    outer_first,
    outer_second,
    norm_first,
    norm_second,
):
    side = lax.axis_index("ha")
    group = lax.axis_size("pb") * lax.axis_size("ka")
    rows, width = tokens.shape[1:]
    total = rows * group
    w_rows = w_qkv.shape[0]
    half_width = w_qkv.shape[2]
    heads = 2 * half_width // HD
    hidden_half = w_inner.shape[1]
    places = head_places(group, heads)
    head_at = [0] * group
    for h, place in enumerate(places):
        head_at[place] = h
    block = min(SCORE_BLOCK, total)

    def swap(a):
        return lax.ppermute(a, "ha", [(0, 1), (1, 0)])

    def ordered(own, other):
        return jnp.where(side == 0, own, other), jnp.where(side == 0, other, own)

    def own_micro(a):
        return lax.dynamic_index_in_dim(a, side, 0, False)

    def other_micro(a):
        return lax.dynamic_index_in_dim(a, 1 - side, 0, False)

    x = own_micro(tokens)
    along_z, along_ka = lax.axis_size("pb"), lax.axis_size("ka")
    stepped = along_z == 4 and along_ka == 4

    def flip(a, axis, size, bit):
        return lax.ppermute(a, axis, [(i, i ^ bit) for i in range(size)])

    if stepped:

        def z_flip(a, bit):
            return flip(a, "pb", along_z, bit)

        def x_flip(a):
            return flip(a, "ka", along_ka, 2)

        def c_flip(a):
            return flip(a, "ka", along_ka, 1)

        own = x[None]
        near, far, own_x, own_c = z_flip(own, 1), z_flip(own, 2), x_flip(own), c_flip(own)
    else:
        x_full = lax.all_gather(x, PLANE, axis=0, tiled=True)
    mine = jnp.concatenate(
        [w_qkv.astype(BF).reshape(w_rows, 3 * half_width), w_proj.astype(BF).T], axis=1
    )
    tok_row = own_micro(slot_token).reshape(1, total)
    mine_other, slot_row = swap(mine), slots_of_tokens(tok_row)
    if stepped:
        near, far, own_x, own_c, mine_other, slot_row = tie(
            near, far, own_x, own_c, mine_other, slot_row
        )
        mid_z = jnp.concatenate([near, far])
        last_z, mid_x, mid_c, own_xc = z_flip(far, 1), x_flip(mid_z), c_flip(mid_z), c_flip(own_x)
    low_half, high_half = ordered(mine, mine_other)
    qkv_rows = jnp.concatenate(
        [
            a[:, : 3 * half_width].reshape(w_rows, 3, heads // 2, HD).swapaxes(1, 2)
            for a in (low_half, high_half)
        ],
        axis=1,
    ).reshape(w_rows, heads, 3 * HD)
    proj_rows = jnp.concatenate(
        [a[:, 3 * half_width :] for a in (low_half, high_half)], axis=1
    )
    norm_master = jnp.concatenate([norm_gains, norm_biases], axis=0)
    head_rows = jnp.stack([qkv_rows[:, head_at[d]] for d in range(group)], axis=0)
    head_rows = jnp.concatenate(
        [
            head_rows,
            jnp.broadcast_to(norm_master.astype(BF).T[None], (group, w_rows, 4)),
            jnp.zeros((group, w_rows, HD - 4), BF),
        ],
        axis=2,
    )
    head_w = lax.all_to_all(head_rows, PLANE, 0, 0, tiled=True)
    if stepped:
        last_z, mid_x, mid_c, own_xc, head_w = tie(last_z, mid_x, mid_c, own_xc, head_w)
        last_x, last_c, mid_xc = x_flip(last_z), c_flip(last_z), c_flip(mid_x)
    else:
        head_w, slot_row = tie(head_w, slot_row)
    head_w = head_w.reshape(width, 4 * HD)
    norms = head_w[:, 3 * HD : 3 * HD + 4].astype(F32).T
    head_w = head_w[:, : 3 * HD].T
    main_rows = jnp.concatenate(
        [
            w_inner.astype(BF),
            w_outer.astype(BF).T,
            proj_rows,
        ],
        axis=1,
    )
    if stepped:
        main_rows, mid_x = tie(main_rows, mid_x)
    else:
        main_rows, x_full = tie(main_rows, x_full)
    main_w = lax.all_gather(main_rows, PLANE, axis=0, tiled=True)
    proj_at = 2 * hidden_half // width

    ends = jnp.cumsum(own_micro(seq_lengths))
    starts = jnp.arange(total // block, dtype=jnp.int32) * block
    first_block = jnp.max(jnp.where(ends[None] <= starts[:, None], ends[None], 0), axis=1) // block
    last_block = jnp.min(jnp.where(ends[None] > starts[:, None], ends[None], total), axis=1) // block
    first_block = first_block.astype(jnp.int32)
    last_block = last_block.astype(jnp.int32)

    if stepped:
        z, xc = lax.axis_index("pb"), lax.axis_index("ka")
        at = jnp.stack([z, 0 * z, xc // 2, xc % 2]).astype(jnp.int32)
        groups = ((own, own_x, own_c, own_xc), (mid_z, mid_x, mid_c, mid_xc))
        buffers = qkv_of_piece(at, groups, head_w, norms, total, ())
        last_x, last_c, *buffers = tie(last_x, last_c, *buffers)
        at = jnp.stack([z, 0 * z + 3, xc // 2, xc % 2]).astype(jnp.int32)
        groups = ((last_z, last_x, last_c, c_flip(last_x)),)
        buffers = qkv_of_piece(at, groups, head_w, norms, total, buffers)
        unit, qkv = buffers
    else:
        unit, qkv = qkv_of_head(x_full, head_w, norms)
    q, qt, k, v, vt = sort_qkv(slot_row, qkv)
    o, o_low, lse = attend(first_block, qt, k, vt, block)
    late_rows, o_low = tie(qkv_rows.reshape(w_rows, -1), o_low)
    late_w = lax.all_gather(late_rows, PLANE, axis=0, tiled=True)
    o_packed = lax.all_to_all(slots_out(tok_row, o_low, group), PLANE, 0, 0, tiled=True)
    mid, h_own, o_own = middle(places, x, o_packed, main_w, proj_at, norms)
    h_other = swap(h_own)
    dy_own, dy_other = own_micro(cotangent), other_micro(cotangent)
    act_own, dpre_own, dh_own, out_own = hidden(h_own, dy_own, main_w, hidden_half, F32)
    h_other, dh_own = tie(h_other, dh_own)
    act_other, dpre_other, dh_send, out_send = hidden(h_other, dy_other, main_w, hidden_half, BF)
    dh_got = swap(dh_send)
    main_grad = weight_grads(
        (h_own, h_other), (dpre_own, dpre_other), (dy_own, dy_other), (act_own, act_other)
    )
    dh_got, main_grad = tie(dh_got, main_grad)

    dmid, dmid_low, g_packed, sums_two = middle_back(
        places, group, dh_own, dh_got, dy_own, mid, norms, main_w, proj_at
    )
    late_w, main_grad, _ = tie(late_w, main_grad, dmid_low)
    main_sum = lax.psum_scatter(main_grad, PLANE, scatter_dimension=0, tiled=True)
    g_packed = lax.all_to_all(g_packed, PLANE, 0, 0, tiled=True)
    proj_grad = proj_grads(dmid_low, o_own).reshape(group, w_rows, width)
    proj_grad, g_packed, out_send, out_own = tie(proj_grad, g_packed, out_send, out_own)
    proj_grad = lax.all_to_all(proj_grad, PLANE, 0, 0, tiled=True)
    out_got = swap(out_send)
    layer_own = (mid + out_own + out_got.astype(F32)).astype(BF)
    layer_out = jnp.stack(ordered(layer_own, swap(layer_own)))
    g, gt, delta = sort_grad(slot_row, g_packed, o)
    dqkv = attend_back(last_block, q, qt, k, v, g, gt, lse, delta, block)
    packed, head_grad = all_grads_out(tok_row, dqkv, unit, head_w, norms, sums_two, group)
    packed, proj_grad, layer_out = tie(packed, proj_grad, layer_out)
    dqkv_own = lax.all_to_all(packed, PLANE, 0, 0, tiled=True)

    head_grad = head_grad.reshape(group, 2, w_rows // 2, 4 * HD)
    keep, send = ordered(head_grad[:, 0], head_grad[:, 1])
    keep = (keep.astype(F32) + swap(send).astype(F32)).astype(BF)
    keep, dqkv_own, main_sum = tie(keep, dqkv_own, main_sum)
    input_low = input_back(places, dqkv_own, late_w, 0, x, dmid, norms)
    head_grad = lax.all_to_all(keep, PLANE, 0, 0, tiled=True)
    input_grad = jnp.stack(ordered(input_low, swap(input_low))).astype(F32)

    norm_parts = head_grad[:, :, 3 * HD : 3 * HD + 8].astype(F32)
    norm_parts = norm_parts[:, :, :4] + norm_parts[:, :, 4:]
    first_sums = sum(norm_parts[place] for place in places)
    second_sums = jnp.sum(norm_parts, axis=0)
    norm_grad = jnp.stack(
        [first_sums[:, 0], second_sums[:, 1], first_sums[:, 2], second_sums[:, 3]]
    )
    norm_grad = jnp.concatenate(ordered(norm_grad, swap(norm_grad)), axis=1)
    qkv_part = jnp.stack([head_grad[place, :, : 3 * HD] for place in places], axis=1)
    qkv_part = qkv_part.reshape(w_rows // 2, 2, heads // 2, 3, HD)
    keep, send = ordered(qkv_part[:, 0], qkv_part[:, 1])
    qkv_grad = jnp.concatenate(ordered(keep, swap(send)), axis=0).astype(F32)
    qkv_grad = qkv_grad.swapaxes(1, 2).reshape(w_rows, 3, half_width)
    inner_grad = main_sum[:, :hidden_half].astype(F32)
    outer_grad = main_sum[:, hidden_half:].astype(F32).T
    proj_part = jnp.sum(proj_grad.astype(F32), axis=0)
    keep, send = ordered(proj_part[:, :half_width], proj_part[:, half_width:])
    proj_grad = (keep + swap(send.astype(BF)).astype(F32)).T

    qkv_out = adam_step(w_qkv, qkv_first, qkv_second, qkv_grad / MICRO, RATE_MATRIX, DECAY_RATE)
    proj_out = adam_step(w_proj, proj_first, proj_second, proj_grad / MICRO, RATE_PROJ, DECAY_RATE)
    inner_out = adam_step(
        w_inner, inner_first, inner_second, inner_grad / MICRO, RATE_MATRIX, DECAY_RATE
    )
    outer_out = adam_step(
        w_outer, outer_first, outer_second, outer_grad / MICRO, RATE_MATRIX, DECAY_RATE
    )
    norm_grad = norm_grad / MICRO
    norm_out = adam_step(norm_master, norm_first, norm_second, norm_grad, RATE_NORM, 0.0)
    norm_two_grad = jnp.stack([norm_grad[1], norm_grad[3]])
    return (
        layer_out,
        input_grad,
        *qkv_out,
        *proj_out,
        *inner_out,
        *outer_out,
        *norm_out,
        norm_two_grad,
    )


def solution(mesh):
    tok = P(None, PLANE, None)
    qkv = P(PLANE, None, "ha")
    down = P("ha", PLANE)
    inner = P(PLANE, "ha")
    norm = P(None, PLANE)
    in_specs = (
        (tok, tok, P(), P(), qkv, down, inner, down, norm, norm)
        + (qkv, qkv, down, down, inner, inner, down, down, norm, norm)
    )
    out_specs = (
        (tok, tok, qkv, qkv, qkv, down, down, down)
        + (inner, inner, inner, down, down, down, norm, norm, norm, norm)
    )
    return jax.shard_map(shards, mesh=mesh, in_specs=in_specs, out_specs=out_specs, check_vma=False)
```

time: 419 us -> 314 us (0.75)
  waiting for transfers between devices: 201 us -> 92.6 us
  starting transfers between devices: 38.7 us -> 56.2 us
  Pallas kernels: 128 us -> 118 us
    all_gather x1, waiting for transfers between devices: 59.1 us -> 1.12 us  [shards(): main_w = lax.all_gather(main_rows, PLANE, axis=0, tiled=True)]
    all_gather x2 -> x1, waiting for transfers between devices: 48.2 us -> 15.1 us  [shards(): late_w = lax.all_gather(late_rows, PLANE, axis=0, tiled=True)]
    ppermute x8 -> x10, waiting for transfers between devices: 31.2 us -> 9.54 us  [swap(): return lax.ppermute(a, 'ha', [(0, 1), (1, 0)])]
    ppermute x0 -> x12, waiting for transfers between devices: none -> 12.8 us  [flip(): return lax.ppermute(a, axis, [(i, i ^ bit) for i in range(size)])]
    ppermute x0 -> x12, starting transfers between devices: none -> 12.4 us  [flip(): return lax.ppermute(a, axis, [(i, i ^ bit) for i in range(size)])]
    pallas_call x7 -> x9, Pallas kernels: 69.2 us -> 60.7 us  [the longest x2 12.3 us: qkv_of_piece(): pl.pallas_call(functools.partial(qkv_piece_kernel, counts), grid_spec=plt...]
    all_to_all x4 -> x5, starting transfers between devices: 20 us -> 26.4 us  [the longest x1 7.48 us: shards(): head_grad = lax.all_to_all(keep, PLANE, 0, 0, tiled=True)]
    all_to_all x4 -> x5, waiting for transfers between devices: 50.4 us -> 44.4 us  [the longest x1 25.3 us: shards(): dqkv_own = lax.all_to_all(packed, PLANE, 0, 0, tiled=True)]
  transfers between devices with their start and end apart: 17 -> 31, of which waited for: 13 -> 13; matrix products, arithmetic and copies ran while one was open for 6% -> 7% of each run, Pallas kernels for 31% -> 36%
where the time goes in v2:
time: 314 us; the launch traced here: 313 us
  Pallas kernels  118 us (38%)
  waiting for transfers between devices  92.6 us (29%)
  starting transfers between devices  56.2 us (18%)
  other arithmetic  16.3 us (5%)
  local copies, waits for them, and re-layouts  15 us (5%)
  between operations  14.7 us (5%)
    all_to_all x1, waiting for transfers between devices, shards(): dqkv_own = lax.all_to_all(packed, PLANE, 0, 0, tiled=True)  25.3 us
    pallas_call x1, Pallas kernels, attend_back(): pl.pallas_call(backward_kernel, grid_spec=pltpu.PrefetchScalarGridSpec(nu...  19.4 us
    all_gather x1, waiting for transfers between devices, shards(): late_w = lax.all_gather(late_rows, PLANE, axis=0, tiled=True)  15.1 us
    all_to_all x1, waiting for transfers between devices, shards(): lax.all_to_all(slots_out(tok_row, o_low, group), PLANE, 0, 0, tiled=True)  14.3 us
    ppermute x10, starting transfers between devices, swap(): return lax.ppermute(a, 'ha', [(0, 1), (1, 0)])  13.4 us
    pallas_call x1, Pallas kernels, attend(): pl.pallas_call(forward_kernel, grid_spec=pltpu.PrefetchScalarGridSpec(num...  13.3 us
    pallas_call x2, Pallas kernels, hidden(): pl.pallas_call(hidden_kernel, grid=(steps,), in_specs=[whole(h.shape), wh...  13.3 us
    ppermute x12, waiting for transfers between devices, flip(): return lax.ppermute(a, axis, [(i, i ^ bit) for i in range(size)])  12.8 us
  transfers between devices with their start and end apart: 31, of which 13 were waited for; matrix products, arithmetic and copies ran while one was open for 7% of the time, Pallas kernels for 36%

profile of v2, /device:TPU:0, one launch (start us, length us, event | category | flops | bytes accessed | tf_op | source)
XLA Modules:
  0.0 313.0 jit_solution(15067600506840588715)
XLA Ops:
  8.3 3.1 collective-permute-start
  11.4 2.6 collective-permute-start.1
  14.0 1.5 collective-permute-start.2
  17.4 1.6 collective-permute-start.4
  19.8 7.8 %slots_of_tokens.1.slot_ref = s32[1,3072]{1,0:T(1,128)} custom-call(s32[1,3072]{1,0:T(1,128)} %constant_dynamic-slice_fusion.2.tok_ref), custom_call_target="tpu_custom_call" | custom-call | flops 1600000000 | bytes 8000000 | tf_op jit(solution)/shard_map/slots_of_tokens/pallas_call | solution.py:124
  32.7 4.0 %all-to-all-start = ((bf16[16,48,256]{2,1,0:T(8,128)(2,1)}), bf16[16,48,256]{2,1,0:T(8,128)(2,1)S(1)}, u32[]{:S(2)}, u32[]{:S(2)}) async-start(bf16[16,48,256]{2,1,0:T(8,128)(2,1)} %maximum_maximum_fusion), calls=%async_computation | async-start | bytes 786432 | tf_op jit(solution)/shard_map/all_to_all | solution.py:888
  36.8 2.0 collective-permute-start.5
  39.7 12.7 %collective-permute-done.5.refs_0_ = bf16[1,192,768]{2,1,0:T(8,128)(2,1)S(1)} collective-permute-done((bf16[1,192,768]{2,1,0:T(8,128)(2,1)S(1)}, bf16[1,192,768]{2,1,0:T(8,128)(2,1)S(1)}, u32[]{:S(2)}, u32[]{:S(2)}) %collective-permute-start.5) | collective-permute-done | bytes 294944 | tf_op jit(solution)/shard_map/ppermute | solution.py:839
  53.5 1.5 collective-permute-start.9
  57.0 8.2 %qkv_piece.2 = (bf16[3072,768]{1,0:T(8,128)(2,1)}, bf16[192,3072]{1,0:T(8,128)(2,1)}) custom-call(s32[4]{0:T(128)} %add_add_fusion.1.at_ref, bf16[1,192,768]{2,1,0:T(8,128)(2,1)} %copy-done.19, bf16[1,192,768]{2,1,0:T(8,128)(2,1)} %copy-done.35, bf16[1,192,768]{2,1,0:T(8,128)(2,1)} %copy-done.36, bf16[1,192,768]{2,1,0:T(8,128)(2,1)} %copy-done.37, ...), custom_call_target="tpu_custom_call" | custom-call | flops 1800000000 | bytes 9000000 | tf_op jit(solution)/shard_map/qkv_piece/pallas_call | solution.py:178
  66.9 1.1 reshape_reshape.3
  68.7 4.2 %qkv_piece.3 = (bf16[3072,768]{1,0:T(8,128)(2,1)}, bf16[192,3072]{1,0:T(8,128)(2,1)}) custom-call(s32[4]{0:T(128)} %add_add_fusion.at_ref, bf16[1,192,768]{2,1,0:T(8,128)(2,1)} %copy-done.14, bf16[1,192,768]{2,1,0:T(8,128)(2,1)} %copy-done.15, bf16[1,192,768]{2,1,0:T(8,128)(2,1)} %copy-done.16, ...), custom_call_target="tpu_custom_call", output_to_operand_aliasing={{0}: (7, {}), {1}: (8, {})} | custom-call | flops 600000000 | bytes 3000000 | tf_op jit(solution)/shard_map/qkv_piece/pallas_call | solution.py:178
  72.9 7.0 %sort_qkv.1 = (bf16[3072,64]{1,0:T(8,128)(2,1)}, bf16[64,3072]{1,0:T(8,128)(2,1)}, bf16[3072,64]{1,0:T(8,128)(2,1)}, bf16[3072,64]{1,0:T(8,128)(2,1)}, bf16[64,3072]{1,0:T(8,128)(2,1)}) custom-call(s32[1,3072]{1,0:T(1,128)} %slots_of_tokens.1.slot_ref, bf16[192,3072]{1,0:T(8,128)(2,1)} %get-tuple-element.103.qkv_ref), custom_call_target="tpu_custom_call" | custom-call | flops 1400000000 | bytes 7000000 | tf_op jit(solution)/shard_map/sort_qkv/pallas_call | solution.py:236
  79.9 13.3 %attend_fwd.1 = (f32[64,3072]{1,0:T(8,128)}, bf16[64,3072]{1,0:T(8,128)(2,1)}, f32[1,3072]{1,0:T(1,128)}) custom-call(s32[6]{0:T(128)} %and_select_fusion.first_ref, bf16[64,3072]{1,0:T(8,128)(2,1)} %get-tuple-element.105.qt_ref, bf16[3072,64]{1,0:T(8,128)(2,1)} %get-tuple-element.106.k_ref, bf16[64,3072]{1,0:T(8,128)(2,1)} %get-tuple-element.108.vt_ref), custom_call_target="tpu_custom_call" | custom-call | flops 2600000000 | bytes 13000000 | tf_op jit(solution)/shard_map/attend_fwd/pallas_call | solution.py:291
  93.2 6.1 %slots_out.1 = bf16[16,96,128]{2,1,0:T(8,128)(2,1)} custom-call(s32[1,3072]{1,0:T(1,128)} %constant_dynamic-slice_fusion.2.tok_ref, bf16[64,3072]{1,0:T(8,128)(2,1)} %get-tuple-element.110.low_ref), custom_call_target="tpu_custom_call" | custom-call | flops 1200000000 | bytes 6000000 | tf_op jit(solution)/shard_map/slots_out/pallas_call | solution.py:326
  99.3 3.8 %all-to-all-start.1 = ((bf16[16,96,128]{2,1,0:T(8,128)(2,1)}), bf16[16,96,128]{2,1,0:T(8,128)(2,1)S(1)}, u32[]{:S(2)}, u32[]{:S(2)}) async-start(bf16[16,96,128]{2,1,0:T(8,128)(2,1)} %slots_out.1), calls=%async_computation.1 | async-start | bytes 786432 | tf_op jit(solution)/shard_map/all_to_all | solution.py:935
  104.1 14.3 %all-to-all-done.1.packed_ref = bf16[16,96,128]{2,1,0:T(8,128)(2,1)S(1)} async-done(((bf16[16,96,128]{2,1,0:T(8,128)(2,1)}), bf16[16,96,128]{2,1,0:T(8,128)(2,1)S(1)}, u32[]{:S(2)}, u32[]{:S(2)}) %all-to-all-start.1) | async-done | bytes 393248 | tf_op jit(solution)/shard_map/all_to_all | solution.py:935
  118.4 1.1 all-gather.3.cloned.1.call-done.proj_ref.inner_ref.outer_ref
  119.6 3.1 %middle.1 = (f32[192,768]{1,0:T(8,128)}, bf16[192,768]{1,0:T(8,128)(2,1)}, bf16[192,768]{1,0:T(8,128)(2,1)}) custom-call(bf16[192,768]{1,0:T(8,128)(2,1)} %fusion.23.x_ref, bf16[16,96,128]{2,1,0:T(8,128)(2,1)} %copy-done.4, bf16[768,3840]{1,0:T(8,128)(2,1)} %all-gather.3.cloned.1.call-done.proj_ref.inner_ref.outer_ref, f32[4,768]{1,0:T(4,128)} %bitcast.212), custom_call_target="tpu_custom_call" | custom-call | flops 600000000 | bytes 3000000 | tf_op jit(solution)/shard_map/middle/pallas_call | solution.py:555
  122.7 1.4 collective-permute-start.13
  125.0 6.8 %hidden.2 = (bf16[192,1536]{1,0:T(8,128)(2,1)}, bf16[192,1536]{1,0:T(8,128)(2,1)}, f32[192,768]{1,0:T(8,128)}, f32[192,768]{1,0:T(8,128)}) custom-call(bf16[192,768]{1,0:T(8,128)(2,1)} %get-tuple-element.112.h_ref.h0, bf16[192,768]{1,0:T(8,128)(2,1)} %get-tuple-element.178.dy_ref.dy0, ...), custom_call_target="tpu_custom_call" | custom-call | flops 1200000000 | bytes 6000000 | tf_op jit(solution)/shard_map/hidden/pallas_call | solution.py:613
  132.8 6.5 %hidden.3 = (bf16[192,1536]{1,0:T(8,128)(2,1)}, bf16[192,1536]{1,0:T(8,128)(2,1)}, bf16[192,768]{1,0:T(8,128)(2,1)}, bf16[192,768]{1,0:T(8,128)(2,1)}) custom-call(bf16[192,768]{1,0:T(8,128)(2,1)} %copy-done.6, bf16[192,768]{1,0:T(8,128)(2,1)} %get-tuple-element.177.dy_ref.dy1, bf16[768,3840]{1,0:T(8,128)(2,1)} %all-gather.3.cloned.1.call-done.proj_ref.inner_ref.outer_ref, ...), custom_call_target="tpu_custom_call" | custom-call | flops 1200000000 | bytes 6000000 | tf_op jit(solution)/shard_map/hidden/pallas_call | solution.py:613
  139.3 1.5 collective-permute-start.14
  140.8 6.9 %weight_grads.1 = bf16[768,3072]{1,0:T(8,128)(2,1)} custom-call(bf16[192,768]{1,0:T(8,128)(2,1)} %get-tuple-element.112.h_ref.h0, bf16[192,768]{1,0:T(8,128)(2,1)} %copy-done.6, bf16[192,1536]{1,0:T(8,128)(2,1)} %get-tuple-element.117.p0, bf16[192,1536]{1,0:T(8,128)(2,1)} %get-tuple-element.118.p1, bf16[192,768]{1,0:T(8,128)(2,1)} %get-tuple-element.178.dy_ref.dy0, ...), custom_call_target="tpu_custom_call" | custom-call | flops 1400000000 | bytes 7000000 | tf_op jit(solution)/shard_map/weight_grads/pallas_call | solution.py:709
  148.9 3.5 %middle_back.1 = (f32[192,768]{1,0:T(8,128)}, bf16[192,768]{1,0:T(8,128)(2,1)}, bf16[16,96,128]{2,1,0:T(8,128)(2,1)}, f32[2,768]{1,0:T(2,128)}) custom-call(f32[192,768]{1,0:T(8,128)} %get-tuple-element.114.own_ref, bf16[192,768]{1,0:T(8,128)(2,1)} %copy-done.18, bf16[192,768]{1,0:T(8,128)(2,1)} %get-tuple-element.178.dy_ref.dy0, ...), custom_call_target="tpu_custom_call" | custom-call | flops 800000000 | bytes 4000000 | tf_op jit(solution)/shard_map/middle_back/pallas_call | solution.py:662
  152.4 15.1 %all-gather.5.cloned.1.call-done.w_ref = bf16[768,2304]{1,0:T(8,128)(2,1)} async-done(((bf16[48,2304]{1,0:T(8,128)(2,1)}), bf16[768,2304]{1,0:T(8,128)(2,1)}) %all-gather.5.cloned.1.call-update) | async-done | bytes 3538960 | tf_op jit(solution)/shard_map/all_gather | solution.py:934
  167.5 3.7 %all-to-all-start.2 = ((bf16[16,96,128]{2,1,0:T(8,128)(2,1)}), bf16[16,96,128]{2,1,0:T(8,128)(2,1)S(1)}, u32[]{:S(2)}, u32[]{:S(2)}) async-start(bf16[16,96,128]{2,1,0:T(8,128)(2,1)} %get-tuple-element.125), calls=%async_computation.2 | async-start | bytes 786432 | tf_op jit(solution)/shard_map/all_to_all | solution.py:953
  171.3 2.6 proj_grads.1
  173.9 9.6 %all-to-all-done.2.packed_ref = bf16[16,96,128]{2,1,0:T(8,128)(2,1)S(1)} async-done(((bf16[16,96,128]{2,1,0:T(8,128)(2,1)}), bf16[16,96,128]{2,1,0:T(8,128)(2,1)S(1)}, u32[]{:S(2)}, u32[]{:S(2)}) %all-to-all-start.2) | async-done | bytes 393248 | tf_op jit(solution)/shard_map/all_to_all | solution.py:953
  184.2 3.9 %all-to-all-start.3 = ((bf16[16,48,768]{2,1,0:T(8,128)(2,1)}), bf16[16,48,768]{2,1,0:T(8,128)(2,1)S(1)}, u32[]{:S(2)}, u32[]{:S(2)}) async-start(bf16[16,48,768]{2,1,0:T(8,128)(2,1)} %bitcast.198), calls=%async_computation.3 | async-start | bytes 2359296 | tf_op jit(solution)/shard_map/all_to_all | solution.py:956
  188.1 1.5 collective-permute-start.15
  190.2 6.4 %sort_grad.1 = (bf16[3072,64]{1,0:T(8,128)(2,1)}, bf16[64,3072]{1,0:T(8,128)(2,1)}, f32[1,3072]{1,0:T(1,128)}) custom-call(s32[1,3072]{1,0:T(1,128)} %slots_of_tokens.1.slot_ref, bf16[16,96,128]{2,1,0:T(8,128)(2,1)} %copy-done.13, f32[64,3072]{1,0:T(8,128)} %get-tuple-element.129.o_ref), custom_call_target="tpu_custom_call" | custom-call | flops 1200000000 | bytes 6000000 | tf_op jit(solution)/shard_map/sort_grad/pallas_call | solution.py:369
  197.5 1.5 collective-permute-start.16
  199.0 19.4 %attend_bwd.1.grad_ref = bf16[192,3072]{1,0:T(8,128)(2,1)} custom-call(s32[6]{0:T(128)} %and_select_fusion.1.last_ref, bf16[3072,64]{1,0:T(8,128)(2,1)} %get-tuple-element.104.q_ref, bf16[64,3072]{1,0:T(8,128)(2,1)} %get-tuple-element.105.qt_ref, bf16[3072,64]{1,0:T(8,128)(2,1)} %get-tuple-element.106.k_ref, bf16[3072,64]{1,0:T(8,128)(2,1)} %get-tuple-element.107.v_ref, ...), custom_call_target="tpu_custom_call" | custom-call | flops 3800000000 | bytes 19000000 | tf_op jit(solution)/shard_map/attend_bwd/pallas_call | solution.py:432
  218.5 11.5 %all_grads_out.1 = (bf16[16,288,128]{2,1,0:T(8,128)(2,1)}, bf16[768,256]{1,0:T(8,128)(2,1)}) custom-call(s32[1,3072]{1,0:T(1,128)} %constant_dynamic-slice_fusion.2.tok_ref, bf16[192,3072]{1,0:T(8,128)(2,1)} %attend_bwd.1.grad_ref, bf16[3072,768]{1,0:T(8,128)(2,1)} %get-tuple-element.134.unit_ref, bf16[192,768]{1,0:T(8,128)(2,1)} %bitcast.205, ...), custom_call_target="tpu_custom_call" | custom-call | flops 1800000000 | bytes 9000000 | tf_op jit(solution)/shard_map/all_grads_out/pallas_call | solution.py:518
  230.9 7.2 %all-to-all-start.4 = ((bf16[16,288,128]{2,1,0:T(8,128)(2,1)}), bf16[16,288,128]{2,1,0:T(8,128)(2,1)S(1)}, u32[]{:S(2)}, u32[]{:S(2)}) async-start(bf16[16,288,128]{2,1,0:T(8,128)(2,1)} %get-tuple-element.142), calls=%async_computation.4 | async-start | bytes 2359296 | tf_op jit(solution)/shard_map/all_to_all | solution.py:964
  238.2 1.5 collective-permute-start.17
  240.6 5.4 %collective-permute-done.17 = bf16[16,24,256]{2,1,0:T(8,128)(2,1)S(1)} collective-permute-done((bf16[16,24,256]{2,1,0:T(8,128)(2,1)S(1)}, bf16[16,24,256]{2,1,0:T(8,128)(2,1)S(1)}, u32[]{:S(2)}, u32[]{:S(2)}) %collective-permute-start.17) | collective-permute-done | bytes 196640 | tf_op jit(solution)/shard_map/ppermute | solution.py:823
  247.4 25.3 %all-to-all-done.4.packed_ref = bf16[16,288,128]{2,1,0:T(8,128)(2,1)S(1)} async-done(((bf16[16,288,128]{2,1,0:T(8,128)(2,1)}), bf16[16,288,128]{2,1,0:T(8,128)(2,1)S(1)}, u32[]{:S(2)}, u32[]{:S(2)}) %all-to-all-start.4) | async-done | bytes 1179680 | tf_op jit(solution)/shard_map/all_to_all | solution.py:964
  273.7 4.9 %input_back.1 = bf16[192,768]{1,0:T(8,128)(2,1)} custom-call(bf16[16,288,128]{2,1,0:T(8,128)(2,1)} %copy-done.2, bf16[768,2304]{1,0:T(8,128)(2,1)} %all-gather.5.cloned.1.call-done.w_ref, bf16[192,768]{1,0:T(8,128)(2,1)} %fusion.23.x_ref, f32[192,768]{1,0:T(8,128)} %get-tuple-element.148.dmid_ref, f32[4,768]{1,0:T(4,128)} %bitcast.215), custom_call_target="tpu_custom_call" | custom-call | flops 1000000000 | bytes 5000000 | tf_op jit(solution)/shard_map/input_back/pallas_call | solution.py:756
  278.6 1.5 collective-permute-start.18
  280.1 7.5 %all-to-all-start.5 = ((bf16[16,24,256]{2,1,0:T(8,128)(2,1)}), bf16[16,24,256]{2,1,0:T(8,128)(2,1)S(1)}, u32[]{:S(2)}, u32[]{:S(2)}) async-start(bf16[16,24,256]{2,1,0:T(8,128)(2,1)} %fusion.3), calls=%async_computation.6 | async-start | bytes 393216 | tf_op jit(solution)/shard_map/all_to_all | solution.py:971
  287.6 2.0 multiply_subtract_fusion.1
  290.7 1.1 maximum_convert_fusion
  291.8 4.8 %all-to-all-done.5 = bf16[16,24,256]{2,1,0:T(8,128)(2,1)S(1)} async-done(((bf16[16,24,256]{2,1,0:T(8,128)(2,1)}), bf16[16,24,256]{2,1,0:T(8,128)(2,1)S(1)}, u32[]{:S(2)}, u32[]{:S(2)}) %all-to-all-start.5) | async-done | bytes 196640 | tf_op jit(solution)/shard_map/all_to_all | solution.py:971
  298.2 1.4 collective-permute-start.19
  299.6 1.4 collective-permute-done.21
  302.3 1.1 collective-permute-done.19
  (213 shorter events, 32.2 us)
Async XLA Ops:
  7.2 11.7 %copy-start.30 = (s32[2,3072]{1,0:T(2,128)S(1)}, s32[2,3072]{1,0:T(2,128)}, u32[]{:S(2)}) copy-start(s32[2,3072]{1,0:T(2,128)} %param.23) | copy-start | bytes 73732
  7.2 12.3 %copy-start.31 = (f32[2,48]{1,0:T(2,128)S(1)}, f32[2,48]{1,0:T(2,128)}, u32[]{:S(2)}) copy-start(f32[2,48]{1,0:T(2,128)} %param.29) | copy-start | bytes 1156
  7.2 12.3 %copy-start.32 = (f32[2,48]{1,0:T(2,128)S(1)}, f32[2,48]{1,0:T(2,128)}, u32[]{:S(2)}) copy-start(f32[2,48]{1,0:T(2,128)} %param.28) | copy-start | bytes 1156
  8.3 19.3 %copy-start.19 = (bf16[1,192,768]{2,1,0:T(8,128)(2,1)}, bf16[1,192,768]{2,1,0:T(8,128)(2,1)S(1)}, u32[]{:S(2)}) copy-start(bf16[1,192,768]{2,1,0:T(8,128)(2,1)S(1)} %constant_dynamic-slice_fusion.refs_0_) | copy-start | bytes 884740
  8.3 19.3 %collective-permute-start = (bf16[1,192,768]{2,1,0:T(8,128)(2,1)S(1)}, bf16[1,192,768]{2,1,0:T(8,128)(2,1)S(1)}, u32[]{:S(2)}, u32[]{:S(2)}) collective-permute-start(bf16[1,192,768]{2,1,0:T(8,128)(2,1)S(1)} %constant_dynamic-slice_fusion.refs_0_), channel_id=1, source_target_pairs={{0,8},{8,0},{16,24},{24,16},{1,9},{9,1},{17,25},{25,17},{2,10},{10... | collective-permute-start | bytes 884744 | tf_op jit(solution)/shard_map/ppermute | solution.py:839
  11.4 16.2 %collective-permute-start.1 = (bf16[1,192,768]{2,1,0:T(8,128)(2,1)S(1)}, bf16[1,192,768]{2,1,0:T(8,128)(2,1)S(1)}, u32[]{:S(2)}, u32[]{:S(2)}) collective-permute-start(bf16[1,192,768]{2,1,0:T(8,128)(2,1)S(1)} %constant_dynamic-slice_fusion.refs_0_), channel_id=1, source_target_pairs={{0,16},{8,24},{16,0},{24,8},{1,17},{9,25},{17,1},{25,9},{2,18},{10... | collective-permute-start | bytes 884744 | tf_op jit(solution)/shard_map/ppermute | solution.py:839
  14.0 13.6 %collective-permute-start.2 = (bf16[1,192,768]{2,1,0:T(8,128)(2,1)S(1)}, bf16[1,192,768]{2,1,0:T(8,128)(2,1)S(1)}, u32[]{:S(2)}, u32[]{:S(2)}) collective-permute-start(bf16[1,192,768]{2,1,0:T(8,128)(2,1)S(1)} %constant_dynamic-slice_fusion.refs_0_), channel_id=1, source_target_pairs={{0,4},{2,6},{4,0},{6,2},{1,5},{3,7},{5,1},{7,3},{8,12},{10,14},{12... | collective-permute-start | bytes 884744 | tf_op jit(solution)/shard_map/ppermute | solution.py:839
  15.5 12.2 %collective-permute-start.3 = (bf16[1,192,768]{2,1,0:T(8,128)(2,1)S(1)}, bf16[1,192,768]{2,1,0:T(8,128)(2,1)S(1)}, u32[]{:S(2)}, u32[]{:S(2)}) collective-permute-start(bf16[1,192,768]{2,1,0:T(8,128)(2,1)S(1)} %constant_dynamic-slice_fusion.refs_0_), channel_id=1, source_target_pairs={{0,2},{2,0},{4,6},{6,4},{1,3},{3,1},{5,7},{7,5},{8,10},{10,8},{12,... | collective-permute-start | bytes 884744 | tf_op jit(solution)/shard_map/ppermute | solution.py:839
  17.4 10.2 %collective-permute-start.4 = (bf16[48,1536]{1,0:T(8,128)(2,1)S(1)}, bf16[48,1536]{1,0:T(8,128)(2,1)S(1)}, u32[]{:S(2)}, u32[]{:S(2)}) collective-permute-start(bf16[48,1536]{1,0:T(8,128)(2,1)S(1)} %pad_maximum_fusion.4), channel_id=1, source_target_pairs={{0,1},{1,0},{2,3},{3,2},{4,5},{5,4},{6,7},{7,6},{8,9},{9,8},{10,11... | collective-permute-start | bytes 442376 | tf_op jit(solution)/shard_map/ppermute | solution.py:823
  29.2 23.2 %collective-permute-start.6 = (bf16[2,192,768]{2,1,0:T(8,128)(2,1)}, bf16[2,192,768]{2,1,0:T(8,128)(2,1)}, u32[]{:S(2)}, u32[]{:S(2)}) collective-permute-start(bf16[2,192,768]{2,1,0:T(8,128)(2,1)} %constant_dynamic-update-slice_fusion.refs_4_), channel_id=1, source_target_pairs={{0,4},{2,6},{4,0},{6,2},{1,5},{3,7},{5,1},{7,3},{8,12},{10,14},{12... | collective-permute-start | bytes 1769480 | tf_op jit(solution)/shard_map/ppermute | solution.py:839
  30.2 22.3 %collective-permute-start.7 = (bf16[2,192,768]{2,1,0:T(8,128)(2,1)}, bf16[2,192,768]{2,1,0:T(8,128)(2,1)}, u32[]{:S(2)}, u32[]{:S(2)}) collective-permute-start(bf16[2,192,768]{2,1,0:T(8,128)(2,1)} %constant_dynamic-update-slice_fusion.refs_4_), channel_id=1, source_target_pairs={{0,2},{2,0},{4,6},{6,4},{1,3},{3,1},{5,7},{7,5},{8,10},{10,8},{12,... | collective-permute-start | bytes 1769480 | tf_op jit(solution)/shard_map/ppermute | solution.py:839
  32.7 19.8 %all-to-all-start = ((bf16[16,48,256]{2,1,0:T(8,128)(2,1)}), bf16[16,48,256]{2,1,0:T(8,128)(2,1)S(1)}, u32[]{:S(2)}, u32[]{:S(2)}) async-start(bf16[16,48,256]{2,1,0:T(8,128)(2,1)} %maximum_maximum_fusion), calls=%async_computation | async-start | bytes 786432 | tf_op jit(solution)/shard_map/all_to_all | solution.py:888
  36.7 16.0 %copy-start.38 = (s32[2,2]{1,0:T(2,128)S(1)}, s32[2,2]{1,0:T(2,128)}, u32[]{:S(2)}) copy-start(s32[2,2]{1,0:T(2,128)} %param.22) | copy-start | bytes 52
  36.7 82.9 %all-gather.3.cloned.1.call-start = ((), (), s32[]{:S(2)}) async-start(), calls=%async_computation.7 | async-start | bytes 6266880 | tf_op jit(solution)/shard_map/all_gather | solution.py:909
  36.8 15.6 %collective-permute-start.5 = (bf16[1,192,768]{2,1,0:T(8,128)(2,1)S(1)}, bf16[1,192,768]{2,1,0:T(8,128)(2,1)S(1)}, u32[]{:S(2)}, u32[]{:S(2)}) collective-permute-start(bf16[1,192,768]{2,1,0:T(8,128)(2,1)S(1)} %collective-permute-done.1), channel_id=1, source_target_pairs={{0,8},{8,0},{16,24},{24,16},{1,9},{9,1},{17,25},{25,17},{2,10},{10... | collective-permute-start | bytes 884744 | tf_op jit(solution)/shard_map/ppermute | solution.py:839
  38.8 13.6 %collective-permute-start.8 = (bf16[1,192,768]{2,1,0:T(8,128)(2,1)}, bf16[1,192,768]{2,1,0:T(8,128)(2,1)S(1)}, u32[]{:S(2)}, u32[]{:S(2)}) collective-permute-start(bf16[1,192,768]{2,1,0:T(8,128)(2,1)} %copy-done.35), channel_id=1, source_target_pairs={{0,2},{2,0},{4,6},{6,4},{1,3},{3,1},{5,7},{7,5},{8,10},{10,8},{12,... | collective-permute-start | bytes 884744 | tf_op jit(solution)/shard_map/ppermute | solution.py:839
  52.5 12.7 %copy-start.14 = (bf16[1,192,768]{2,1,0:T(8,128)(2,1)}, bf16[1,192,768]{2,1,0:T(8,128)(2,1)S(1)}, u32[]{:S(2)}) copy-start(bf16[1,192,768]{2,1,0:T(8,128)(2,1)S(1)} %collective-permute-done.5.refs_0_) | copy-start | bytes 884740
  52.5 115.0 %all-gather.5.cloned.1.call-start = ((), (), s32[]{:S(2)}) async-start(), calls=%async_computation.8 | async-start | bytes 3760128 | tf_op jit(solution)/shard_map/all_gather | solution.py:934
  52.6 4.4 %collective-permute-start.11 = (bf16[2,192,768]{2,1,0:T(8,128)(2,1)}, bf16[2,192,768]{2,1,0:T(8,128)(2,1)}, u32[]{:S(2)}, u32[]{:S(2)}) collective-permute-start(bf16[2,192,768]{2,1,0:T(8,128)(2,1)} %collective-permute-done.6.refs_5_), channel_id=1, source_target_pairs={{0,2},{2,0},{4,6},{6,4},{1,3},{3,1},{5,7},{7,5},{8,10},{10,8},{12,... | collective-permute-start | bytes 1769480 | tf_op jit(solution)/shard_map/ppermute | solution.py:839
  53.5 11.6 %collective-permute-start.9 = (bf16[1,192,768]{2,1,0:T(8,128)(2,1)S(1)}, bf16[1,192,768]{2,1,0:T(8,128)(2,1)S(1)}, u32[]{:S(2)}, u32[]{:S(2)}) collective-permute-start(bf16[1,192,768]{2,1,0:T(8,128)(2,1)S(1)} %collective-permute-done.5.refs_0_), channel_id=1, source_target_pairs={{0,4},{2,6},{4,0},{6,2},{1,5},{3,7},{5,1},{7,3},{8,12},{10,14},{12... | collective-permute-start | bytes 884744 | tf_op jit(solution)/shard_map/ppermute | solution.py:839
  55.1 10.1 %collective-permute-start.10 = (bf16[1,192,768]{2,1,0:T(8,128)(2,1)S(1)}, bf16[1,192,768]{2,1,0:T(8,128)(2,1)S(1)}, u32[]{:S(2)}, u32[]{:S(2)}) collective-permute-start(bf16[1,192,768]{2,1,0:T(8,128)(2,1)S(1)} %collective-permute-done.5.refs_0_), channel_id=1, source_target_pairs={{0,2},{2,0},{4,6},{6,4},{1,3},{3,1},{5,7},{7,5},{8,10},{10,8},{12,... | collective-permute-start | bytes 884744 | tf_op jit(solution)/shard_map/ppermute | solution.py:839
  65.2 2.8 collective-permute-start.12
  99.3 19.1 %all-to-all-start.1 = ((bf16[16,96,128]{2,1,0:T(8,128)(2,1)}), bf16[16,96,128]{2,1,0:T(8,128)(2,1)S(1)}, u32[]{:S(2)}, u32[]{:S(2)}) async-start(bf16[16,96,128]{2,1,0:T(8,128)(2,1)} %slots_out.1), calls=%async_computation.1 | async-start | bytes 786432 | tf_op jit(solution)/shard_map/all_to_all | solution.py:935
  103.1 169.6 %reduce-scatter.2.cloned.1.call-start = ((), (), s32[]{:S(2)}) async-start(), calls=%async_computation.9 | async-start | bytes 5013504 | tf_op jit(solution)/shard_map/reduce_scatter | solution.py:952
  104.1 20.0 %copy-start.12 = (bf16[2,192,768]{2,1,0:T(8,128)(2,1)S(1)}, bf16[2,192,768]{2,1,0:T(8,128)(2,1)}, u32[]{:S(2)}) copy-start(bf16[2,192,768]{2,1,0:T(8,128)(2,1)} %param.21) | copy-start | bytes 1769476
  122.7 9.4 %collective-permute-start.13 = (bf16[192,768]{1,0:T(8,128)(2,1)}, bf16[192,768]{1,0:T(8,128)(2,1)S(1)}, u32[]{:S(2)}, u32[]{:S(2)}) collective-permute-start(bf16[192,768]{1,0:T(8,128)(2,1)} %get-tuple-element.112.h_ref.h0), channel_id=1, source_target_pairs={{0,1},{1,0},{2,3},{3,2},{4,5},{5,4},{6,7},{7,6},{8,9},{9,8},{10,11... | collective-permute-start | bytes 884744 | tf_op jit(solution)/shard_map/ppermute | solution.py:823
  139.3 8.9 %collective-permute-start.14 = (bf16[192,768]{1,0:T(8,128)(2,1)}, bf16[192,768]{1,0:T(8,128)(2,1)S(1)}, u32[]{:S(2)}, u32[]{:S(2)}) collective-permute-start(bf16[192,768]{1,0:T(8,128)(2,1)} %get-tuple-element.116), channel_id=1, source_target_pairs={{0,1},{1,0},{2,3},{3,2},{4,5},{5,4},{6,7},{7,6},{8,9},{9,8},{10,11... | collective-permute-start | bytes 884744 | tf_op jit(solution)/shard_map/ppermute | solution.py:823
  167.5 15.9 %all-to-all-start.2 = ((bf16[16,96,128]{2,1,0:T(8,128)(2,1)}), bf16[16,96,128]{2,1,0:T(8,128)(2,1)S(1)}, u32[]{:S(2)}, u32[]{:S(2)}) async-start(bf16[16,96,128]{2,1,0:T(8,128)(2,1)} %get-tuple-element.125), calls=%async_computation.2 | async-start | bytes 786432 | tf_op jit(solution)/shard_map/all_to_all | solution.py:953
  184.2 46.7 %all-to-all-start.3 = ((bf16[16,48,768]{2,1,0:T(8,128)(2,1)}), bf16[16,48,768]{2,1,0:T(8,128)(2,1)S(1)}, u32[]{:S(2)}, u32[]{:S(2)}) async-start(bf16[16,48,768]{2,1,0:T(8,128)(2,1)} %bitcast.198), calls=%async_computation.3 | async-start | bytes 2359296 | tf_op jit(solution)/shard_map/all_to_all | solution.py:956
  188.1 9.3 %collective-permute-start.15 = (bf16[192,768]{1,0:T(8,128)(2,1)}, bf16[192,768]{1,0:T(8,128)(2,1)S(1)}, u32[]{:S(2)}, u32[]{:S(2)}) collective-permute-start(bf16[192,768]{1,0:T(8,128)(2,1)} %get-tuple-element.139), channel_id=1, source_target_pairs={{0,1},{1,0},{2,3},{3,2},{4,5},{5,4},{6,7},{7,6},{8,9},{9,8},{10,11... | collective-permute-start | bytes 884744 | tf_op jit(solution)/shard_map/ppermute | solution.py:823
  197.5 32.5 %collective-permute-start.16 = (bf16[192,768]{1,0:T(8,128)(2,1)S(1)}, bf16[192,768]{1,0:T(8,128)(2,1)S(1)}, u32[]{:S(2)}, u32[]{:S(2)}) collective-permute-start(bf16[192,768]{1,0:T(8,128)(2,1)S(1)} %add_convert_fusion), channel_id=1, source_target_pairs={{0,1},{1,0},{2,3},{3,2},{4,5},{5,4},{6,7},{7,6},{8,9},{9,8},{10,11... | collective-permute-start | bytes 884744 | tf_op jit(solution)/shard_map/ppermute | solution.py:823
  230.9 41.8 %all-to-all-start.4 = ((bf16[16,288,128]{2,1,0:T(8,128)(2,1)}), bf16[16,288,128]{2,1,0:T(8,128)(2,1)S(1)}, u32[]{:S(2)}, u32[]{:S(2)}) async-start(bf16[16,288,128]{2,1,0:T(8,128)(2,1)} %get-tuple-element.142), calls=%async_computation.4 | async-start | bytes 2359296 | tf_op jit(solution)/shard_map/all_to_all | solution.py:964
  238.2 8.5 %copy-start.20 = (f32[384,48]{0,1:T(8,128)S(1)}, f32[384,48]{0,1:T(8,128)}, u32[]{:S(2)}) copy-start(f32[384,48]{0,1:T(8,128)} %param.25) | copy-start | bytes 221188
  238.2 8.5 %copy-start.28 = (f32[384,48]{0,1:T(8,128)S(1)}, f32[384,48]{0,1:T(8,128)}, u32[]{:S(2)}) copy-start(f32[384,48]{0,1:T(8,128)} %param.33) | copy-start | bytes 221188
  238.2 8.5 %copy-start.29 = (f32[384,48]{0,1:T(8,128)S(1)}, f32[384,48]{0,1:T(8,128)}, u32[]{:S(2)}) copy-start(f32[384,48]{0,1:T(8,128)} %param.32) | copy-start | bytes 221188
  238.2 7.7 %collective-permute-start.17 = (bf16[16,24,256]{2,1,0:T(8,128)(2,1)S(1)}, bf16[16,24,256]{2,1,0:T(8,128)(2,1)S(1)}, u32[]{:S(2)}, u32[]{:S(2)}) collective-permute-start(bf16[16,24,256]{2,1,0:T(8,128)(2,1)S(1)} %select_bitcast_fusion.4), channel_id=1, source_target_pairs={{0,1},{1,0},{2,3},{3,2},{4,5},{5,4},{6,7},{7,6},{8,9},{9,8},{10,11... | collective-permute-start | bytes 589832 | tf_op jit(solution)/shard_map/ppermute | solution.py:823
  239.9 6.8 %collective-permute-start.20 = (bf16[48,384]{1,0:T(8,128)(2,1)S(1)}, bf16[48,384]{1,0:T(8,128)(2,1)S(1)}, u32[]{:S(2)}, u32[]{:S(2)}) collective-permute-start(bf16[48,384]{1,0:T(8,128)(2,1)S(1)} %select_convert_fusion), channel_id=1, source_target_pairs={{0,1},{1,0},{2,3},{3,2},{4,5},{5,4},{6,7},{7,6},{8,9},{9,8},{10,11... | collective-permute-start | bytes 110600 | tf_op jit(solution)/shard_map/ppermute | solution.py:823
  273.7 13.9 %copy-start.21 = (f32[48,1536]{1,0:T(8,128)S(1)}, f32[48,1536]{1,0:T(8,128)}, u32[]{:S(2)}) copy-start(f32[48,1536]{1,0:T(8,128)} %param.35) | copy-start | bytes 884740
  273.7 13.9 %copy-start.22 = (f32[48,1536]{1,0:T(8,128)S(1)}, f32[48,1536]{1,0:T(8,128)}, u32[]{:S(2)}) copy-start(f32[48,1536]{1,0:T(8,128)} %param.34) | copy-start | bytes 884740
  278.6 11.0 %copy-start.23 = (f32[1536,48]{0,1:T(8,128)S(1)}, f32[1536,48]{0,1:T(8,128)}, u32[]{:S(2)}) copy-start(f32[1536,48]{0,1:T(8,128)} %param.37) | copy-start | bytes 884740
  278.6 11.0 %copy-start.24 = (f32[1536,48]{0,1:T(8,128)S(1)}, f32[1536,48]{0,1:T(8,128)}, u32[]{:S(2)}) copy-start(f32[1536,48]{0,1:T(8,128)} %param.36) | copy-start | bytes 884740
  278.6 11.0 %copy-start.25 = (bf16[48,3072]{1,0:T(8,128)(2,1)S(1)}, bf16[48,3072]{1,0:T(8,128)(2,1)}, u32[]{:S(2)}) copy-start(bf16[48,3072]{1,0:T(8,128)(2,1)} %reduce-scatter.2.cloned.1.call-done) | copy-start | bytes 884740
  278.6 12.0 %collective-permute-start.18 = (bf16[192,768]{1,0:T(8,128)(2,1)}, bf16[192,768]{1,0:T(8,128)(2,1)S(1)}, u32[]{:S(2)}, u32[]{:S(2)}) collective-permute-start(bf16[192,768]{1,0:T(8,128)(2,1)} %input_back.1), channel_id=1, source_target_pairs={{0,1},{1,0},{2,3},{3,2},{4,5},{5,4},{6,7},{7,6},{8,9},{9,8},{10,11... | collective-permute-start | bytes 884744 | tf_op jit(solution)/shard_map/ppermute | solution.py:823
  280.1 16.5 %all-to-all-start.5 = ((bf16[16,24,256]{2,1,0:T(8,128)(2,1)}), bf16[16,24,256]{2,1,0:T(8,128)(2,1)S(1)}, u32[]{:S(2)}, u32[]{:S(2)}) async-start(bf16[16,24,256]{2,1,0:T(8,128)(2,1)} %fusion.3), calls=%async_computation.6 | async-start | bytes 393216 | tf_op jit(solution)/shard_map/all_to_all | solution.py:971
  291.8 9.2 %copy-start.33 = (f32[4,48]{1,0:T(4,128)S(1)}, f32[4,48]{1,0:T(4,128)}, u32[]{:S(2)}) copy-start(f32[4,48]{1,0:T(4,128)} %param.39) | copy-start | bytes 2308
  291.8 9.2 %copy-start.34 = (f32[4,48]{1,0:T(4,128)S(1)}, f32[4,48]{1,0:T(4,128)}, u32[]{:S(2)}) copy-start(f32[4,48]{1,0:T(4,128)} %param.38) | copy-start | bytes 2308
  297.4 3.7 %collective-permute-start.21 = (f32[4,24]{1,0:T(4,128)S(1)}, f32[4,24]{1,0:T(4,128)S(1)}, u32[]{:S(2)}, u32[]{:S(2)}) collective-permute-start(f32[4,24]{1,0:T(4,128)S(1)} %pad_maximum_fusion.6), channel_id=1, source_target_pairs={{0,1},{1,0},{2,3},{3,2},{4,5},{5,4},{6,7},{7,6},{8,9},{9,8},{10,11... | collective-permute-start | bytes 1160 | tf_op jit(solution)/shard_map/ppermute | solution.py:823
  298.2 5.3 %collective-permute-start.19 = (bf16[24,6,3,64]{3,2,0,1:T(4,128)(2,1)S(1)}, bf16[24,6,3,64]{3,2,0,1:T(4,128)(2,1)S(1)}, u32[]{:S(2)}, u32[]{:S(2)}) collective-permute-start(bf16[24,6,3,64]{3,2,0,1:T(4,128)(2,1)S(1)} %select_bitcast_fusion.5), channel_id=1, source_target_pairs={{0,1},{1,0},{2,3},{3,2},{4,5},{5,4},{6,7},{7,6},{8,9},{9,8},{10,11... | collective-permute-start | bytes 165896 | tf_op jit(solution)/shard_map/ppermute | solution.py:823
  (22 other events, 57.7 us)
Sparse Core Ops, SparseCore 0:
  52.6 66.8 all-gather.2
  122.4 45.0 all-gather.4
  171.4 99.6 reduce-scatter.1
